TPU v7x, 512 devices: a whole 4x8x8 slice. The times are simulated.
512 devices in a mesh: rows: 8 (over z), vocab: 16 (over y, core), mp: 4 (over x).
Axes of the slice: x: 4, y: 8, z: 8, core: 2. Of those that a mesh axis runs over, the one named last changes fastest.
Arguments:
- hidden: bfloat16 [2, 32768, 5120], P(None, ('rows', 'vocab'), 'mp'), may hold values from -2 to 2
- gain: bfloat16 [5120], replicated, may hold values from 0.5 to 1.5
- head: bfloat16 [5120, 32000], P('rows', ('vocab', 'mp')), may hold values from -0.36336105 to 0.36336105
- exit_slots: int32 [2, 768], P(None, ('rows', 'vocab')), may hold values from 0 to 256, as said below
- targets: int32 [32768], P(('rows', 'vocab')), may hold values from 0 to 31999
Outputs:
- exit_grads: bfloat16 [2, 768, 5120], P(None, ('rows', 'vocab'), 'mp')
- group_loss: float32 [2, 8], P(None, 'rows')
Inputs may be any that keep to these rules, and one draw needn't show every extreme that they name: `exit_slots`: each block of 6 entries (one layer, one device of rows+vocab) starts with its live entries, distinct local rows below 256; all its other entries equal 256. In each layer the 16 blocks of one index of rows hold exactly 36 live entries together, and one of them holds 6.
All inputs are finite; a program needn't handle non-finite values.
Results may differ from a plain program's by a relative error of at most 0.014.
Values may be sent and summed in bfloat16 or wider, within the bound.
No kernel may reach another device: no remote copies, remote signals or barrier semaphores. Data moves between devices by JAX's collectives and lax.ppermute only.
A program may use at most 64 MiB of HBM per device.

v0:
```python
import jax
import jax.numpy as jnp
from jax import lax
from jax.sharding import PartitionSpec as P

EPS = 1e-05


def decode_rows(rows, labels, live, full_head, gain_f):
    width = rows.shape[2]
    span = full_head.shape[1]
    values = rows.astype(jnp.float32)
    scale = lax.rsqrt(jnp.sum(values * values, axis=2) / width + EPS)
    normed = (values * scale[:, :, None] * gain_f).astype(jnp.bfloat16)
    logits = jnp.einsum("lgd,dv->lgv", normed, full_head, preferred_element_type=jnp.float32)
    shard = lax.axis_index("vocab") * lax.axis_size("mp") + lax.axis_index("mp")
    columns = shard * span + lax.broadcasted_iota(jnp.int32, (1, 1, span), 2)
    hits = columns == labels[:, :, None]
    aimed = jnp.sum(jnp.where(hits, logits, jnp.zeros((), jnp.float32)), axis=2)
    peak = lax.pmax(jnp.max(logits, axis=2), ("vocab", "mp"))
    mass_own = jnp.sum(jnp.exp(logits - peak[:, :, None]), axis=2)
    mass, target = lax.psum((mass_own, aimed), ("vocab", "mp"))
    loss_rows = (peak + jnp.log(mass) - target) * live
    probs = jnp.exp(logits - peak[:, :, None]) / mass[:, :, None]
    slope = ((probs - hits.astype(jnp.float32)) * live[:, :, None]).astype(jnp.bfloat16)
    partial_value = jnp.einsum("lgv,dv->lgd", slope, full_head, preferred_element_type=jnp.float32)
    dots = jnp.sum(values * gain_f * partial_value, axis=2)
    return (loss_rows, partial_value, dots, scale)


def body(hidden, gain, head, exit_slots, targets):
    layers, row_dev, part_width = hidden.shape
    most = exit_slots.shape[1]
    vocab_devs = lax.axis_size("vocab")
    mp_devs = lax.axis_size("mp")
    vocab_rank = lax.axis_index("vocab")
    mp_rank = lax.axis_index("mp")
    width = gain.shape[0]
    gain_f = gain.astype(jnp.float32)
    live_own = exit_slots < row_dev
    local = jnp.minimum(exit_slots, row_dev - 1)
    picked = jax.vmap(lambda block, index: block[index])(hidden, local)
    picked = jnp.where(live_own[:, :, None], picked, jnp.zeros_like(picked))
    own_labels = jnp.where(live_own, targets[local], -1)
    full_head = lax.all_gather(head, "rows", axis=0, tiled=True)
    own_values = picked.astype(jnp.float32)
    gain_own = lax.dynamic_slice_in_dim(gain_f, mp_rank * part_width, part_width)
    gathered, label_rows = (
        lax.all_gather(picked, ("vocab", "mp"), axis=1, tiled=True),
        lax.all_gather(own_labels, ("vocab", "mp"), axis=1, tiled=True),
    )
    rows = gathered.reshape(layers, vocab_devs, mp_devs, most, part_width)
    rows = rows.transpose(0, 1, 3, 2, 4).reshape(layers, vocab_devs * most, width)
    labels = label_rows.reshape(layers, vocab_devs, mp_devs, most)[:, :, 0, :].reshape(
        layers, vocab_devs * most
    )
    live = (labels >= 0).astype(jnp.float32)
    loss_rows, partial_value, dots, scale = decode_rows(rows, labels, live, full_head, gain_f)
    sent = partial_value.reshape(layers, vocab_devs, most, mp_devs, part_width)
    sent = sent.transpose(0, 1, 3, 2, 4).reshape(layers, vocab_devs * mp_devs * most, part_width)
    sent_dots = jnp.broadcast_to(
        dots.reshape(layers, vocab_devs, 1, most), (layers, vocab_devs, mp_devs, most)
    )
    sent_dots = sent_dots.reshape(layers, vocab_devs * mp_devs * most)
    own_grad, own_dots = (
        lax.psum_scatter(sent, ("vocab", "mp"), scatter_dimension=1, tiled=True),
        lax.psum_scatter(sent_dots, ("vocab", "mp"), scatter_dimension=1, tiled=True),
    )
    own_scale = lax.dynamic_slice_in_dim(scale, vocab_rank * most, most, 1)
    group_loss = (jnp.sum(loss_rows, axis=1) / jnp.sum(live, axis=1))[:, None]
    exit_grads = (
        own_scale[:, :, None] * gain_own * own_grad
        - own_values * (own_scale**3)[:, :, None] * own_dots[:, :, None] / width
    )
    return (exit_grads.astype(jnp.bfloat16), group_loss)


def solution(mesh):
    in_specs = (
        P(None, ("rows", "vocab"), "mp"),
        P(),
        P("rows", ("vocab", "mp")),
        P(None, ("rows", "vocab")),
        P(("rows", "vocab")),
    )
    out_specs = (P(None, ("rows", "vocab"), "mp"), P(None, "rows"))
    return jax.shard_map(body, mesh=mesh, in_specs=in_specs, out_specs=out_specs, check_vma=False)
```

profile of v0, /device:TPU:1, one launch (start us, length us, event | category | flops | bytes accessed | tf_op | source)
XLA Modules:
  0.0 653.8 jit_solution(13347096265205226689)
XLA Ops:
  7.2 0.8 compare_select_fusion.1
  8.0 0.7 bitcast_or_fusion
  8.8 1.3 gather_fusion
  10.2 0.7 select_bitcast_fusion
  11.0 0.8 gather_fusion.1
  11.8 0.6 copy.29
  12.6 0.7 all-gather.6.cloned.1.call-update
  13.3 0.7 convert_element_type.46
  14.0 72.8 %all-gather = s32[64,6,2]{1,2,0:T(2,128)S(1)} all-gather(s32[1,6,2]{1,2,0:T(2,128)S(1)} %get-tuple-element.16), channel_id=1, replica_groups=mesh['rows'=8,'vocab'=16,'mp'=4] {'vocab','mp'}, dimensions={0}, use_global_device_ids=true | all-gather | bytes 3120 | tf_op jit(solution)/shard_map/all_gather | solution.py:50
  87.0 0.2 reshape.73
  87.4 13.7 %all-gather.4.cloned.1.call-done = bf16[2,384,1280]{2,0,1:T(2,128)(2,1)} async-done(((bf16[2,6,1280]{2,0,1:T(2,128)(2,1)}), bf16[2,384,1280]{2,0,1:T(2,128)(2,1)}) %all-gather.4.cloned.1.call-update) | async-done | bytes 1966096 | tf_op jit(solution)/shard_map/all_gather | solution.py:49
  101.1 2.9 convert_element_type.45
  104.0 2.9 copy.31
  106.9 5.9 reshape.77
  112.8 2.1 multiply_reduce_fusion.1
  115.0 0.2 reduce_sum.62
  115.4 52.7 %all-gather.6.cloned.1.call-done = bf16[5120,500]{0,1:T(8,128)(2,1)} async-done(((bf16[640,500]{0,1:T(8,128)(2,1)}), bf16[5120,500]{0,1:T(8,128)(2,1)}) %all-gather.6.cloned.1.call-update) | async-done | bytes 5120016 | tf_op jit(solution)/shard_map/all_gather | solution.py:45
  168.1 5.5 fusion.21
  173.5 124.1 %pmax.7 = f32[2,96]{1,0:T(2,128)S(1)} all-reduce(f32[2,96]{1,0:T(2,128)S(1)} %get-tuple-element.18), channel_id=1, replica_groups=mesh['rows'=8,'vocab'=16,'mp'=4] {'vocab','mp'}, use_global_device_ids=true, to_apply=%region_3.4 | all-reduce | flops 192 | bytes 1536 | tf_op jit(solution)/shard_map/pmax | solution.py:20
  297.7 0.3 fusion.9
  297.9 124.2 %psum.14 = f32[2,96]{1,0:T(2,128)S(1)} all-reduce(f32[2,96]{1,0:T(2,128)S(1)} %get-tuple-element.11), channel_id=1, replica_groups=mesh['rows'=8,'vocab'=16,'mp'=4] {'vocab','mp'}, use_global_device_ids=true, to_apply=%region_5.6 | all-reduce | flops 192 | bytes 1536 | tf_op jit(solution)/shard_map/psum | solution.py:22
  422.2 7.1 %multiply_reduce_fusion = (f32[2,96]{1,0:T(2,128)S(1)}, f32[2,96,5120]{2,1,0:T(8,128)}) fusion(f32[2,96,5120]{2,1,0:T(8,128)} %reshape.77, f32[5120]{0:T(1024)S(1)} %convert_element_type.46, bf16[5120,500]{0,1:T(8,128)(2,1)} %all-gather.6.cloned.1.call-done, f32[2,96,500]{2,1,0:T(8,128)S(1)} %get-tuple-element.19, f32[2,96]{1,0:T(2,128)S(1)} %fusion.20, ...), kind=kOutput, calls=%fused_computation.6 | convolution fusion | flops 986660928 | bytes 13394640 | tf_op jit(solution)/shard_map/lgv,dv->lgd/dot_general | solution.py:26
  429.3 5.7 reshape.74
  435.0 7.0 %copy.33 = f32[2,16,6,4,1280]{4,0,2,3,1:T(2,128)} copy(f32[2,16,6,4,1280]{4,3,2,1,0:T(4,128)} %reshape.74) | data formatting | bytes 7864320 | tf_op jit(solution)/shard_map/reshape | solution.py:59
  442.0 0.7 copy-done.3
  442.8 1.3 dynamic-slice
  444.7 1.0 fusion.19
  446.0 126.9 %all-reduce.2 = (f32[2,384]{1,0:T(2,128)S(1)}, f32[2,96]{1,0:T(2,128)S(1)}) all-reduce(f32[2,384]{1,0:T(2,128)S(1)} %reshape.76, f32[2,96]{1,0:T(2,128)S(1)} %get-tuple-element.10), channel_id=3, replica_groups=mesh['rows'=8,'vocab'=16,'mp'=4] {'vocab','mp'}, use_global_device_ids=true, to_apply=%region_8.9.clone | all-reduce | flops 960 | bytes 7680
  573.1 0.5 divide_bitcast_fusion
  573.6 72.1 %all-reduce.5.cloned.1.call-done = f32[2,384,1280]{2,0,1:T(2,128)} async-done(((f32[2,384,1280]{2,0,1:T(2,128)}), f32[2,384,1280]{2,0,1:T(2,128)}) %all-reduce.5.cloned.1.call-update) | async-done | bytes 3932176
  645.7 0.8 constant_dynamic-slice_fusion.1
  646.6 0.6 copy.35
  (36 shorter events, 1.7 us)
Async XLA Ops:
  7.2 3.8 copy-start
  7.2 93.9 %all-gather.4.cloned.1.call-start = ((), (), s32[]{:S(2)}) async-start(), calls=%async_computation | async-start | bytes 1996800 | tf_op jit(solution)/shard_map/all_gather | solution.py:49
  12.5 155.5 %all-gather.6.cloned.1.call-start = ((), (), s32[]{:S(2)}) async-start(), calls=%async_computation.1 | async-start | bytes 5806080 | tf_op jit(solution)/shard_map/all_gather | solution.py:45
  13.3 632.4 %all-reduce.5.cloned.1.call-start = ((), (), s32[]{:S(2)}) async-start(), calls=%async_computation.2 | async-start | bytes 7864320
  87.2 16.8 %copy-start.2 = (s32[2,16,4,6]{3,2,1,0:T(4,128)}, s32[2,16,4,6]{3,2,1,0:T(4,128)S(1)}, u32[]{:S(2)}) copy-start(s32[2,16,4,6]{3,2,1,0:T(4,128)S(1)} %reshape.73) | copy-start | bytes 9220
  106.9 5.9 copy-start.1
  442.0 0.7 copy-start.3
Sparse Core Ops, SparseCore 0:
  12.6 88.4 all-gather.3
  103.2 64.8 all-gather.5
  442.1 203.4 all-reduce.4
where the time goes:
time: 656 us; the launch traced here: 654 us
  blocking collectives  448 us (68%)
  waiting for transfers between devices  139 us (21%)
  local copies, waits for them, and re-layouts  29.1 us (4%)
  between operations  14.6 us (2%)
  matrix products  12.6 us (2%)
  other arithmetic  10 us (2%)
    unnamed x1, blocking collectives  127 us
    psum x1, blocking collectives, decode_rows(): mass, target = lax.psum((mass_own, aimed), ('vocab', 'mp'))  124 us
    pmax x1, blocking collectives, decode_rows(): peak = lax.pmax(jnp.max(logits, axis=2), ('vocab', 'mp'))  124 us
    all_gather x1, blocking collectives, body(): lax.all_gather(own_labels, ('vocab', 'mp'), axis=1, tiled=True)  72.8 us
    unnamed x4, waiting for transfers between devices  72.8 us
    all_gather x1, waiting for transfers between devices, body(): full_head = lax.all_gather(head, 'rows', axis=0, tiled=True)  52.7 us
    all_gather x1, waiting for transfers between devices, body(): lax.all_gather(picked, ('vocab', 'mp'), axis=1, tiled=True)  13.7 us
  transfers between devices with their start and end apart: 3, of which 3 were waited for; matrix products, arithmetic and copies ran while one was open for 3% of the time, Pallas kernels for 0%

commit v1 on v0

v1 whole, which is shorter than its diff:
```python
import functools

import jax
import jax.numpy as jnp
from jax import lax
from jax.experimental import pallas as pl
from jax.experimental.pallas import tpu as pltpu
from jax.sharding import Mesh, PartitionSpec as P

EPS = 1e-05
LIVE = 72
F32 = jnp.float32
BF16 = jnp.bfloat16


def params():
    return pltpu.CompilerParams(vmem_limit_bytes=40 * 1024 * 1024)


def hits_of(label, first, span):
    column = first + lax.broadcasted_iota(jnp.int32, (span, LIVE), 0)
    return column == label


def logits_kernel(first_ref, normed_ref, head_ref, label_ref, logits_ref, stats_ref):
    step = pl.program_id(0)
    part = lax.dot_general(
        head_ref[0], normed_ref[0], (((1,), (1,)), ((), ())), preferred_element_type=F32
    )

    @pl.when(step == 0)
    def _():
        logits_ref[...] = part

    @pl.when(step > 0)
    def _():
        logits_ref[...] += part

    @pl.when(step == pl.num_programs(0) - 1)
    def _():
        logits = logits_ref[...]
        hits = hits_of(label_ref[...], first_ref[0], logits.shape[0])
        peak = jnp.max(logits, axis=0, keepdims=True)
        shifted = jnp.exp(logits - peak)
        stats_ref[0:1, :] = peak
        stats_ref[1:2, :] = jnp.sum(shifted, axis=0, keepdims=True)
        stats_ref[2:3, :] = jnp.sum(shifted * logits, axis=0, keepdims=True)
        stats_ref[3:4, :] = jnp.sum(jnp.where(hits, logits, 0.0), axis=0, keepdims=True)


def local_logits(first, normed, head, label):
    parts, span, width = head.shape
    return pl.pallas_call(
        logits_kernel,
        grid=(parts,),
        in_specs=[
            pl.BlockSpec(memory_space=pltpu.SMEM),
            pl.BlockSpec((1, LIVE, width), lambda i: (i // 2, 0, i % 2)),
            pl.BlockSpec((1, span, width), lambda i: (i, 0, 0)),
            pl.BlockSpec((1, LIVE), lambda i: (0, 0)),
        ],
        out_specs=[
            pl.BlockSpec((span, LIVE), lambda i: (0, 0)),
            pl.BlockSpec((4, LIVE), lambda i: (0, 0)),
        ],
        out_shape=[
            jax.ShapeDtypeStruct((span, LIVE), F32),
            jax.ShapeDtypeStruct((4, LIVE), F32),
        ],
        compiler_params=params(),
        name="logits",
    )(first, normed, head, label)


def back_kernel(
    first_ref, core_ref, stats_ref, logits_ref, head_ref, label_ref, layer_ref,
    keep_ref, send_ref, row_ref, loss_ref, slope_ref,
):
    step = pl.program_id(0)

    @pl.when(step == 0)
    def _():
        stats = stats_ref[...]
        peaks = [stats[:, 4 * c, :] for c in range(2)]
        peak = jnp.max(jnp.maximum(peaks[0], peaks[1]), axis=0, keepdims=True)
        weight = [jnp.exp(p - peak) for p in peaks]
        mass = sum(weight[c] * stats[:, 4 * c + 1, :] for c in range(2))
        mass = jnp.sum(mass, axis=0, keepdims=True)
        mean = sum(weight[c] * stats[:, 4 * c + 2, :] for c in range(2))
        mean = jnp.sum(mean, axis=0, keepdims=True) / mass
        aimed = jnp.sum(stats[:, 3, :] + stats[:, 7, :], axis=0, keepdims=True)
        row_ref[...] = mean - aimed
        loss = peak + jnp.log(mass) - aimed
        for layer in range(2):
            mine = (layer_ref[...] == layer).astype(F32)
            total = jnp.sum(loss * mine, axis=1, keepdims=True)
            loss_ref[layer : layer + 1, :] = total / jnp.sum(mine, axis=1, keepdims=True)
        logits = logits_ref[...]
        hits = hits_of(label_ref[...], first_ref[0], logits.shape[0])
        slope = jnp.exp(logits - peak) / mass - hits.astype(F32)
        slope_ref[...] = slope.T.astype(BF16)

    part = jnp.dot(slope_ref[...], head_ref[0], preferred_element_type=F32)

    @pl.when(step % 2 == core_ref[0])
    def _():
        keep_ref[step // 2] = part

    @pl.when(step % 2 != core_ref[0])
    def _():
        send_ref[step // 2] = part


def local_back(first, core, stats, logits, head, label, layer):
    parts, span, width = head.shape
    whole = lambda shape: pl.BlockSpec(shape, lambda i: (0,) * len(shape))
    half = (parts // 2, LIVE, width)
    return pl.pallas_call(
        back_kernel,
        grid=(parts,),
        in_specs=[
            pl.BlockSpec(memory_space=pltpu.SMEM),
            pl.BlockSpec(memory_space=pltpu.SMEM),
            whole(stats.shape),
            whole(logits.shape),
            pl.BlockSpec((1, span, width), lambda i: (i, 0, 0)),
            whole((1, LIVE)),
            whole((1, LIVE)),
        ],
        out_specs=[whole(half), whole(half), whole((1, LIVE)), whole((2, 1))],
        out_shape=[
            jax.ShapeDtypeStruct(half, F32),
            jax.ShapeDtypeStruct(half, F32),
            jax.ShapeDtypeStruct((1, LIVE), F32),
            jax.ShapeDtypeStruct((2, 1), F32),
        ],
        scratch_shapes=[pltpu.VMEM((LIVE, span), BF16)],
        compiler_params=params(),
        name="back",
    )(first, core, stats, logits, head, label, layer)


def spread(values, axes, count):
    copies = jnp.broadcast_to(values[None], (count, *values.shape))
    return lax.all_to_all(copies, axes, 0, 0, tiled=True)


def swap_core(values):
    return lax.ppermute(values, "c", [(0, 1), (1, 0)])


def body(hidden, gain, head, exit_slots, targets):
    layers, row_dev, part_width = hidden.shape
    most = exit_slots.shape[1]
    own = layers * most
    width = gain.shape[0]
    span = head.shape[1]
    y, c, x = (lax.axis_index(name) for name in ("y", "c", "x"))
    first = (((y * 2 + c) * 4 + x) * span).astype(jnp.int32).reshape(1)
    core = c.astype(jnp.int32).reshape(1)

    full_head = lax.all_gather(head.T, "z", axis=0)

    live = exit_slots < row_dev
    local = jnp.minimum(exit_slots, row_dev - 1)
    picked = jax.vmap(lambda block, index: block[index])(hidden, local)
    picked = jnp.where(live[:, :, None], picked, jnp.zeros_like(picked))
    label = jnp.where(live, targets[local], 0)
    layer = jnp.broadcast_to(jnp.arange(layers)[:, None], live.shape)
    facts = jnp.stack([live.astype(jnp.int32), label // 256, label % 256, layer], axis=2)
    facts = jnp.pad(facts.astype(BF16), ((0, 0), (0, 0), (0, 124)))
    packed = jnp.concatenate([picked, facts], axis=2).reshape(own, part_width + 128)
    pair = lax.all_gather(packed, "c", axis=0, tiled=True)
    slots = spread(pair, "y", 8).reshape(16 * own, part_width + 128)

    total = slots.shape[0]
    flag = slots[:, part_width].astype(F32)
    below = (jnp.arange(total)[:, None] < jnp.arange(total)[None, :]).astype(F32)
    rank = jnp.sum(below * flag[:, None], axis=0)
    place = (rank[None, :] == jnp.arange(LIVE, dtype=F32)[:, None]) & (flag > 0)[None, :]
    place = place.astype(BF16)
    compact = jnp.dot(place, slots, preferred_element_type=F32)
    fact = compact[:, part_width : part_width + 4].astype(jnp.int32).T
    label_row = (fact[1] * 256 + fact[2]).reshape(1, LIVE)
    layer_row = fact[3].reshape(1, LIVE)
    rows = spread(compact[:, :part_width].astype(BF16), "x", 4)

    values = rows.astype(F32)
    scale = lax.rsqrt(jnp.sum(values * values, axis=(0, 2)) / width + EPS)
    gain_f = gain.astype(F32)
    normed = values * scale[None, :, None] * gain_f.reshape(4, 1, part_width)
    normed = normed.astype(BF16)

    logits, stats = local_logits(first, normed, full_head, label_row)
    stats = lax.all_gather(stats, "c", axis=0, tiled=True)
    stats = spread(stats, ("y", "x"), 32)
    keep, send, gap, group_loss = local_back(
        first, core, stats, logits, full_head, label_row, layer_row
    )
    part = (keep + swap_core(send)).astype(BF16)
    part = lax.all_to_all(part, "x", 0, 0, tiled=True)
    part = jnp.sum(part.astype(F32), axis=0).astype(BF16)
    sent = lax.dot_general(place, part, (((0,), (0,)), ((), ())), preferred_element_type=F32)
    sent = sent.astype(BF16).reshape(8, 2 * own, part_width // 2)
    back = jnp.sum(lax.all_to_all(sent, "y", 0, 0, tiled=True).astype(F32), axis=0)

    half = part_width // 2
    start = x * part_width + c * half
    gain_half = lax.dynamic_slice_in_dim(gain_f, start, half)
    value_half = lax.dynamic_slice_in_dim(pair, c * half, half, 1).astype(F32)
    mine = lax.dynamic_slice_in_dim(place, y * 2 * own, 2 * own, 1).astype(F32)
    scale_own = jnp.sum(mine * scale[:, None], axis=0)
    shift_own = jnp.sum(mine * (scale**3 * gap[0] / scale / width)[:, None], axis=0)
    grads = scale_own[:, None] * gain_half * back - value_half * shift_own[:, None]
    grads = grads.astype(BF16).reshape(2, own, half)
    kept = lax.dynamic_index_in_dim(grads, c, 0, keepdims=False)
    came = swap_core(lax.dynamic_index_in_dim(grads, 1 - c, 0, keepdims=False))
    low = jnp.where(c == 0, kept, came)
    high = jnp.where(c == 0, came, kept)
    exit_grads = jnp.concatenate([low, high], axis=1).reshape(layers, most, part_width)
    return exit_grads, group_loss


def solution(mesh):
    split = Mesh(mesh.devices.reshape(8, 8, 2, 4), ("z", "y", "c", "x"))
    in_specs = (
        P(None, ("z", "y", "c"), "x"),
        P(),
        P("z", ("y", "c", "x")),
        P(None, ("z", "y", "c")),
        P(("z", "y", "c")),
    )
    out_specs = (P(None, ("z", "y", "c"), "x"), P(None, "z"))
    return jax.shard_map(body, mesh=split, in_specs=in_specs, out_specs=out_specs, check_vma=False)
```

time: 656 us -> 157 us (0.24)
  blocking collectives: 448 us -> 49.7 us
  waiting for transfers between devices: 139 us -> 55.9 us
  local copies, waits for them, and re-layouts: 29.1 us -> 7.66 us
  starting transfers between devices: 0.12 us -> 19 us
  matrix products: 12.6 us -> 1.31 us
  other arithmetic: 10 us -> 3 us
    unnamed x1 -> x0, blocking collectives: 127 us -> none
    psum x1 -> x0, blocking collectives: 124 us -> none  [decode_rows(): mass, target = lax.psum((mass_own, aimed), ('vocab', 'mp'))]
    pmax x1 -> x0, blocking collectives: 124 us -> none  [decode_rows(): peak = lax.pmax(jnp.max(logits, axis=2), ('vocab', 'mp'))]
    unnamed x4 -> x1, waiting for transfers between devices: 72.8 us -> 0.68 us
    all_gather x1 -> x2, blocking collectives: 72.8 us -> 10.6 us  [the longest x1 8.4 us: body(): pair = lax.all_gather(packed, 'c', axis=0, tiled=True)]
    all_gather x2 -> x1, waiting for transfers between devices: 66.4 us -> 25.3 us  [body(): full_head = lax.all_gather(head.T, 'z', axis=0)]
    all_to_all x0 -> x2, blocking collectives: none -> 39.1 us  [spread(): return lax.all_to_all(copies, axes, 0, 0, tiled=True)]
    all_to_all x0 -> x3, waiting for transfers between devices: none -> 27.9 us  [the longest x1 11.1 us: spread(): return lax.all_to_all(copies, axes, 0, 0, tiled=True)]
  transfers between devices with their start and end apart: 3 -> 6, of which waited for: 3 -> 6; matrix products, arithmetic and copies ran while one was open for 3% -> 4% of each run, Pallas kernels for 0% -> 0%
where the time goes in v1:
time: 157 us; the launch traced here: 156 us
  waiting for transfers between devices  55.9 us (36%)
  blocking collectives  49.7 us (32%)
  starting transfers between devices  19 us (12%)
  between operations  14.3 us (9%)
  local copies, waits for them, and re-layouts  7.66 us (5%)
  Pallas kernels  5.61 us (4%)
  other arithmetic  3 us (2%)
    all_to_all x2, blocking collectives, spread(): return lax.all_to_all(copies, axes, 0, 0, tiled=True)  39.1 us
    all_gather x1, waiting for transfers between devices, body(): full_head = lax.all_gather(head.T, 'z', axis=0)  25.3 us
    all_to_all x1, waiting for transfers between devices, spread(): return lax.all_to_all(copies, axes, 0, 0, tiled=True)  11.1 us
    all_to_all x1, waiting for transfers between devices, body(): lax.all_to_all(sent, 'y', 0, 0, tiled=True).astype(F32)  9.36 us
    ppermute x2, starting transfers between devices, swap_core(): return lax.ppermute(values, 'c', [(0, 1), (1, 0)])  8.63 us
    all_gather x1, blocking collectives, body(): pair = lax.all_gather(packed, 'c', axis=0, tiled=True)  8.4 us
    all_to_all x1, waiting for transfers between devices, body(): part = lax.all_to_all(part, 'x', 0, 0, tiled=True)  7.44 us
    unnamed x15, local copies, waits for them, and re-layouts  3.82 us
  transfers between devices with their start and end apart: 6, of which 6 were waited for; matrix products, arithmetic and copies ran while one was open for 4% of the time, Pallas kernels for 0%

profile of v1, /device:TPU:1, one launch (start us, length us, event | category | flops | bytes accessed | tf_op | source)
XLA Modules:
  0.0 156.5 jit_solution(9607455362650147709)
XLA Ops:
  7.2 0.7 all-gather.6.cloned.1.call-update
  7.9 0.7 compare_select_fusion
  8.7 1.3 gather_fusion
  10.6 0.8 gather_fusion.1
  11.6 8.4 %all-gather.1 = bf16[2,12,1408]{2,1,0:T(8,128)(2,1)S(1)} all-gather(bf16[1,12,1408]{2,1,0:T(8,128)(2,1)S(1)} %reshape.100), channel_id=1, replica_groups=mesh['z'=8,'y'=8,'c'=2,'x'=4] {'c'}, dimensions={0}, use_global_device_ids=true | all-gather | bytes 101376 | tf_op jit(solution)/shard_map/all_gather | solution.py:173
  20.1 20.7 %all_to_all.25 = bf16[8,24,1408]{2,1,0:T(8,128)(2,1)S(1)} all-to-all(bf16[8,24,1408]{2,1,0:T(8,128)(2,1)S(1)} %broadcast_in_dim.23), channel_id=1, replica_groups=mesh['z'=8,'y'=8,'c'=2,'x'=4] {'y'}, dimensions={0} | all-to-all | bytes 1081344 | tf_op jit(solution)/shard_map/all_to_all | solution.py:145
  40.8 0.1 fusion.4
  41.1 0.4 fusion.23
  41.5 0.9 broadcast_in_dim.24
  42.4 3.5 %all-to-all-start.1 = ((bf16[4,72,1280]{2,1,0:T(8,128)(2,1)}), bf16[4,72,1280]{2,1,0:T(8,128)(2,1)S(1)}, u32[]{:S(2)}, u32[]{:S(2)}) async-start(bf16[4,72,1280]{2,1,0:T(8,128)(2,1)} %broadcast_in_dim.24), calls=%async_computation.1 | async-start | bytes 1474560 | tf_op jit(solution)/shard_map/all_to_all | solution.py:145
  46.0 11.1 %all-to-all-done.1 = bf16[4,72,1280]{2,1,0:T(8,128)(2,1)S(1)} async-done(((bf16[4,72,1280]{2,1,0:T(8,128)(2,1)}), bf16[4,72,1280]{2,1,0:T(8,128)(2,1)S(1)}, u32[]{:S(2)}, u32[]{:S(2)}) %all-to-all-start.1) | async-done | bytes 737312 | tf_op jit(solution)/shard_map/all_to_all | solution.py:145
  57.2 0.3 fusion
  57.4 0.2 fusion.2.normed_ref
  57.7 25.3 %all-gather.6.cloned.1.call-done.head_ref = bf16[8,500,640]{2,1,0:T(8,128)(2,1)} async-done(((bf16[1,500,640]{2,1,0:T(8,128)(2,1)}), bf16[8,500,640]{2,1,0:T(8,128)(2,1)}) %all-gather.6.cloned.1.call-update) | async-done | bytes 5120016 | tf_op jit(solution)/shard_map/all_gather | solution.py:162
  83.0 2.5 %copy-done.1 = bf16[8,500,640]{2,1,0:T(8,128)(2,1)S(1)} copy-done((bf16[8,500,640]{2,1,0:T(8,128)(2,1)S(1)}, bf16[8,500,640]{2,1,0:T(8,128)(2,1)}, u32[]{:S(2)}) %copy-start.1) | copy-done | bytes 5120024
  85.4 3.2 %logits.1 = (f32[500,72]{1,0:T(8,128)S(1)}, f32[4,72]{1,0:T(4,128)S(1)}) custom-call(s32[1]{0:T(128)} %bitcast.5.first_ref, bf16[4,72,1280]{2,1,0:T(8,128)(2,1)S(1)} %fusion.2.normed_ref, bf16[8,500,640]{2,1,0:T(8,128)(2,1)S(1)} %copy-done.1, s32[1,72]{1,0:T(1,128)S(1)} %get-tuple-element.31.label_ref), custom_call_target="tpu_custom_call" | custom-call | tf_op jit(solution)/shard_map/logits/pallas_call | solution.py:53
  88.6 2.2 %all-gather.3 = f32[2,4,72]{2,1,0:T(4,128)S(1)} all-gather(f32[1,4,72]{2,1,0:T(4,128)S(1)} %bitcast.31), channel_id=1, replica_groups=mesh['z'=8,'y'=8,'c'=2,'x'=4] {'c'}, dimensions={0}, use_global_device_ids=true | all-gather | bytes 3456 | tf_op jit(solution)/shard_map/all_gather | solution.py:195
  90.8 18.5 %all_to_all.26.stats_ref = f32[32,8,72]{2,1,0:T(8,128)S(1)} all-to-all(f32[32,8,72]{2,1,0:T(8,128)S(1)} %broadcast_in_dim.25), channel_id=1, replica_groups=mesh['z'=8,'y'=8,'c'=2,'x'=4] {'y','x'}, dimensions={0} | all-to-all | bytes 147456 | tf_op jit(solution)/shard_map/all_to_all | solution.py:145
  109.3 2.4 %back.1 = (f32[4,72,640]{2,1,0:T(8,128)S(1)}, f32[4,72,640]{2,1,0:T(8,128)S(1)}, f32[1,72]{1,0:T(1,128)S(1)}, f32[2,1]{1,0:T(2,128)S(1)}) custom-call(s32[1]{0:T(128)} %bitcast.5.first_ref, s32[1]{0:T(128)} %bitcast.6.core_ref, f32[32,8,72]{2,1,0:T(8,128)S(1)} %all_to_all.26.stats_ref, f32[500,72]{1,0:T(8,128)S(1)} %get-tuple-element.9.logits_ref, ...), custom_call_target="tpu_custom_call" | custom-call | tf_op jit(solution)/shard_map/back/pallas_call | solution.py:118
  111.7 3.9 %collective-permute-start = (f32[4,72,640]{2,1,0:T(8,128)S(1)}, f32[4,72,640]{2,1,0:T(8,128)S(1)}, u32[]{:S(2)}, u32[]{:S(2)}) collective-permute-start(f32[4,72,640]{2,1,0:T(8,128)S(1)} %get-tuple-element.11), channel_id=1, source_target_pairs={{0,4},{4,0},{1,5},{5,1},{2,6},{6,2},{3,7},{7,3},{8,12},{12,8},{9,1... | collective-permute-start | bytes 2211848 | tf_op jit(solution)/shard_map/ppermute | solution.py:149
  115.6 1.8 %collective-permute-done = f32[4,72,640]{2,1,0:T(8,128)S(1)} collective-permute-done((f32[4,72,640]{2,1,0:T(8,128)S(1)}, f32[4,72,640]{2,1,0:T(8,128)S(1)}, u32[]{:S(2)}, u32[]{:S(2)}) %collective-permute-start) | collective-permute-done | bytes 737312 | tf_op jit(solution)/shard_map/ppermute | solution.py:149
  117.4 0.8 add_convert_fusion
  118.2 3.5 %all-to-all-start.3 = ((bf16[4,72,640]{2,1,0:T(8,128)(2,1)}), bf16[4,72,640]{2,1,0:T(8,128)(2,1)S(1)}, u32[]{:S(2)}, u32[]{:S(2)}) async-start(bf16[4,72,640]{2,1,0:T(8,128)(2,1)} %add_convert_fusion), calls=%async_computation.3 | async-start | bytes 737280 | tf_op jit(solution)/shard_map/all_to_all | solution.py:201
  121.8 7.4 %all-to-all-done.3 = bf16[4,72,640]{2,1,0:T(8,128)(2,1)S(1)} async-done(((bf16[4,72,640]{2,1,0:T(8,128)(2,1)}), bf16[4,72,640]{2,1,0:T(8,128)(2,1)S(1)}, u32[]{:S(2)}, u32[]{:S(2)}) %all-to-all-start.3) | async-done | bytes 368672 | tf_op jit(solution)/shard_map/all_to_all | solution.py:201
  129.3 1.0 convolution_convert_fusion
  130.2 3.4 %all-to-all-start.4 = ((bf16[8,24,640]{2,1,0:T(8,128)(2,1)}), bf16[8,24,640]{2,1,0:T(8,128)(2,1)S(1)}, u32[]{:S(2)}, u32[]{:S(2)}) async-start(bf16[8,24,640]{2,1,0:T(8,128)(2,1)} %bitcast.12), calls=%async_computation.4 | async-start | bytes 491520 | tf_op jit(solution)/shard_map/all_to_all | solution.py:205
  133.8 0.1 fusion.5
  133.9 9.4 %all-to-all-done.4 = bf16[8,24,640]{2,1,0:T(8,128)(2,1)S(1)} async-done(((bf16[8,24,640]{2,1,0:T(8,128)(2,1)}), bf16[8,24,640]{2,1,0:T(8,128)(2,1)S(1)}, u32[]{:S(2)}, u32[]{:S(2)}) %all-to-all-start.4) | async-done | bytes 245792 | tf_op jit(solution)/shard_map/all_to_all | solution.py:205
  143.4 4.7 %collective-permute-start.1 = (bf16[12,640]{1,0:T(8,128)(2,1)S(1)}, bf16[12,640]{1,0:T(8,128)(2,1)S(1)}, u32[]{:S(2)}, u32[]{:S(2)}) collective-permute-start(bf16[12,640]{1,0:T(8,128)(2,1)S(1)} %dynamic-slice_bitcast_fusion), channel_id=1, source_target_pairs={{0,4},{4,0},{1,5},{5,1},{2,6},{6,2},{3,7},{7,3},{8,12},{12,8},{9,1... | collective-permute-start | bytes 46088 | tf_op jit(solution)/shard_map/ppermute | solution.py:149
  148.1 0.6 copy.34
  148.7 0.2 collective-permute-done.1
  149.0 0.6 copy.33
  (48 shorter events, 1.8 us)
Async XLA Ops:
  7.2 3.4 %copy-start = (bf16[2,256,1280]{2,1,0:T(8,128)(2,1)S(1)}, bf16[2,256,1280]{2,1,0:T(8,128)(2,1)}, u32[]{:S(2)}) copy-start(bf16[2,256,1280]{2,1,0:T(8,128)(2,1)} %param.5) | copy-start | bytes 3932164
  7.2 2.9 %copy-start.4 = (s32[2,6]{1,0:T(2,128)S(1)}, s32[2,6]{1,0:T(2,128)}, u32[]{:S(2)}) copy-start(s32[2,6]{1,0:T(2,128)} %param.8) | copy-start | bytes 148
  7.2 75.8 %all-gather.6.cloned.1.call-start = ((), (), s32[]{:S(2)}) async-start(), calls=%async_computation.5 | async-start | bytes 5806080 | tf_op jit(solution)/shard_map/all_gather | solution.py:162
  41.4 4.5 %copy-start.3 = (bf16[5120]{0:T(1024)(128)(2,1)S(1)}, bf16[5120]{0:T(1024)(128)(2,1)}, u32[]{:S(2)}) copy-start(bf16[5120]{0:T(1024)(128)(2,1)} %param.6) | copy-start | bytes 30724
  42.4 14.8 %all-to-all-start.1 = ((bf16[4,72,1280]{2,1,0:T(8,128)(2,1)}), bf16[4,72,1280]{2,1,0:T(8,128)(2,1)S(1)}, u32[]{:S(2)}, u32[]{:S(2)}) async-start(bf16[4,72,1280]{2,1,0:T(8,128)(2,1)} %broadcast_in_dim.24), calls=%async_computation.1 | async-start | bytes 1474560 | tf_op jit(solution)/shard_map/all_to_all | solution.py:145
  83.0 2.5 %copy-start.1 = (bf16[8,500,640]{2,1,0:T(8,128)(2,1)S(1)}, bf16[8,500,640]{2,1,0:T(8,128)(2,1)}, u32[]{:S(2)}) copy-start(bf16[8,500,640]{2,1,0:T(8,128)(2,1)} %all-gather.6.cloned.1.call-done.head_ref) | copy-start | bytes 15360004
  85.4 23.8 %copy-start.2 = (bf16[8,500,640]{2,1,0:T(8,128)(2,1)S(1)}, bf16[8,500,640]{2,1,0:T(8,128)(2,1)}, u32[]{:S(2)}) copy-start(bf16[8,500,640]{2,1,0:T(8,128)(2,1)} %all-gather.6.cloned.1.call-done.head_ref) | copy-start | bytes 15360004
  111.7 5.8 %collective-permute-start = (f32[4,72,640]{2,1,0:T(8,128)S(1)}, f32[4,72,640]{2,1,0:T(8,128)S(1)}, u32[]{:S(2)}, u32[]{:S(2)}) collective-permute-start(f32[4,72,640]{2,1,0:T(8,128)S(1)} %get-tuple-element.11), channel_id=1, source_target_pairs={{0,4},{4,0},{1,5},{5,1},{2,6},{6,2},{3,7},{7,3},{8,12},{12,8},{9,1... | collective-permute-start | bytes 2211848 | tf_op jit(solution)/shard_map/ppermute | solution.py:149
  118.2 11.0 %all-to-all-start.3 = ((bf16[4,72,640]{2,1,0:T(8,128)(2,1)}), bf16[4,72,640]{2,1,0:T(8,128)(2,1)S(1)}, u32[]{:S(2)}, u32[]{:S(2)}) async-start(bf16[4,72,640]{2,1,0:T(8,128)(2,1)} %add_convert_fusion), calls=%async_computation.3 | async-start | bytes 737280 | tf_op jit(solution)/shard_map/all_to_all | solution.py:201
  130.2 13.0 %all-to-all-start.4 = ((bf16[8,24,640]{2,1,0:T(8,128)(2,1)}), bf16[8,24,640]{2,1,0:T(8,128)(2,1)S(1)}, u32[]{:S(2)}, u32[]{:S(2)}) async-start(bf16[8,24,640]{2,1,0:T(8,128)(2,1)} %bitcast.12), calls=%async_computation.4 | async-start | bytes 491520 | tf_op jit(solution)/shard_map/all_to_all | solution.py:205
  143.4 5.5 %collective-permute-start.1 = (bf16[12,640]{1,0:T(8,128)(2,1)S(1)}, bf16[12,640]{1,0:T(8,128)(2,1)S(1)}, u32[]{:S(2)}, u32[]{:S(2)}) collective-permute-start(bf16[12,640]{1,0:T(8,128)(2,1)S(1)} %dynamic-slice_bitcast_fusion), channel_id=1, source_target_pairs={{0,4},{4,0},{1,5},{5,1},{2,6},{6,2},{3,7},{7,3},{8,12},{12,8},{9,1... | collective-permute-start | bytes 46088 | tf_op jit(solution)/shard_map/ppermute | solution.py:149
Sparse Core Ops, SparseCore 0:
  10.1 72.7 all-gather.5

commit v2 on v1

v2 whole, which is shorter than its diff:
```python
import functools

import jax
import jax.numpy as jnp
from jax import lax
from jax.experimental import pallas as pl
from jax.experimental.pallas import tpu as pltpu
from jax.sharding import Mesh, PartitionSpec as P

EPS = 1e-05
LIVE = 72
SPAN = 500
PART = 256
EARLY = 5
WIDTH = 640
F32 = jnp.float32
BF16 = jnp.bfloat16


def params():
    return pltpu.CompilerParams(vmem_limit_bytes=56 * 1024 * 1024)


def fetch(refs, buffers, sem):
    copies = [pltpu.make_async_copy(ref, buf, sem.at[i]) for i, (ref, buf) in enumerate(zip(refs, buffers))]
    for copy in copies:
        copy.start()
    return copies


def scores(shard, normed_ref, head):
    normed = normed_ref[lax.rem(shard, 2), shard // 2]
    return lax.dot_general(head, normed, (((1,), (1,)), ((), ())), preferred_element_type=F32)


def first_kernel(meta_ref, normed_ref, *rest):
    refs, (logits_ref, full, sem) = rest[:EARLY], rest[EARLY:]
    copies = fetch(refs, [full.at[i] for i in range(EARLY)], sem)
    total = jnp.zeros((SPAN, LIVE), F32)
    for place, copy in enumerate(copies):
        copy.wait()
        total += scores(meta_ref[2 + place], normed_ref, full[place])
    logits_ref[...] = total


def logits_kernel(meta_ref, normed_ref, label_ref, first_ref, *rest):
    refs, (logits_ref, stats_ref, full, low, high, sem) = rest[: 9 - EARLY], rest[9 - EARLY :]
    count = 7 - EARLY
    copies = fetch(refs, [*(full.at[i] for i in range(count)), low, high], sem)
    total = first_ref[...]
    for i in range(count):
        copies[i].wait()
        total += scores(meta_ref[2 + EARLY + i], normed_ref, full[i])
    copies[count].wait()
    part = scores(meta_ref[9], normed_ref, low[...])
    copies[count + 1].wait()
    logits = total + jnp.concatenate([part, scores(meta_ref[9], normed_ref, high[...])], axis=0)
    logits_ref[...] = logits
    column = lax.broadcasted_iota(jnp.int32, (SPAN, LIVE), 0)
    hits = column + meta_ref[0] == label_ref[...]
    peak = jnp.max(logits, axis=0, keepdims=True)
    shifted = jnp.exp(logits - peak)
    stats_ref[0:1, :] = peak
    stats_ref[1:2, :] = jnp.sum(shifted, axis=0, keepdims=True)
    stats_ref[2:3, :] = jnp.sum(shifted * (logits - peak), axis=0, keepdims=True)
    stats_ref[3:4, :] = jnp.sum(jnp.where(hits, logits, 0.0), axis=0, keepdims=True)


VMEM = pl.BlockSpec(memory_space=pltpu.VMEM)
SMEM = pl.BlockSpec(memory_space=pltpu.SMEM)
ANY = pl.BlockSpec(memory_space=pl.ANY)


def head_scratch(full, halves):
    buffers = [pltpu.VMEM((full, SPAN, WIDTH), BF16)]
    if halves:
        buffers += [pltpu.VMEM((rows, WIDTH), BF16) for rows in (PART, SPAN - PART)]
    return [*buffers, pltpu.SemaphoreType.DMA((full + 2 * halves,))]


def local_logits(meta, normed, label, near):
    first = pl.pallas_call(
        first_kernel,
        in_specs=[SMEM, VMEM, *[ANY] * EARLY],
        out_specs=VMEM,
        out_shape=jax.ShapeDtypeStruct((SPAN, LIVE), F32),
        scratch_shapes=head_scratch(EARLY, 0),
        compiler_params=params(),
        cost_estimate=pl.CostEstimate(
            flops=2 * EARLY * SPAN * LIVE * WIDTH,
            bytes_accessed=2 * EARLY * SPAN * WIDTH,
            transcendentals=0,
        ),
        name="logits_early",
    )(meta, normed, *near[:EARLY])
    return pl.pallas_call(
        logits_kernel,
        in_specs=[SMEM, VMEM, VMEM, VMEM, *[ANY] * (9 - EARLY)],
        out_specs=[VMEM, VMEM],
        out_shape=[
            jax.ShapeDtypeStruct((SPAN, LIVE), F32),
            jax.ShapeDtypeStruct((4, LIVE), F32),
        ],
        scratch_shapes=head_scratch(7 - EARLY, 1),
        compiler_params=params(),
        name="logits",
    )(meta, normed, label, first, *near[EARLY:])


def back_kernel(meta_ref, stats_ref, logits_ref, label_ref, layer_ref, *rest):
    refs, (keep_ref, send_ref, row_ref, loss_ref, full, low, high, sem) = rest[:9], rest[9:]
    copies = fetch(refs, [*(full.at[i] for i in range(7)), low, high], sem)
    stats = stats_ref[...]
    peaks = [stats[:, 4 * c, :] for c in range(2)]
    peak = jnp.max(jnp.maximum(peaks[0], peaks[1]), axis=0, keepdims=True)
    mass = mean = aimed = jnp.zeros((1, LIVE), F32)
    for c in range(2):
        weight = jnp.exp(peaks[c] - peak)
        own = stats[:, 4 * c + 1, :]
        mass += jnp.sum(weight * own, axis=0, keepdims=True)
        moved = stats[:, 4 * c + 2, :] + (peaks[c] - peak) * own
        mean += jnp.sum(weight * moved, axis=0, keepdims=True)
        aimed += jnp.sum(stats[:, 4 * c + 3, :], axis=0, keepdims=True)
    row_ref[...] = mean / mass + (peak - aimed)
    loss = jnp.log(mass) + (peak - aimed)
    for layer in range(2):
        mine = (layer_ref[...] == layer).astype(F32)
        total = jnp.sum(loss * mine, axis=1, keepdims=True)
        loss_ref[layer : layer + 1, :] = total / jnp.sum(mine, axis=1, keepdims=True)
    logits = logits_ref[...]
    column = lax.broadcasted_iota(jnp.int32, (SPAN, LIVE), 0)
    hits = (column + meta_ref[0] == label_ref[...]).astype(F32)
    slope = (jnp.exp(logits - peak) / mass - hits).T.astype(BF16)
    for place in range(8):
        shard = meta_ref[2 + place]
        copies[place].wait()
        if place < 7:
            part = jnp.dot(slope, full[place], preferred_element_type=F32)
        else:
            copies[8].wait()
            part = jnp.dot(slope[:, :PART], low[...], preferred_element_type=F32)
            part += jnp.dot(slope[:, PART:], high[...], preferred_element_type=F32)
        kept = lax.rem(shard, 2) == meta_ref[1]

        @pl.when(kept)
        def _():
            keep_ref[shard // 2] = part

        @pl.when(jnp.logical_not(kept))
        def _():
            send_ref[shard // 2] = part


def local_back(meta, stats, logits, label, layer, near):
    half = (4, LIVE, WIDTH)
    return pl.pallas_call(
        back_kernel,
        in_specs=[SMEM, VMEM, VMEM, VMEM, VMEM, *[ANY] * 9],
        out_specs=[VMEM] * 4,
        out_shape=[
            jax.ShapeDtypeStruct(half, F32),
            jax.ShapeDtypeStruct(half, F32),
            jax.ShapeDtypeStruct((1, LIVE), F32),
            jax.ShapeDtypeStruct((2, 1), F32),
        ],
        scratch_shapes=head_scratch(7, 1),
        compiler_params=params(),
        name="back",
    )(meta, stats, logits, label, layer, *near)


def spread(values, axes, count):
    copies = jnp.broadcast_to(values[None], (count, *values.shape))
    return lax.all_to_all(copies, axes, 0, 0, tiled=True)


def swap_core(values):
    return lax.ppermute(values, "c", [(0, 1), (1, 0)])


def ring(own):
    up = [(i, (i + 1) % 8) for i in range(8)]
    down = [(i, (i - 1) % 8) for i in range(8)]
    right = left = own
    near = [own]
    for _ in range(3):
        right = lax.ppermute(right, "z", up)
        left = lax.ppermute(left, "z", down)
        near += [right, left]
    near.append(lax.ppermute(right[:PART], "z", up))
    near.append(lax.ppermute(left[PART:], "z", down))
    return near


def body(hidden, gain, head, exit_slots, targets):
    layers, row_dev, part_width = hidden.shape
    most = exit_slots.shape[1]
    own = layers * most
    width = gain.shape[0]
    half = part_width // 2
    z, y, c, x = (lax.axis_index(name) for name in ("z", "y", "c", "x"))
    shards = [lax.rem(z + s, 8) for s in (0, 7, 1, 6, 2, 5, 3, 4)]
    first = ((y * 2 + c) * 4 + x) * SPAN
    meta = jnp.stack([first, c, *shards]).astype(jnp.int32)
    near = ring(head.T)

    live = exit_slots < row_dev
    local = jnp.minimum(exit_slots, row_dev - 1)
    picked = jax.vmap(lambda block, index: block[index])(hidden, local)
    picked = jnp.where(live[:, :, None], picked, jnp.zeros_like(picked))
    label = jnp.where(live, targets[local], 0)
    layer = jnp.broadcast_to(jnp.arange(layers)[:, None], live.shape)
    facts = jnp.stack([live.astype(jnp.int32), label // 256, label % 256, layer], axis=2)
    facts = jnp.pad(facts.astype(BF16), ((0, 0), (0, 0), (0, 124)))
    packed = jnp.concatenate([picked, facts], axis=2).reshape(own, part_width + 128)
    pair = lax.all_gather(packed, "c", axis=0, tiled=True)
    pair_half = lax.dynamic_slice_in_dim(pair, c * half, half, 1)
    slots = jnp.concatenate([pair_half, pair[:, part_width:]], axis=1)
    slots = spread(slots, "y", 8).reshape(16 * own, half + 128)

    total = slots.shape[0]
    flag = slots[:, half].astype(F32)
    below = (jnp.arange(total)[:, None] < jnp.arange(total)[None, :]).astype(F32)
    rank = jnp.sum(below * flag[:, None], axis=0)
    place = (rank[None, :] == jnp.arange(LIVE, dtype=F32)[:, None]) & (flag > 0)[None, :]
    place = place.astype(BF16)
    compact = jnp.dot(place, slots, preferred_element_type=F32)
    fact = compact[:, half : half + 4].astype(jnp.int32).T
    label_row = (fact[1] * 256 + fact[2]).reshape(1, LIVE)
    layer_row = fact[3].reshape(1, LIVE)
    rows = spread(compact[:, :half].astype(BF16), "x", 4)
    rows = lax.all_gather(rows, "c", axis=0)

    values = rows.astype(F32)
    scale = lax.rsqrt(jnp.sum(values * values, axis=(0, 1, 3)) / width + EPS)
    gain_f = gain.astype(F32)
    gain_rows = gain_f.reshape(4, 2, 1, half).transpose(1, 0, 2, 3)
    normed = (values * scale[:, None] * gain_rows).astype(BF16)

    logits, stats = local_logits(meta, normed, label_row, near)
    stats = lax.all_gather(stats, "c", axis=0, tiled=True)
    stats = spread(stats, ("y", "x"), 32)
    keep, send, gap, group_loss = local_back(
        meta, stats, logits, label_row, layer_row, near
    )
    part = (keep + swap_core(send)).astype(BF16)
    part = lax.all_to_all(part, "x", 0, 0, tiled=True)
    part = jnp.sum(part.astype(F32), axis=0).astype(BF16)
    sent = lax.dot_general(place, part, (((0,), (0,)), ((), ())), preferred_element_type=F32)
    sent = sent.astype(BF16).reshape(8, 2 * own, half)
    back = jnp.sum(lax.all_to_all(sent, "y", 0, 0, tiled=True).astype(F32), axis=0)

    start = x * part_width + c * half
    gain_half = lax.dynamic_slice_in_dim(gain_f, start, half)
    value_half = pair_half.astype(F32)
    mine = lax.dynamic_slice_in_dim(place, y * 2 * own, 2 * own, 1).astype(F32)
    scale_own = jnp.sum(mine * scale[:, None], axis=0)
    shift_own = jnp.sum(mine * (scale**2 * gap[0] / width)[:, None], axis=0)
    grads = scale_own[:, None] * gain_half * back - value_half * shift_own[:, None]
    grads = grads.astype(BF16).reshape(2, own, half)
    kept = lax.dynamic_index_in_dim(grads, c, 0, keepdims=False)
    came = swap_core(lax.dynamic_index_in_dim(grads, 1 - c, 0, keepdims=False))
    low = jnp.where(c == 0, kept, came)
    high = jnp.where(c == 0, came, kept)
    exit_grads = jnp.concatenate([low, high], axis=1).reshape(layers, most, part_width)
    return exit_grads, group_loss


def solution(mesh):
    split = Mesh(mesh.devices.reshape(8, 8, 2, 4), ("z", "y", "c", "x"))
    in_specs = (
        P(None, ("z", "y", "c"), "x"),
        P(),
        P("z", ("y", "c", "x")),
        P(None, ("z", "y", "c")),
        P(("z", "y", "c")),
    )
    out_specs = (P(None, ("z", "y", "c"), "x"), P(None, "z"))
    return jax.shard_map(body, mesh=split, in_specs=in_specs, out_specs=out_specs, check_vma=False)
```

time: 157 us -> 153 us (0.975)
  starting transfers between devices: 19 us -> 59.6 us
  waiting for transfers between devices: 55.9 us -> 28.9 us
  blocking collectives: 49.7 us -> 29.9 us
  between operations: 14.3 us -> 1.14 us
  Pallas kernels: 5.61 us -> 14.8 us
  other arithmetic: 3 us -> 7.6 us
    ppermute x0 -> x8, starting transfers between devices: none -> 33 us  [the longest x3 17.7 us: ring(): left = lax.ppermute(left, 'z', down)]
    all_gather x1 -> x0, waiting for transfers between devices: 25.3 us -> none  [body(): full_head = lax.all_gather(head.T, 'z', axis=0)]
    all_to_all x2 -> x1, blocking collectives: 39.1 us -> 18.5 us  [spread(): return lax.all_to_all(copies, axes, 0, 0, tiled=True)]
    pallas_call x2 -> x3, Pallas kernels: 5.61 us -> 14.8 us  [the longest x1 5.38 us: local_back(): pl.pallas_call(back_kernel, in_specs=[SMEM, VMEM, VMEM, VMEM, VMEM, *[ANY...]
    all_to_all x1 -> x2, starting transfers between devices: 3.49 us -> 10.9 us  [spread(): return lax.all_to_all(copies, axes, 0, 0, tiled=True)]
    all_to_all x1 -> x2, waiting for transfers between devices: 11.1 us -> 4.59 us  [spread(): return lax.all_to_all(copies, axes, 0, 0, tiled=True)]
    all_gather x1, blocking collectives: 8.4 us -> 2.48 us  [body(): pair = lax.all_gather(packed, 'c', axis=0, tiled=True)]
    ppermute x0 -> x8, waiting for transfers between devices: none -> 5.29 us  [the longest x3 5.28 us: ring(): right = lax.ppermute(right, 'z', up)]
  transfers between devices with their start and end apart: 6 -> 14, of which waited for: 6 -> 7; matrix products, arithmetic and copies ran while one was open for 4% -> 8% of each run, Pallas kernels for 0% -> 3%
where the time goes in v2:
time: 153 us; the launch traced here: 152 us
  starting transfers between devices  59.6 us (39%)
  blocking collectives  29.9 us (20%)
  waiting for transfers between devices  28.9 us (19%)
  Pallas kernels  14.8 us (10%)
  local copies, waits for them, and re-layouts  8.71 us (6%)
  other arithmetic  7.6 us (5%)
    all_to_all x1, blocking collectives, spread(): return lax.all_to_all(copies, axes, 0, 0, tiled=True)  18.5 us
    ppermute x3, starting transfers between devices, ring(): left = lax.ppermute(left, 'z', down)  17.7 us
    all_to_all x2, starting transfers between devices, spread(): return lax.all_to_all(copies, axes, 0, 0, tiled=True)  10.9 us
    all_to_all x1, waiting for transfers between devices, body(): lax.all_to_all(sent, 'y', 0, 0, tiled=True).astype(F32)  9.34 us
    ppermute x3, starting transfers between devices, ring(): right = lax.ppermute(right, 'z', up)  8.79 us
    ppermute x2, starting transfers between devices, swap_core(): return lax.ppermute(values, 'c', [(0, 1), (1, 0)])  8.63 us
    all_to_all x1, waiting for transfers between devices, body(): part = lax.all_to_all(part, 'x', 0, 0, tiled=True)  7.43 us
    pallas_call x1, Pallas kernels, local_back(): pl.pallas_call(back_kernel, in_specs=[SMEM, VMEM, VMEM, VMEM, VMEM, *[ANY...  5.38 us
  transfers between devices with their start and end apart: 14, of which 7 were waited for; matrix products, arithmetic and copies ran while one was open for 8% of the time, Pallas kernels for 3%

profile of v2, /device:TPU:1, one launch (start us, length us, event | category | flops | bytes accessed | tf_op | source)
XLA Modules:
  0.0 151.9 jit_solution(2051113280375469936)
XLA Ops:
  0.6 5.0 %collective-permute-start = (bf16[500,640]{1,0:T(8,128)(2,1)}, bf16[500,640]{1,0:T(8,128)(2,1)S(1)}, u32[]{:S(2)}, u32[]{:S(2)}) collective-permute-start(bf16[500,640]{1,0:T(8,128)(2,1)} %bitcast.44), channel_id=1, source_target_pairs={{0,64},{64,128},{128,192},{192,256},{256,320},{320,384},{384,448},... | collective-permute-start | bytes 1920008 | tf_op jit(solution)/shard_map/ppermute | solution.py:187
  5.6 8.6 %collective-permute-start.1 = (bf16[500,640]{1,0:T(8,128)(2,1)}, bf16[500,640]{1,0:T(8,128)(2,1)S(1)}, u32[]{:S(2)}, u32[]{:S(2)}) collective-permute-start(bf16[500,640]{1,0:T(8,128)(2,1)} %bitcast.45), channel_id=1, source_target_pairs={{0,448},{64,0},{128,64},{192,128},{256,192},{320,256},{384,320},{4... | collective-permute-start | bytes 1920008 | tf_op jit(solution)/shard_map/ppermute | solution.py:188
  16.4 1.3 gather_fusion
  19.2 2.5 %all-gather.1 = bf16[2,12,1408]{2,1,0:T(8,128)(2,1)S(1)} all-gather(bf16[1,12,1408]{2,1,0:T(8,128)(2,1)S(1)} %reshape.93), channel_id=1, replica_groups=mesh['z'=8,'y'=8,'c'=2,'x'=4] {'c'}, dimensions={0}, use_global_device_ids=true | all-gather | bytes 101376 | tf_op jit(solution)/shard_map/all_gather | solution.py:216
  22.5 6.8 %all-to-all-start = ((bf16[8,24,768]{2,1,0:T(8,128)(2,1)}), bf16[8,24,768]{2,1,0:T(8,128)(2,1)S(1)}, u32[]{:S(2)}, u32[]{:S(2)}) async-start(bf16[8,24,768]{2,1,0:T(8,128)(2,1)} %broadcast_in_dim.23), calls=%async_computation | async-start | bytes 589824 | tf_op jit(solution)/shard_map/all_to_all | solution.py:174
  29.3 1.9 %collective-permute-start.2 = (bf16[500,640]{1,0:T(8,128)(2,1)S(1)}, bf16[500,640]{1,0:T(8,128)(2,1)}, u32[]{:S(2)}, u32[]{:S(2)}) collective-permute-start(bf16[500,640]{1,0:T(8,128)(2,1)S(1)} %collective-permute-done.rest_1_), channel_id=1, source_target_pairs={{0,64},{64,128},{128,192},{192,256},{256,320},{320,384},{384,448},... | collective-permute-start | bytes 1920008 | tf_op jit(solution)/shard_map/ppermute | solution.py:187
  31.3 4.6 %collective-permute-start.3 = (bf16[500,640]{1,0:T(8,128)(2,1)S(1)}, bf16[500,640]{1,0:T(8,128)(2,1)}, u32[]{:S(2)}, u32[]{:S(2)}) collective-permute-start(bf16[500,640]{1,0:T(8,128)(2,1)S(1)} %collective-permute-done.1.rest_2_), channel_id=1, source_target_pairs={{0,448},{64,0},{128,64},{192,128},{256,192},{320,256},{384,320},{4... | collective-permute-start | bytes 1920008 | tf_op jit(solution)/shard_map/ppermute | solution.py:188
  37.2 4.6 %all-to-all-done = bf16[8,24,768]{2,1,0:T(8,128)(2,1)S(1)} async-done(((bf16[8,24,768]{2,1,0:T(8,128)(2,1)}), bf16[8,24,768]{2,1,0:T(8,128)(2,1)S(1)}, u32[]{:S(2)}, u32[]{:S(2)}) %all-to-all-start) | async-done | bytes 294944 | tf_op jit(solution)/shard_map/all_to_all | solution.py:174
  42.5 0.8 broadcast_in_dim.24
  43.2 4.1 %all-to-all-start.1 = ((bf16[4,72,640]{2,1,0:T(8,128)(2,1)}), bf16[4,72,640]{2,1,0:T(8,128)(2,1)}, u32[]{:S(2)}, u32[]{:S(2)}) async-start(bf16[4,72,640]{2,1,0:T(8,128)(2,1)} %broadcast_in_dim.24), calls=%async_computation.1 | async-start | bytes 737280 | tf_op jit(solution)/shard_map/all_to_all | solution.py:174
  48.0 1.9 %collective-permute-start.4 = (bf16[500,640]{1,0:T(8,128)(2,1)}, bf16[500,640]{1,0:T(8,128)(2,1)S(1)}, u32[]{:S(2)}, u32[]{:S(2)}) collective-permute-start(bf16[500,640]{1,0:T(8,128)(2,1)} %collective-permute-done.2.rest_3_), channel_id=1, source_target_pairs={{0,64},{64,128},{128,192},{192,256},{256,320},{320,384},{384,448},... | collective-permute-start | bytes 1920008 | tf_op jit(solution)/shard_map/ppermute | solution.py:187
  49.9 4.6 %collective-permute-start.5 = (bf16[500,640]{1,0:T(8,128)(2,1)}, bf16[500,640]{1,0:T(8,128)(2,1)S(1)}, u32[]{:S(2)}, u32[]{:S(2)}) collective-permute-start(bf16[500,640]{1,0:T(8,128)(2,1)} %collective-permute-done.3.rest_4_), channel_id=1, source_target_pairs={{0,448},{64,0},{128,64},{192,128},{256,192},{320,256},{384,320},{4... | collective-permute-start | bytes 1920008 | tf_op jit(solution)/shard_map/ppermute | solution.py:188
  55.1 0.8 copy.40
  56.5 4.3 %all-gather = bf16[8,72,640]{2,1,0:T(8,128)(2,1)S(1)} all-gather(bf16[4,72,640]{2,1,0:T(8,128)(2,1)} %all-to-all-done.1), channel_id=2, replica_groups=mesh['z'=8,'y'=8,'c'=2,'x'=4] {'c'}, dimensions={0}, use_global_device_ids=true | all-gather | bytes 1105920 | tf_op jit(solution)/shard_map/all_gather | solution.py:232
  61.1 4.7 %collective-permute-done.4.rest_0_.rest_5_ = bf16[500,640]{1,0:T(8,128)(2,1)S(1)} collective-permute-done((bf16[500,640]{1,0:T(8,128)(2,1)}, bf16[500,640]{1,0:T(8,128)(2,1)S(1)}, u32[]{:S(2)}, u32[]{:S(2)}) %collective-permute-start.4) | collective-permute-done | bytes 640032 | tf_op jit(solution)/shard_map/ppermute | solution.py:187
  65.8 1.9 %collective-permute-start.6 = (bf16[256,640]{1,0:T(8,128)(2,1)S(1)}, bf16[256,640]{1,0:T(8,128)(2,1)S(1)}, u32[]{:S(2)}, u32[]{:S(2)}) collective-permute-start(bf16[256,640]{1,0:T(8,128)(2,1)S(1)} %slice.45), channel_id=1, source_target_pairs={{0,64},{64,128},{128,192},{192,256},{256,320},{320,384},{384,448},... | collective-permute-start | bytes 983048 | tf_op jit(solution)/shard_map/ppermute | solution.py:190
  67.8 4.6 %collective-permute-start.7 = (bf16[244,640]{1,0:T(8,128)(2,1)S(1)}, bf16[244,640]{1,0:T(8,128)(2,1)S(1)}, u32[]{:S(2)}, u32[]{:S(2)}) collective-permute-start(bf16[244,640]{1,0:T(8,128)(2,1)S(1)} %slice.46), channel_id=1, source_target_pairs={{0,448},{64,0},{128,64},{192,128},{256,192},{320,256},{384,320},{4... | collective-permute-start | bytes 936968 | tf_op jit(solution)/shard_map/ppermute | solution.py:191
  72.4 1.1 fusion.2.normed_ref
  73.6 5.0 %logits_early.1.first_ref = f32[500,72]{1,0:T(8,128)} custom-call(s32[10]{0:T(128)} %stack.66.meta_ref, bf16[2,4,72,640]{3,2,1,0:T(8,128)(2,1)} %fusion.2.normed_ref, bf16[500,640]{1,0:T(8,128)(2,1)} %bitcast.46, bf16[500,640]{1,0:T(8,128)(2,1)} %copy-done.3, bf16[500,640]{1,0:T(8,128)(2,1)} %copy-done.4, bf16[500,640]{1,0:T(8,128)(2,1)} %collective-permute-done.2.rest_3_, ...), custom_call_target="tpu_custom_call" | custom-call | flops 230400000 | bytes 3200000 | tf_op jit(solution)/shard_map/logits_early/pallas_call | solution.py:82
  79.4 4.4 %logits.1 = (f32[500,72]{1,0:T(8,128)}, f32[4,72]{1,0:T(4,128)}) custom-call(s32[10]{0:T(128)} %stack.66.meta_ref, bf16[2,4,72,640]{3,2,1,0:T(8,128)(2,1)} %fusion.2.normed_ref, s32[1,72]{1,0:T(1,128)} %get-tuple-element.31.label_ref, f32[500,72]{1,0:T(8,128)} %logits_early.1.first_ref, bf16[500,640]{1,0:T(8,128)(2,1)} %copy-done.1, ...), custom_call_target="tpu_custom_call" | custom-call | tf_op jit(solution)/shard_map/logits/pallas_call | solution.py:96
  83.9 4.6 %all-gather.2 = f32[2,4,72]{2,1,0:T(4,128)S(1)} all-gather(f32[1,4,72]{2,1,0:T(4,128)} %bitcast.54), channel_id=1, replica_groups=mesh['z'=8,'y'=8,'c'=2,'x'=4] {'c'}, dimensions={0}, use_global_device_ids=true | all-gather | bytes 3456 | tf_op jit(solution)/shard_map/all_gather | solution.py:241
  88.5 18.5 %all_to_all.25.stats_ref = f32[32,8,72]{2,1,0:T(8,128)} all-to-all(f32[32,8,72]{2,1,0:T(8,128)S(1)} %broadcast_in_dim.25), channel_id=1, replica_groups=mesh['z'=8,'y'=8,'c'=2,'x'=4] {'y','x'}, dimensions={0} | all-to-all | bytes 147456 | tf_op jit(solution)/shard_map/all_to_all | solution.py:174
  106.9 5.4 %back.1 = (f32[4,72,640]{2,1,0:T(8,128)}, f32[4,72,640]{2,1,0:T(8,128)}, f32[1,72]{1,0:T(1,128)}, f32[2,1]{1,0:T(2,128)}) custom-call(s32[10]{0:T(128)} %stack.66.meta_ref, f32[32,8,72]{2,1,0:T(8,128)} %all_to_all.25.stats_ref, f32[500,72]{1,0:T(8,128)} %get-tuple-element.9.logits_ref, s32[1,72]{1,0:T(1,128)} %get-tuple-element.31.label_ref, ...), custom_call_target="tpu_custom_call" | custom-call | tf_op jit(solution)/shard_map/back/pallas_call | solution.py:156
  112.3 3.9 %collective-permute-start.8 = (f32[4,72,640]{2,1,0:T(8,128)}, f32[4,72,640]{2,1,0:T(8,128)S(1)}, u32[]{:S(2)}, u32[]{:S(2)}) collective-permute-start(f32[4,72,640]{2,1,0:T(8,128)} %get-tuple-element.11), channel_id=1, source_target_pairs={{0,4},{4,0},{1,5},{5,1},{2,6},{6,2},{3,7},{7,3},{8,12},{12,8},{9,1... | collective-permute-start | bytes 2211848 | tf_op jit(solution)/shard_map/ppermute | solution.py:178
  116.3 2.0 %collective-permute-done.8 = f32[4,72,640]{2,1,0:T(8,128)S(1)} collective-permute-done((f32[4,72,640]{2,1,0:T(8,128)}, f32[4,72,640]{2,1,0:T(8,128)S(1)}, u32[]{:S(2)}, u32[]{:S(2)}) %collective-permute-start.8) | collective-permute-done | bytes 737312 | tf_op jit(solution)/shard_map/ppermute | solution.py:178
  118.3 2.0 %add_convert_fusion = bf16[4,72,640]{2,1,0:T(8,128)(2,1)} fusion(f32[4,72,640]{2,1,0:T(8,128)} %get-tuple-element.10, f32[4,72,640]{2,1,0:T(8,128)S(1)} %collective-permute-done.8), kind=kLoop, calls=%fused_computation.8 | loop fusion | flops 368640 | bytes 1843200 | tf_op jit(solution)/shard_map/convert_element_type | solution.py:246
  120.3 3.6 %all-to-all-start.3 = ((bf16[4,72,640]{2,1,0:T(8,128)(2,1)}), bf16[4,72,640]{2,1,0:T(8,128)(2,1)S(1)}, u32[]{:S(2)}, u32[]{:S(2)}) async-start(bf16[4,72,640]{2,1,0:T(8,128)(2,1)} %add_convert_fusion), calls=%async_computation.3 | async-start | bytes 737280 | tf_op jit(solution)/shard_map/all_to_all | solution.py:247
  124.0 7.4 %all-to-all-done.3 = bf16[4,72,640]{2,1,0:T(8,128)(2,1)S(1)} async-done(((bf16[4,72,640]{2,1,0:T(8,128)(2,1)}), bf16[4,72,640]{2,1,0:T(8,128)(2,1)S(1)}, u32[]{:S(2)}, u32[]{:S(2)}) %all-to-all-start.3) | async-done | bytes 368672 | tf_op jit(solution)/shard_map/all_to_all | solution.py:247
  131.5 1.0 convolution_convert_fusion
  132.5 3.4 %all-to-all-start.4 = ((bf16[8,24,640]{2,1,0:T(8,128)(2,1)}), bf16[8,24,640]{2,1,0:T(8,128)(2,1)S(1)}, u32[]{:S(2)}, u32[]{:S(2)}) async-start(bf16[8,24,640]{2,1,0:T(8,128)(2,1)} %bitcast.23), calls=%async_computation.4 | async-start | bytes 491520 | tf_op jit(solution)/shard_map/all_to_all | solution.py:251
  136.2 9.3 %all-to-all-done.4 = bf16[8,24,640]{2,1,0:T(8,128)(2,1)S(1)} async-done(((bf16[8,24,640]{2,1,0:T(8,128)(2,1)}), bf16[8,24,640]{2,1,0:T(8,128)(2,1)S(1)}, u32[]{:S(2)}, u32[]{:S(2)}) %all-to-all-start.4) | async-done | bytes 245792 | tf_op jit(solution)/shard_map/all_to_all | solution.py:251
  145.7 4.7 %collective-permute-start.9 = (bf16[12,640]{1,0:T(8,128)(2,1)S(1)}, bf16[12,640]{1,0:T(8,128)(2,1)S(1)}, u32[]{:S(2)}, u32[]{:S(2)}) collective-permute-start(bf16[12,640]{1,0:T(8,128)(2,1)S(1)} %dynamic-slice_bitcast_fusion), channel_id=1, source_target_pairs={{0,4},{4,0},{1,5},{5,1},{2,6},{6,2},{3,7},{7,3},{8,12},{12,8},{9,1... | collective-permute-start | bytes 46088 | tf_op jit(solution)/shard_map/ppermute | solution.py:178
  (91 shorter events, 11.4 us)
Async XLA Ops:
  0.6 17.6 %copy-start = (bf16[2,256,1280]{2,1,0:T(8,128)(2,1)S(1)}, bf16[2,256,1280]{2,1,0:T(8,128)(2,1)}, u32[]{:S(2)}) copy-start(bf16[2,256,1280]{2,1,0:T(8,128)(2,1)} %param.5) | copy-start | bytes 3932164
  0.6 28.7 %collective-permute-start = (bf16[500,640]{1,0:T(8,128)(2,1)}, bf16[500,640]{1,0:T(8,128)(2,1)S(1)}, u32[]{:S(2)}, u32[]{:S(2)}) collective-permute-start(bf16[500,640]{1,0:T(8,128)(2,1)} %bitcast.44), channel_id=1, source_target_pairs={{0,64},{64,128},{128,192},{192,256},{256,320},{320,384},{384,448},... | collective-permute-start | bytes 1920008 | tf_op jit(solution)/shard_map/ppermute | solution.py:187
  5.6 25.7 %collective-permute-start.1 = (bf16[500,640]{1,0:T(8,128)(2,1)}, bf16[500,640]{1,0:T(8,128)(2,1)S(1)}, u32[]{:S(2)}, u32[]{:S(2)}) collective-permute-start(bf16[500,640]{1,0:T(8,128)(2,1)} %bitcast.45), channel_id=1, source_target_pairs={{0,448},{64,0},{128,64},{192,128},{256,192},{320,256},{384,320},{4... | collective-permute-start | bytes 1920008 | tf_op jit(solution)/shard_map/ppermute | solution.py:188
  17.7 18.2 %copy-start.8 = (bf16[5120]{0:T(1024)(128)(2,1)S(1)}, bf16[5120]{0:T(1024)(128)(2,1)}, u32[]{:S(2)}) copy-start(bf16[5120]{0:T(1024)(128)(2,1)} %param.6) | copy-start | bytes 30724
  22.5 19.3 %all-to-all-start = ((bf16[8,24,768]{2,1,0:T(8,128)(2,1)}), bf16[8,24,768]{2,1,0:T(8,128)(2,1)S(1)}, u32[]{:S(2)}, u32[]{:S(2)}) async-start(bf16[8,24,768]{2,1,0:T(8,128)(2,1)} %broadcast_in_dim.23), calls=%async_computation | async-start | bytes 589824 | tf_op jit(solution)/shard_map/all_to_all | solution.py:174
  29.3 31.5 %copy-start.3 = (bf16[500,640]{1,0:T(8,128)(2,1)}, bf16[500,640]{1,0:T(8,128)(2,1)S(1)}, u32[]{:S(2)}) copy-start(bf16[500,640]{1,0:T(8,128)(2,1)S(1)} %collective-permute-done.rest_1_) | copy-start | bytes 1920004
  29.3 18.6 %collective-permute-start.2 = (bf16[500,640]{1,0:T(8,128)(2,1)S(1)}, bf16[500,640]{1,0:T(8,128)(2,1)}, u32[]{:S(2)}, u32[]{:S(2)}) collective-permute-start(bf16[500,640]{1,0:T(8,128)(2,1)S(1)} %collective-permute-done.rest_1_), channel_id=1, source_target_pairs={{0,64},{64,128},{128,192},{192,256},{256,320},{320,384},{384,448},... | collective-permute-start | bytes 1920008 | tf_op jit(solution)/shard_map/ppermute | solution.py:187
  31.3 18.6 %copy-start.4 = (bf16[500,640]{1,0:T(8,128)(2,1)}, bf16[500,640]{1,0:T(8,128)(2,1)S(1)}, u32[]{:S(2)}) copy-start(bf16[500,640]{1,0:T(8,128)(2,1)S(1)} %collective-permute-done.1.rest_2_) | copy-start | bytes 1920004
  31.3 18.6 %collective-permute-start.3 = (bf16[500,640]{1,0:T(8,128)(2,1)S(1)}, bf16[500,640]{1,0:T(8,128)(2,1)}, u32[]{:S(2)}, u32[]{:S(2)}) collective-permute-start(bf16[500,640]{1,0:T(8,128)(2,1)S(1)} %collective-permute-done.1.rest_2_), channel_id=1, source_target_pairs={{0,448},{64,0},{128,64},{192,128},{256,192},{320,256},{384,320},{4... | collective-permute-start | bytes 1920008 | tf_op jit(solution)/shard_map/ppermute | solution.py:188
  42.0 5.3 %copy-start.11 = (pred[192]{0:T(512)(128)(4,1)}, pred[192]{0:T(512)(128)(4,1)S(1)}, u32[]{:S(2)}) copy-start(pred[192]{0:T(512)(128)(4,1)S(1)} %fusion.4) | copy-start | bytes 580
  42.1 5.2 %copy-start.9 = (f32[192]{0:T(256)}, f32[192]{0:T(256)S(1)}, u32[]{:S(2)}) copy-start(f32[192]{0:T(256)S(1)} %select_reduce_fusion) | copy-start | bytes 2308
  43.2 13.3 %all-to-all-start.1 = ((bf16[4,72,640]{2,1,0:T(8,128)(2,1)}), bf16[4,72,640]{2,1,0:T(8,128)(2,1)}, u32[]{:S(2)}, u32[]{:S(2)}) async-start(bf16[4,72,640]{2,1,0:T(8,128)(2,1)} %broadcast_in_dim.24), calls=%async_computation.1 | async-start | bytes 737280 | tf_op jit(solution)/shard_map/all_to_all | solution.py:174
  48.0 17.8 %collective-permute-start.4 = (bf16[500,640]{1,0:T(8,128)(2,1)}, bf16[500,640]{1,0:T(8,128)(2,1)S(1)}, u32[]{:S(2)}, u32[]{:S(2)}) collective-permute-start(bf16[500,640]{1,0:T(8,128)(2,1)} %collective-permute-done.2.rest_3_), channel_id=1, source_target_pairs={{0,64},{64,128},{128,192},{192,256},{256,320},{320,384},{384,448},... | collective-permute-start | bytes 1920008 | tf_op jit(solution)/shard_map/ppermute | solution.py:187
  49.9 17.8 %collective-permute-start.5 = (bf16[500,640]{1,0:T(8,128)(2,1)}, bf16[500,640]{1,0:T(8,128)(2,1)S(1)}, u32[]{:S(2)}, u32[]{:S(2)}) collective-permute-start(bf16[500,640]{1,0:T(8,128)(2,1)} %collective-permute-done.3.rest_4_), channel_id=1, source_target_pairs={{0,448},{64,0},{128,64},{192,128},{256,192},{320,256},{384,320},{4... | collective-permute-start | bytes 1920008 | tf_op jit(solution)/shard_map/ppermute | solution.py:188
  56.5 15.9 %copy-start.7 = (f32[2,4,640]{2,1,0:T(4,128)S(1)}, f32[2,4,640]{2,1,0:T(4,128)}, u32[]{:S(2)}) copy-start(f32[2,4,640]{2,1,0:T(4,128)} %copy.35) | copy-start | bytes 61444
  65.8 7.8 %copy-start.1 = (bf16[500,640]{1,0:T(8,128)(2,1)}, bf16[500,640]{1,0:T(8,128)(2,1)S(1)}, u32[]{:S(2)}) copy-start(bf16[500,640]{1,0:T(8,128)(2,1)S(1)} %collective-permute-done.4.rest_0_.rest_5_) | copy-start | bytes 1920004
  65.8 12.8 %collective-permute-start.6 = (bf16[256,640]{1,0:T(8,128)(2,1)S(1)}, bf16[256,640]{1,0:T(8,128)(2,1)S(1)}, u32[]{:S(2)}, u32[]{:S(2)}) collective-permute-start(bf16[256,640]{1,0:T(8,128)(2,1)S(1)} %slice.45), channel_id=1, source_target_pairs={{0,64},{64,128},{128,192},{192,256},{256,320},{320,384},{384,448},... | collective-permute-start | bytes 983048 | tf_op jit(solution)/shard_map/ppermute | solution.py:190
  67.8 10.8 %copy-start.2 = (bf16[500,640]{1,0:T(8,128)(2,1)}, bf16[500,640]{1,0:T(8,128)(2,1)S(1)}, u32[]{:S(2)}) copy-start(bf16[500,640]{1,0:T(8,128)(2,1)S(1)} %collective-permute-done.5.rest_1_.rest_6_) | copy-start | bytes 1920004
  67.8 10.8 %collective-permute-start.7 = (bf16[244,640]{1,0:T(8,128)(2,1)S(1)}, bf16[244,640]{1,0:T(8,128)(2,1)S(1)}, u32[]{:S(2)}, u32[]{:S(2)}) collective-permute-start(bf16[244,640]{1,0:T(8,128)(2,1)S(1)} %slice.46), channel_id=1, source_target_pairs={{0,448},{64,0},{128,64},{192,128},{256,192},{320,256},{384,320},{4... | collective-permute-start | bytes 936968 | tf_op jit(solution)/shard_map/ppermute | solution.py:191
  78.6 0.7 copy-start.6
  78.6 0.8 copy-start.5
  112.3 6.0 %collective-permute-start.8 = (f32[4,72,640]{2,1,0:T(8,128)}, f32[4,72,640]{2,1,0:T(8,128)S(1)}, u32[]{:S(2)}, u32[]{:S(2)}) collective-permute-start(f32[4,72,640]{2,1,0:T(8,128)} %get-tuple-element.11), channel_id=1, source_target_pairs={{0,4},{4,0},{1,5},{5,1},{2,6},{6,2},{3,7},{7,3},{8,12},{12,8},{9,1... | collective-permute-start | bytes 2211848 | tf_op jit(solution)/shard_map/ppermute | solution.py:178
  118.3 13.2 %copy-start.10 = (f32[192]{0:T(256)S(1)}, f32[192]{0:T(256)}, u32[]{:S(2)}) copy-start(f32[192]{0:T(256)} %copy-done.9) | copy-start | bytes 2308
  118.3 13.2 %copy-start.12 = (pred[192]{0:T(512)(128)(4,1)S(1)}, pred[192]{0:T(512)(128)(4,1)}, u32[]{:S(2)}) copy-start(pred[192]{0:T(512)(128)(4,1)} %copy-done.11) | copy-start | bytes 580
  120.3 15.7 %copy-start.14 = (f32[1,72]{1,0:T(1,128)S(1)}, f32[1,72]{1,0:T(1,128)}, u32[]{:S(2)}) copy-start(f32[1,72]{1,0:T(1,128)} %get-tuple-element.12) | copy-start | bytes 868
  120.3 30.1 %copy-start.13 = (f32[2,1]{1,0:T(2,128)S(1)}, f32[2,1]{1,0:T(2,128)}, u32[]{:S(2)}) copy-start(f32[2,1]{1,0:T(2,128)} %get-tuple-element.23) | copy-start | bytes 28
  120.3 11.1 %all-to-all-start.3 = ((bf16[4,72,640]{2,1,0:T(8,128)(2,1)}), bf16[4,72,640]{2,1,0:T(8,128)(2,1)S(1)}, u32[]{:S(2)}, u32[]{:S(2)}) async-start(bf16[4,72,640]{2,1,0:T(8,128)(2,1)} %add_convert_fusion), calls=%async_computation.3 | async-start | bytes 737280 | tf_op jit(solution)/shard_map/all_to_all | solution.py:247
  132.5 13.0 %all-to-all-start.4 = ((bf16[8,24,640]{2,1,0:T(8,128)(2,1)}), bf16[8,24,640]{2,1,0:T(8,128)(2,1)S(1)}, u32[]{:S(2)}, u32[]{:S(2)}) async-start(bf16[8,24,640]{2,1,0:T(8,128)(2,1)} %bitcast.23), calls=%async_computation.4 | async-start | bytes 491520 | tf_op jit(solution)/shard_map/all_to_all | solution.py:251
  145.7 5.5 %collective-permute-start.9 = (bf16[12,640]{1,0:T(8,128)(2,1)S(1)}, bf16[12,640]{1,0:T(8,128)(2,1)S(1)}, u32[]{:S(2)}, u32[]{:S(2)}) collective-permute-start(bf16[12,640]{1,0:T(8,128)(2,1)S(1)} %dynamic-slice_bitcast_fusion), channel_id=1, source_target_pairs={{0,4},{4,0},{1,5},{5,1},{2,6},{6,2},{3,7},{7,3},{8,12},{12,8},{9,1... | collective-permute-start | bytes 46088 | tf_op jit(solution)/shard_map/ppermute | solution.py:178

commit v3 on v2

v3 whole, which is shorter than its diff:
```python
import functools

import jax
import jax.numpy as jnp
from jax import lax
from jax.experimental import pallas as pl
from jax.experimental.pallas import tpu as pltpu
from jax.sharding import Mesh, PartitionSpec as P

EPS = 1e-05
LIVE = 72
SPAN = 500
PART = 256
NEAR = 7
WIDTH = 640
FACTS = 128
F32 = jnp.float32
BF16 = jnp.bfloat16


def params():
    return pltpu.CompilerParams(vmem_limit_bytes=32 * 1024 * 1024)


def pick_kernel(slots_ref, targets_ref, hidden_ref, out_ref, rows, total, sem):
    layers, most = slots_ref.shape
    part_width = hidden_ref.shape[2]
    copies = []
    for i in range(layers * most):
        row = jnp.minimum(slots_ref[i // most, i % most], hidden_ref.shape[1] - 1)
        block = pl.ds(pl.multiple_of((row // 16) * 16, 16), 16)
        copies.append(pltpu.make_async_copy(hidden_ref.at[i // most, block], rows.at[i], sem.at[i]))
        copies[-1].start()
    lane = lax.broadcasted_iota(jnp.int32, (1, FACTS), 1)
    sub = lax.broadcasted_iota(jnp.int32, (16, 1), 0)
    for i, copy in enumerate(copies):
        entry = slots_ref[i // most, i % most]
        row = jnp.minimum(entry, hidden_ref.shape[1] - 1)
        live = (entry < hidden_ref.shape[1]).astype(jnp.int32)
        label = targets_ref[row] * live
        fact = jnp.where(lane == 0, live, 0) + jnp.where(lane == 1, label // 256, 0)
        fact += jnp.where(lane == 2, label % 256, 0) + jnp.where(lane == 3, i // most, 0)
        total[i : i + 1, part_width:] = fact.astype(F32)
        copy.wait()
        mine = (sub == row % 16) & (live > 0)
        picked = jnp.sum(jnp.where(mine, rows[i].astype(F32), 0.0), axis=0, keepdims=True)
        total[i : i + 1, :part_width] = picked
    out_ref[...] = total[...].astype(BF16)


def pick(slots, targets, hidden):
    own, part_width = slots.size, hidden.shape[2]
    return pl.pallas_call(
        pick_kernel,
        in_specs=[SMEM, SMEM, pl.BlockSpec(memory_space=pltpu.HBM)],
        out_specs=VMEM,
        out_shape=jax.ShapeDtypeStruct((own, part_width + FACTS), BF16),
        scratch_shapes=[
            pltpu.VMEM((own, 16, part_width), BF16),
            pltpu.VMEM((own, part_width + FACTS), F32),
            pltpu.SemaphoreType.DMA((own,)),
        ],
        compiler_params=params(),
        name="pick",
    )(slots, targets, hidden)


def scores(shard, normed_ref, head):
    normed = normed_ref[lax.rem(shard, 2), shard // 2]
    return lax.dot_general(head, normed, (((1,), (1,)), ((), ())), preferred_element_type=F32)


def first_kernel(meta_ref, normed_ref, *rest):
    *refs, logits_ref = rest
    total = jnp.zeros((SPAN, LIVE), F32)
    for place, ref in enumerate(refs):
        total += scores(meta_ref[2 + place], normed_ref, ref[...])
    logits_ref[...] = total


def logits_kernel(meta_ref, normed_ref, label_ref, first_ref, *rest):
    *refs, logits_ref, stats_ref = rest
    parts = [scores(meta_ref[9], normed_ref, ref[...]) for ref in refs]
    logits = first_ref[...] + jnp.concatenate(parts, axis=0)
    logits_ref[...] = logits
    column = lax.broadcasted_iota(jnp.int32, (SPAN, LIVE), 0)
    hits = column + meta_ref[0] == label_ref[...]
    peak = jnp.max(logits, axis=0, keepdims=True)
    shifted = jnp.exp(logits - peak)
    stats_ref[0:1, :] = peak
    stats_ref[1:2, :] = jnp.sum(shifted, axis=0, keepdims=True)
    stats_ref[2:3, :] = jnp.sum(shifted * (logits - peak), axis=0, keepdims=True)
    stats_ref[3:4, :] = jnp.sum(jnp.where(hits, logits, 0.0), axis=0, keepdims=True)


VMEM = pl.BlockSpec(memory_space=pltpu.VMEM)
SMEM = pl.BlockSpec(memory_space=pltpu.SMEM)


def local_logits(meta, normed, label, near):
    first = pl.pallas_call(
        first_kernel,
        in_specs=[SMEM, VMEM, *[VMEM] * NEAR],
        out_specs=VMEM,
        out_shape=jax.ShapeDtypeStruct((SPAN, LIVE), F32),
        compiler_params=params(),
        cost_estimate=pl.CostEstimate(
            flops=2 * NEAR * SPAN * LIVE * WIDTH,
            bytes_accessed=2 * NEAR * SPAN * WIDTH,
            transcendentals=0,
        ),
        name="logits_early",
    )(meta, normed, *near[:NEAR])
    return pl.pallas_call(
        logits_kernel,
        in_specs=[SMEM, VMEM, VMEM, VMEM, *[VMEM] * (9 - NEAR)],
        out_specs=[VMEM, VMEM],
        out_shape=[
            jax.ShapeDtypeStruct((SPAN, LIVE), F32),
            jax.ShapeDtypeStruct((4, LIVE), F32),
        ],
        compiler_params=params(),
        name="logits",
    )(meta, normed, label, first, *near[NEAR:])


def back_kernel(meta_ref, stats_ref, logits_ref, label_ref, layer_ref, *rest):
    *refs, part_ref, row_ref, loss_ref = rest
    stats = stats_ref[...]
    peaks = [stats[:, 4 * c, :] for c in range(2)]
    peak = jnp.max(jnp.maximum(peaks[0], peaks[1]), axis=0, keepdims=True)
    mass = mean = aimed = jnp.zeros((1, LIVE), F32)
    for c in range(2):
        weight = jnp.exp(peaks[c] - peak)
        own = stats[:, 4 * c + 1, :]
        mass += jnp.sum(weight * own, axis=0, keepdims=True)
        moved = stats[:, 4 * c + 2, :] + (peaks[c] - peak) * own
        mean += jnp.sum(weight * moved, axis=0, keepdims=True)
        aimed += jnp.sum(stats[:, 4 * c + 3, :], axis=0, keepdims=True)
    row_ref[...] = mean / mass + (peak - aimed)
    loss = jnp.log(mass) + (peak - aimed)
    for layer in range(2):
        mine = (layer_ref[...] == layer).astype(F32)
        total = jnp.sum(loss * mine, axis=1, keepdims=True)
        loss_ref[layer : layer + 1, :] = total / jnp.sum(mine, axis=1, keepdims=True)
    logits = logits_ref[...]
    column = lax.broadcasted_iota(jnp.int32, (SPAN, LIVE), 0)
    hits = (column + meta_ref[0] == label_ref[...]).astype(F32)
    slope = (jnp.exp(logits - peak) / mass - hits).T.astype(BF16)
    for place in range(8):
        shard = meta_ref[2 + place]
        if place < 7:
            part = jnp.dot(slope, refs[place][...], preferred_element_type=F32)
        else:
            part = jnp.dot(slope[:, :PART], refs[7][...], preferred_element_type=F32)
            part += jnp.dot(slope[:, PART:], refs[8][...], preferred_element_type=F32)
        part_ref[shard] = part.astype(BF16)


def local_back(meta, stats, logits, label, layer, near):
    return pl.pallas_call(
        back_kernel,
        in_specs=[SMEM, VMEM, VMEM, VMEM, VMEM, *[VMEM] * 9],
        out_specs=[VMEM] * 3,
        out_shape=[
            jax.ShapeDtypeStruct((8, LIVE, WIDTH), BF16),
            jax.ShapeDtypeStruct((1, LIVE), F32),
            jax.ShapeDtypeStruct((2, 1), F32),
        ],
        compiler_params=params(),
        name="back",
    )(meta, stats, logits, label, layer, *near)


def spread(values, axes, count):
    copies = jnp.broadcast_to(values[None], (count, *values.shape))
    return lax.all_to_all(copies, axes, 0, 0, tiled=True)


def ring(own):
    up = [(i, (i + 1) % 8) for i in range(8)]
    down = [(i, (i - 1) % 8) for i in range(8)]
    right = left = own
    near = [own]
    for _ in range(3):
        right = lax.ppermute(right, "z", up)
        left = lax.ppermute(left, "z", down)
        near += [right, left]
    near.append(lax.ppermute(right[:PART], "z", up))
    near.append(lax.ppermute(left[PART:], "z", down))
    return near


def body(hidden, gain, head, exit_slots, targets):
    layers, row_dev, part_width = hidden.shape
    most = exit_slots.shape[1]
    own = layers * most
    width = gain.shape[0]
    half = part_width // 2
    z, y, c, x = (lax.axis_index(name) for name in ("z", "y", "c", "x"))
    shards = [lax.rem(z + s, 8) for s in (0, 7, 1, 6, 2, 5, 3, 4)]
    first = ((y * 2 + c) * 4 + x) * SPAN
    meta = jnp.stack([first, c, *shards]).astype(jnp.int32)
    near = ring(head.T)

    packed = pick(exit_slots, targets, hidden)
    picked = packed[:, :part_width]
    pair = lax.all_gather(packed, "c", axis=0, tiled=True)
    pair_half = lax.dynamic_slice_in_dim(pair, c * half, half, 1)
    slots = jnp.concatenate([pair_half, pair[:, part_width:]], axis=1)
    slots = spread(slots, "y", 8).reshape(16 * own, half + 128)

    total = slots.shape[0]
    flag = slots[:, half].astype(F32)
    below = (jnp.arange(total)[:, None] < jnp.arange(total)[None, :]).astype(F32)
    rank = jnp.sum(below * flag[:, None], axis=0)
    place = (rank[None, :] == jnp.arange(LIVE, dtype=F32)[:, None]) & (flag > 0)[None, :]
    place = place.astype(BF16)
    place_out = jnp.pad(place.reshape(LIVE, 16, own), ((0, 0), (0, 0), (0, 16 - own)))
    place_out = place_out.reshape(LIVE, 256)
    compact = jnp.dot(place, slots, preferred_element_type=F32)
    fact = compact[:, half : half + 4].astype(jnp.int32).T
    label_row = (fact[1] * 256 + fact[2]).reshape(1, LIVE)
    layer_row = fact[3].reshape(1, LIVE)
    rows = spread(compact[:, :half].astype(BF16), "x", 4)
    rows = lax.all_gather(rows, "c", axis=0)

    values = rows.astype(F32)
    scale = lax.rsqrt(jnp.sum(values * values, axis=(0, 1, 3)) / width + EPS)
    gain_f = gain.astype(F32)
    gain_rows = gain_f.reshape(4, 2, 1, half).transpose(1, 0, 2, 3)
    normed = (values * scale[:, None] * gain_rows).astype(BF16)

    logits, stats = local_logits(meta, normed, label_row, near)
    stats = lax.all_gather(stats, "c", axis=0, tiled=True)
    stats = spread(stats, ("y", "x"), 32)
    part, gap, group_loss = local_back(meta, stats, logits, label_row, layer_row, near)

    part = lax.all_to_all(part, ("x", "c"), 0, 0, tiled=True)
    part = jnp.sum(part.astype(F32), axis=0).astype(BF16)
    sent = lax.dot_general(place_out, part, (((0,), (0,)), ((), ())), preferred_element_type=F32)
    sent = sent.astype(BF16).reshape(16, 16, half)
    back = lax.all_to_all(sent, ("y", "c"), 0, 0, tiled=True)
    back = jnp.sum(back.reshape(8, 2, 16, half).astype(F32), axis=0)[:, :own]

    gain_own = lax.dynamic_slice_in_dim(gain_f, x * part_width, part_width)
    mine = lax.dynamic_slice_in_dim(place, (y * 2 + c) * own, own, 1).astype(F32)
    scale_own = jnp.sum(mine * scale[:, None], axis=0)
    shift_own = jnp.sum(mine * (scale**2 * gap[0] / width)[:, None], axis=0)
    value_own = picked.reshape(own, 2, half).transpose(1, 0, 2).astype(F32)
    grads = scale_own[:, None] * gain_own.reshape(2, 1, half) * back - value_own * shift_own[:, None]
    exit_grads = grads.astype(BF16).transpose(1, 0, 2).reshape(layers, most, part_width)
    return exit_grads, group_loss


def solution(mesh):
    split = Mesh(mesh.devices.reshape(8, 8, 2, 4), ("z", "y", "c", "x"))
    in_specs = (
        P(None, ("z", "y", "c"), "x"),
        P(),
        P("z", ("y", "c", "x")),
        P(None, ("z", "y", "c")),
        P(("z", "y", "c")),
    )
    out_specs = (P(None, ("z", "y", "c"), "x"), P(None, "z"))
    return jax.shard_map(body, mesh=split, in_specs=in_specs, out_specs=out_specs, check_vma=False)
```

time: 153 us -> 140 us (0.915)
  waiting for transfers between devices: 28.9 us -> 36.7 us
  Pallas kernels: 14.8 us -> 7.56 us
  other arithmetic: 7.6 us -> 1.5 us
  starting transfers between devices: 59.6 us -> 53.6 us
    ppermute x2 -> x0, starting transfers between devices: 8.63 us -> none  [swap_core(): return lax.ppermute(values, 'c', [(0, 1), (1, 0)])]
    pallas_call x3 -> x4, Pallas kernels: 14.8 us -> 7.56 us  [the longest x1 2.47 us: local_logits(): pl.pallas_call(first_kernel, in_specs=[SMEM, VMEM, *[VMEM] * NEAR], out_s...]
    all_to_all x2, waiting for transfers between devices: 16.8 us -> 23.4 us  [the longest x1 12 us: body(): back = lax.all_to_all(sent, ('y', 'c'), 0, 0, tiled=True)]
    all_to_all x2, starting transfers between devices: 6.99 us -> 9.8 us  [the longest x1 5.61 us: body(): part = lax.all_to_all(part, ('x', 'c'), 0, 0, tiled=True)]
    gather x5 -> x0, local copies, waits for them, and re-layouts: 2.28 us -> none  [the longest x2 1.42 us: body(): label = jnp.where(live, targets[local], 0)]
    ppermute x2 -> x0, waiting for transfers between devices: 2.24 us -> none  [swap_core(): return lax.ppermute(values, 'c', [(0, 1), (1, 0)])]
    convert_element_type x2 -> x1, other arithmetic: 2.08 us -> 0.01 us  [body(): value_own = picked.reshape(own, 2, half).transpose(1, 0, 2).astype(F32)]
    unnamed x35 -> x26, local copies, waits for them, and re-layouts: 2.99 us -> 4.87 us
  transfers between devices with their start and end apart: 14 -> 12, of which waited for: 7 -> 6; matrix products, arithmetic and copies ran while one was open for 8% -> 4% of each run, Pallas kernels for 3% -> 3%
where the time goes in v3:
time: 140 us; the launch traced here: 139 us
  starting transfers between devices  53.6 us (38%)
  waiting for transfers between devices  36.7 us (26%)
  blocking collectives  30.1 us (22%)
  local copies, waits for them, and re-layouts  7.59 us (5%)
  Pallas kernels  7.56 us (5%)
  other arithmetic  1.5 us (1%)
    all_to_all x1, blocking collectives, spread(): return lax.all_to_all(copies, axes, 0, 0, tiled=True)  18.1 us
    ppermute x3, starting transfers between devices, ring(): left = lax.ppermute(left, 'z', down)  17.7 us
    all_to_all x1, waiting for transfers between devices, body(): back = lax.all_to_all(sent, ('y', 'c'), 0, 0, tiled=True)  12 us
    all_to_all x1, waiting for transfers between devices, body(): part = lax.all_to_all(part, ('x', 'c'), 0, 0, tiled=True)  11.4 us
    all_to_all x2, starting transfers between devices, spread(): return lax.all_to_all(copies, axes, 0, 0, tiled=True)  10.9 us
    ppermute x3, starting transfers between devices, ring(): right = lax.ppermute(right, 'z', up)  8.66 us
    ppermute x3, waiting for transfers between devices, ring(): right = lax.ppermute(right, 'z', up)  6.96 us
    all_to_all x1, starting transfers between devices, body(): part = lax.all_to_all(part, ('x', 'c'), 0, 0, tiled=True)  5.61 us
  transfers between devices with their start and end apart: 12, of which 6 were waited for; matrix products, arithmetic and copies ran while one was open for 4% of the time, Pallas kernels for 3%

profile of v3, /device:TPU:1, one launch (start us, length us, event | category | flops | bytes accessed | tf_op | source)
XLA Modules:
  0.0 139.4 jit_solution(13326252034813183644)
XLA Ops:
  0.6 4.8 %collective-permute-start = (bf16[500,640]{1,0:T(8,128)(2,1)}, bf16[500,640]{1,0:T(8,128)(2,1)S(1)}, u32[]{:S(2)}, u32[]{:S(2)}) collective-permute-start(bf16[500,640]{1,0:T(8,128)(2,1)} %bitcast.39), channel_id=1, source_target_pairs={{0,64},{64,128},{128,192},{192,256},{256,320},{320,384},{384,448},... | collective-permute-start | bytes 1920008 | tf_op jit(solution)/shard_map/ppermute | solution.py:186
  5.5 8.6 %collective-permute-start.1 = (bf16[500,640]{1,0:T(8,128)(2,1)}, bf16[500,640]{1,0:T(8,128)(2,1)S(1)}, u32[]{:S(2)}, u32[]{:S(2)}) collective-permute-start(bf16[500,640]{1,0:T(8,128)(2,1)} %bitcast.40), channel_id=1, source_target_pairs={{0,448},{64,0},{128,64},{192,128},{256,192},{320,256},{384,320},{4... | collective-permute-start | bytes 1920008 | tf_op jit(solution)/shard_map/ppermute | solution.py:187
  14.1 1.3 copy-done.1
  15.4 0.7 copy-done.3
  16.1 0.7 copy-done.4
  16.8 1.8 %pick.1 = bf16[12,1408]{1,0:T(8,128)(2,1)S(1)} custom-call(s32[2,6]{1,0:T(2,128)S(1)} %copy-done.3, s32[256]{0:T(256)S(1)} %copy-done.4, bf16[2,256,1280]{2,1,0:T(8,128)(2,1)S(1)} %copy-done.1), custom_call_target="tpu_custom_call" | custom-call | tf_op jit(solution)/shard_map/pick/pallas_call | solution.py:53
  18.6 2.5 %all-gather.1 = bf16[2,12,1408]{2,1,0:T(8,128)(2,1)S(1)} all-gather(bf16[1,12,1408]{2,1,0:T(8,128)(2,1)S(1)} %bitcast.43), channel_id=1, replica_groups=mesh['z'=8,'y'=8,'c'=2,'x'=4] {'c'}, dimensions={0}, use_global_device_ids=true | all-gather | bytes 101376 | tf_op jit(solution)/shard_map/all_gather | solution.py:208
  21.1 0.7 broadcast_in_dim.6
  21.9 6.8 %all-to-all-start = ((bf16[8,24,768]{2,1,0:T(8,128)(2,1)}), bf16[8,24,768]{2,1,0:T(8,128)(2,1)S(1)}, u32[]{:S(2)}, u32[]{:S(2)}) async-start(bf16[8,24,768]{2,1,0:T(8,128)(2,1)} %broadcast_in_dim.6), calls=%async_computation | async-start | bytes 589824 | tf_op jit(solution)/shard_map/all_to_all | solution.py:177
  28.7 1.9 %collective-permute-start.2 = (bf16[500,640]{1,0:T(8,128)(2,1)S(1)}, bf16[500,640]{1,0:T(8,128)(2,1)S(1)}, u32[]{:S(2)}, u32[]{:S(2)}) collective-permute-start(bf16[500,640]{1,0:T(8,128)(2,1)S(1)} %collective-permute-done.rest_1_), channel_id=1, source_target_pairs={{0,64},{64,128},{128,192},{192,256},{256,320},{320,384},{384,448},... | collective-permute-start | bytes 1920008 | tf_op jit(solution)/shard_map/ppermute | solution.py:186
  30.6 4.6 %collective-permute-start.3 = (bf16[500,640]{1,0:T(8,128)(2,1)S(1)}, bf16[500,640]{1,0:T(8,128)(2,1)}, u32[]{:S(2)}, u32[]{:S(2)}) collective-permute-start(bf16[500,640]{1,0:T(8,128)(2,1)S(1)} %collective-permute-done.1.rest_2_), channel_id=1, source_target_pairs={{0,448},{64,0},{128,64},{192,128},{256,192},{320,256},{384,320},{4... | collective-permute-start | bytes 1920008 | tf_op jit(solution)/shard_map/ppermute | solution.py:187
  36.0 5.2 %all-to-all-done = bf16[8,24,768]{2,1,0:T(8,128)(2,1)S(1)} async-done(((bf16[8,24,768]{2,1,0:T(8,128)(2,1)}), bf16[8,24,768]{2,1,0:T(8,128)(2,1)S(1)}, u32[]{:S(2)}, u32[]{:S(2)}) %all-to-all-start) | async-done | bytes 294944 | tf_op jit(solution)/shard_map/all_to_all | solution.py:177
  41.8 0.8 broadcast_in_dim.7
  42.6 4.1 %all-to-all-start.1 = ((bf16[4,72,640]{2,1,0:T(8,128)(2,1)}), bf16[4,72,640]{2,1,0:T(8,128)(2,1)}, u32[]{:S(2)}, u32[]{:S(2)}) async-start(bf16[4,72,640]{2,1,0:T(8,128)(2,1)} %broadcast_in_dim.7), calls=%async_computation.1 | async-start | bytes 737280 | tf_op jit(solution)/shard_map/all_to_all | solution.py:177
  47.2 1.9 %collective-permute-start.4 = (bf16[500,640]{1,0:T(8,128)(2,1)S(1)}, bf16[500,640]{1,0:T(8,128)(2,1)S(1)}, u32[]{:S(2)}, u32[]{:S(2)}) collective-permute-start(bf16[500,640]{1,0:T(8,128)(2,1)S(1)} %collective-permute-done.2.rest_3_), channel_id=1, source_target_pairs={{0,64},{64,128},{128,192},{192,256},{256,320},{320,384},{384,448},... | collective-permute-start | bytes 1920008 | tf_op jit(solution)/shard_map/ppermute | solution.py:186
  49.2 4.6 %collective-permute-start.5 = (bf16[500,640]{1,0:T(8,128)(2,1)}, bf16[500,640]{1,0:T(8,128)(2,1)S(1)}, u32[]{:S(2)}, u32[]{:S(2)}) collective-permute-start(bf16[500,640]{1,0:T(8,128)(2,1)} %collective-permute-done.3.rest_4_), channel_id=1, source_target_pairs={{0,448},{64,0},{128,64},{192,128},{256,192},{320,256},{384,320},{4... | collective-permute-start | bytes 1920008 | tf_op jit(solution)/shard_map/ppermute | solution.py:187
  53.9 4.2 %all-gather = bf16[8,72,640]{2,1,0:T(8,128)(2,1)S(1)} all-gather(bf16[4,72,640]{2,1,0:T(8,128)(2,1)} %all-to-all-done.1), channel_id=2, replica_groups=mesh['z'=8,'y'=8,'c'=2,'x'=4] {'c'}, dimensions={0}, use_global_device_ids=true | all-gather | bytes 1105920 | tf_op jit(solution)/shard_map/all_gather | solution.py:226
  58.3 6.5 %collective-permute-done.4.rest_5_ = bf16[500,640]{1,0:T(8,128)(2,1)S(1)} collective-permute-done((bf16[500,640]{1,0:T(8,128)(2,1)S(1)}, bf16[500,640]{1,0:T(8,128)(2,1)S(1)}, u32[]{:S(2)}, u32[]{:S(2)}) %collective-permute-start.4) | collective-permute-done | bytes 640032 | tf_op jit(solution)/shard_map/ppermute | solution.py:186
  64.9 1.9 %collective-permute-start.6 = (bf16[256,640]{1,0:T(8,128)(2,1)S(1)}, bf16[256,640]{1,0:T(8,128)(2,1)S(1)}, u32[]{:S(2)}, u32[]{:S(2)}) collective-permute-start(bf16[256,640]{1,0:T(8,128)(2,1)S(1)} %slice.49), channel_id=1, source_target_pairs={{0,64},{64,128},{128,192},{192,256},{256,320},{320,384},{384,448},... | collective-permute-start | bytes 983048 | tf_op jit(solution)/shard_map/ppermute | solution.py:189
  66.8 4.6 %collective-permute-start.7 = (bf16[244,640]{1,0:T(8,128)(2,1)S(1)}, bf16[244,640]{1,0:T(8,128)(2,1)S(1)}, u32[]{:S(2)}, u32[]{:S(2)}) collective-permute-start(bf16[244,640]{1,0:T(8,128)(2,1)S(1)} %slice.50), channel_id=1, source_target_pairs={{0,448},{64,0},{128,64},{192,128},{256,192},{320,256},{384,320},{4... | collective-permute-start | bytes 936968 | tf_op jit(solution)/shard_map/ppermute | solution.py:190
  71.7 2.5 %logits_early.1.first_ref = f32[500,72]{1,0:T(8,128)S(1)} custom-call(s32[10]{0:T(128)S(1)} %stack.43.meta_ref, bf16[2,4,72,640]{3,2,1,0:T(8,128)(2,1)S(1)} %fusion.2.normed_ref, bf16[500,640]{1,0:T(8,128)(2,1)S(1)} %bitcast.41, bf16[500,640]{1,0:T(8,128)(2,1)S(1)} %collective-permute-done.rest_1_, bf16[500,640]{1,0:T(8,128)(2,1)S(1)} %collective-permute-done.1.rest_2_, ...), custom_call_target="tpu_custom_call" | custom-call | flops 322560000 | bytes 4480000 | tf_op jit(solution)/shard_map/logits_early/pallas_call | solution.py:101
  74.2 1.1 collective-permute-done.7.rest_1_.rest_8_
  75.3 1.0 logits.1
  76.3 5.3 %all-gather.2 = f32[2,4,72]{2,1,0:T(4,128)S(1)} all-gather(f32[1,4,72]{2,1,0:T(4,128)S(1)} %bitcast.44), channel_id=1, replica_groups=mesh['z'=8,'y'=8,'c'=2,'x'=4] {'c'}, dimensions={0}, use_global_device_ids=true | all-gather | bytes 3456 | tf_op jit(solution)/shard_map/all_gather | solution.py:235
  81.6 18.1 %all_to_all.25.stats_ref = f32[32,8,72]{2,1,0:T(8,128)S(1)} all-to-all(f32[32,8,72]{2,1,0:T(8,128)S(1)} %broadcast_in_dim.8), channel_id=1, replica_groups=mesh['z'=8,'y'=8,'c'=2,'x'=4] {'y','x'}, dimensions={0} | all-to-all | bytes 147456 | tf_op jit(solution)/shard_map/all_to_all | solution.py:177
  99.7 2.3 %back.1 = (bf16[8,72,640]{2,1,0:T(8,128)(2,1)S(1)}, f32[1,72]{1,0:T(1,128)S(1)}, f32[2,1]{1,0:T(2,128)S(1)}) custom-call(s32[10]{0:T(128)S(1)} %stack.43.meta_ref, f32[32,8,72]{2,1,0:T(8,128)S(1)} %all_to_all.25.stats_ref, f32[500,72]{1,0:T(8,128)S(1)} %get-tuple-element.8.logits_ref, s32[1,72]{1,0:T(1,128)S(1)} %get-tuple-element.25.label_ref, ...), custom_call_target="tpu_custom_call" | custom-call | tf_op jit(solution)/shard_map/back/pallas_call | solution.py:161
  102.0 0.9 copy-done.2
  102.9 5.6 %all-to-all-start.3 = ((bf16[8,72,640]{2,1,0:T(8,128)(2,1)}), bf16[8,72,640]{2,1,0:T(8,128)(2,1)S(1)}, u32[]{:S(2)}, u32[]{:S(2)}) async-start(bf16[8,72,640]{2,1,0:T(8,128)(2,1)} %copy-done.2), calls=%async_computation.3 | async-start | bytes 1474560 | tf_op jit(solution)/shard_map/all_to_all | solution.py:239
  108.8 11.4 %all-to-all-done.3 = bf16[8,72,640]{2,1,0:T(8,128)(2,1)S(1)} async-done(((bf16[8,72,640]{2,1,0:T(8,128)(2,1)}), bf16[8,72,640]{2,1,0:T(8,128)(2,1)S(1)}, u32[]{:S(2)}, u32[]{:S(2)}) %all-to-all-start.3) | async-done | bytes 737312 | tf_op jit(solution)/shard_map/all_to_all | solution.py:239
  120.4 1.0 convolution_convert_fusion
  121.3 4.2 %all-to-all-start.4 = ((bf16[16,16,640]{2,1,0:T(8,128)(2,1)}), bf16[16,16,640]{2,1,0:T(8,128)(2,1)S(1)}, u32[]{:S(2)}, u32[]{:S(2)}) async-start(bf16[16,16,640]{2,1,0:T(8,128)(2,1)} %bitcast.21), calls=%async_computation.4 | async-start | bytes 655360 | tf_op jit(solution)/shard_map/all_to_all | solution.py:243
  126.5 12.0 %all-to-all-done.4 = bf16[16,16,640]{2,1,0:T(8,128)(2,1)S(1)} async-done(((bf16[16,16,640]{2,1,0:T(8,128)(2,1)}), bf16[16,16,640]{2,1,0:T(8,128)(2,1)S(1)}, u32[]{:S(2)}, u32[]{:S(2)}) %all-to-all-start.4) | async-done | bytes 327712 | tf_op jit(solution)/shard_map/all_to_all | solution.py:243
  (64 shorter events, 4.9 us)
Async XLA Ops:
  0.6 28.1 %collective-permute-start = (bf16[500,640]{1,0:T(8,128)(2,1)}, bf16[500,640]{1,0:T(8,128)(2,1)S(1)}, u32[]{:S(2)}, u32[]{:S(2)}) collective-permute-start(bf16[500,640]{1,0:T(8,128)(2,1)} %bitcast.39), channel_id=1, source_target_pairs={{0,64},{64,128},{128,192},{192,256},{256,320},{320,384},{384,448},... | collective-permute-start | bytes 1920008 | tf_op jit(solution)/shard_map/ppermute | solution.py:186
  5.5 25.1 %collective-permute-start.1 = (bf16[500,640]{1,0:T(8,128)(2,1)}, bf16[500,640]{1,0:T(8,128)(2,1)S(1)}, u32[]{:S(2)}, u32[]{:S(2)}) collective-permute-start(bf16[500,640]{1,0:T(8,128)(2,1)} %bitcast.40), channel_id=1, source_target_pairs={{0,448},{64,0},{128,64},{192,128},{256,192},{320,256},{384,320},{4... | collective-permute-start | bytes 1920008 | tf_op jit(solution)/shard_map/ppermute | solution.py:187
  14.1 1.3 copy-start.1
  15.4 0.7 copy-start.3
  16.1 0.7 copy-start.4
  16.8 18.5 %copy-start.6 = (bf16[5120]{0:T(1024)(128)(2,1)S(1)}, bf16[5120]{0:T(1024)(128)(2,1)}, u32[]{:S(2)}) copy-start(bf16[5120]{0:T(1024)(128)(2,1)} %param.6) | copy-start | bytes 30724
  21.9 19.3 %all-to-all-start = ((bf16[8,24,768]{2,1,0:T(8,128)(2,1)}), bf16[8,24,768]{2,1,0:T(8,128)(2,1)S(1)}, u32[]{:S(2)}, u32[]{:S(2)}) async-start(bf16[8,24,768]{2,1,0:T(8,128)(2,1)} %broadcast_in_dim.6), calls=%async_computation | async-start | bytes 589824 | tf_op jit(solution)/shard_map/all_to_all | solution.py:177
  28.7 18.5 %collective-permute-start.2 = (bf16[500,640]{1,0:T(8,128)(2,1)S(1)}, bf16[500,640]{1,0:T(8,128)(2,1)S(1)}, u32[]{:S(2)}, u32[]{:S(2)}) collective-permute-start(bf16[500,640]{1,0:T(8,128)(2,1)S(1)} %collective-permute-done.rest_1_), channel_id=1, source_target_pairs={{0,64},{64,128},{128,192},{192,256},{256,320},{320,384},{384,448},... | collective-permute-start | bytes 1920008 | tf_op jit(solution)/shard_map/ppermute | solution.py:186
  30.6 18.5 %collective-permute-start.3 = (bf16[500,640]{1,0:T(8,128)(2,1)S(1)}, bf16[500,640]{1,0:T(8,128)(2,1)}, u32[]{:S(2)}, u32[]{:S(2)}) collective-permute-start(bf16[500,640]{1,0:T(8,128)(2,1)S(1)} %collective-permute-done.1.rest_2_), channel_id=1, source_target_pairs={{0,448},{64,0},{128,64},{192,128},{256,192},{320,256},{384,320},{4... | collective-permute-start | bytes 1920008 | tf_op jit(solution)/shard_map/ppermute | solution.py:187
  41.4 7.8 %copy-start.9 = (pred[192]{0:T(512)(128)(4,1)}, pred[192]{0:T(512)(128)(4,1)S(1)}, u32[]{:S(2)}) copy-start(pred[192]{0:T(512)(128)(4,1)S(1)} %fusion.5) | copy-start | bytes 580
  41.5 7.7 %copy-start.7 = (f32[192]{0:T(256)}, f32[192]{0:T(256)S(1)}, u32[]{:S(2)}) copy-start(f32[192]{0:T(256)S(1)} %select_reduce_fusion) | copy-start | bytes 2308
  42.6 11.2 %all-to-all-start.1 = ((bf16[4,72,640]{2,1,0:T(8,128)(2,1)}), bf16[4,72,640]{2,1,0:T(8,128)(2,1)}, u32[]{:S(2)}, u32[]{:S(2)}) async-start(bf16[4,72,640]{2,1,0:T(8,128)(2,1)} %broadcast_in_dim.7), calls=%async_computation.1 | async-start | bytes 737280 | tf_op jit(solution)/shard_map/all_to_all | solution.py:177
  47.2 17.6 %collective-permute-start.4 = (bf16[500,640]{1,0:T(8,128)(2,1)S(1)}, bf16[500,640]{1,0:T(8,128)(2,1)S(1)}, u32[]{:S(2)}, u32[]{:S(2)}) collective-permute-start(bf16[500,640]{1,0:T(8,128)(2,1)S(1)} %collective-permute-done.2.rest_3_), channel_id=1, source_target_pairs={{0,64},{64,128},{128,192},{192,256},{256,320},{320,384},{384,448},... | collective-permute-start | bytes 1920008 | tf_op jit(solution)/shard_map/ppermute | solution.py:186
  49.2 17.6 %collective-permute-start.5 = (bf16[500,640]{1,0:T(8,128)(2,1)}, bf16[500,640]{1,0:T(8,128)(2,1)S(1)}, u32[]{:S(2)}, u32[]{:S(2)}) collective-permute-start(bf16[500,640]{1,0:T(8,128)(2,1)} %collective-permute-done.3.rest_4_), channel_id=1, source_target_pairs={{0,448},{64,0},{128,64},{192,128},{256,192},{320,256},{384,320},{4... | collective-permute-start | bytes 1920008 | tf_op jit(solution)/shard_map/ppermute | solution.py:187
  53.8 17.6 %copy-start.5 = (f32[2,4,640]{2,1,0:T(4,128)S(1)}, f32[2,4,640]{2,1,0:T(4,128)}, u32[]{:S(2)}) copy-start(f32[2,4,640]{2,1,0:T(4,128)} %copy.24) | copy-start | bytes 61444
  58.3 13.3 %copy-start = (bf16[640,500]{0,1:T(8,128)(2,1)S(1)}, bf16[640,500]{0,1:T(8,128)(2,1)}, u32[]{:S(2)}) copy-start(bf16[640,500]{0,1:T(8,128)(2,1)} %param.7) | copy-start | bytes 1920004
  64.9 10.4 %collective-permute-start.6 = (bf16[256,640]{1,0:T(8,128)(2,1)S(1)}, bf16[256,640]{1,0:T(8,128)(2,1)S(1)}, u32[]{:S(2)}, u32[]{:S(2)}) collective-permute-start(bf16[256,640]{1,0:T(8,128)(2,1)S(1)} %slice.49), channel_id=1, source_target_pairs={{0,64},{64,128},{128,192},{192,256},{256,320},{320,384},{384,448},... | collective-permute-start | bytes 983048 | tf_op jit(solution)/shard_map/ppermute | solution.py:189
  66.8 8.5 %collective-permute-start.7 = (bf16[244,640]{1,0:T(8,128)(2,1)S(1)}, bf16[244,640]{1,0:T(8,128)(2,1)S(1)}, u32[]{:S(2)}, u32[]{:S(2)}) collective-permute-start(bf16[244,640]{1,0:T(8,128)(2,1)S(1)} %slice.50), channel_id=1, source_target_pairs={{0,448},{64,0},{128,64},{192,128},{256,192},{320,256},{384,320},{4... | collective-permute-start | bytes 936968 | tf_op jit(solution)/shard_map/ppermute | solution.py:190
  102.0 0.9 copy-start.2
  102.8 5.6 %copy-start.8 = (f32[192]{0:T(256)S(1)}, f32[192]{0:T(256)}, u32[]{:S(2)}) copy-start(f32[192]{0:T(256)} %copy-done.7) | copy-start | bytes 2308
  102.8 5.7 %copy-start.10 = (pred[192]{0:T(512)(128)(4,1)S(1)}, pred[192]{0:T(512)(128)(4,1)}, u32[]{:S(2)}) copy-start(pred[192]{0:T(512)(128)(4,1)} %copy-done.9) | copy-start | bytes 580
  102.9 17.4 %all-to-all-start.3 = ((bf16[8,72,640]{2,1,0:T(8,128)(2,1)}), bf16[8,72,640]{2,1,0:T(8,128)(2,1)S(1)}, u32[]{:S(2)}, u32[]{:S(2)}) async-start(bf16[8,72,640]{2,1,0:T(8,128)(2,1)} %copy-done.2), calls=%async_computation.3 | async-start | bytes 1474560 | tf_op jit(solution)/shard_map/all_to_all | solution.py:239
  121.3 17.2 %all-to-all-start.4 = ((bf16[16,16,640]{2,1,0:T(8,128)(2,1)}), bf16[16,16,640]{2,1,0:T(8,128)(2,1)S(1)}, u32[]{:S(2)}, u32[]{:S(2)}) async-start(bf16[16,16,640]{2,1,0:T(8,128)(2,1)} %bitcast.21), calls=%async_computation.4 | async-start | bytes 655360 | tf_op jit(solution)/shard_map/all_to_all | solution.py:243

commit v4 on v3

--- a/solution.py
+++ b/solution.py
@@ -10,7 +10,7 @@
 EPS = 1e-05
 LIVE = 72
 SPAN = 500
-PART = 256
+PART = 264
 NEAR = 7
 WIDTH = 640
 FACTS = 128
@@ -18,8 +18,8 @@
 BF16 = jnp.bfloat16
 
 
-def params():
-    return pltpu.CompilerParams(vmem_limit_bytes=32 * 1024 * 1024)
+def params(mib=32):
+    return pltpu.CompilerParams(vmem_limit_bytes=mib * 1024 * 1024)
 
 
 def pick_kernel(slots_ref, targets_ref, hidden_ref, out_ref, rows, total, sem):
@@ -60,7 +60,7 @@
             pltpu.VMEM((own, part_width + FACTS), F32),
             pltpu.SemaphoreType.DMA((own,)),
         ],
-        compiler_params=params(),
+        compiler_params=params(56),
         name="pick",
     )(slots, targets, hidden)
 

time: 140 us -> 139 us (level)
  local copies, waits for them, and re-layouts: 7.59 us -> 4.3 us
    unnamed x26 -> x12, local copies, waits for them, and re-layouts: 4.87 us -> 2.2 us
  transfers between devices with their start and end apart: 12 -> 12, of which waited for: 6 -> 6; matrix products, arithmetic and copies ran while one was open for 4% -> 3% of each run, Pallas kernels for 3% -> 4%
where the time goes in v4:
time: 139 us; the launch traced here: 138 us
  starting transfers between devices  53.3 us (38%)
  waiting for transfers between devices  37.3 us (27%)
  blocking collectives  30.3 us (22%)
  Pallas kernels  8.78 us (6%)
  local copies, waits for them, and re-layouts  4.3 us (3%)
  other arithmetic  1.5 us (1%)
    all_to_all x1, blocking collectives, spread(): return lax.all_to_all(copies, axes, 0, 0, tiled=True)  18.2 us
    ppermute x3, starting transfers between devices, ring(): left = lax.ppermute(left, 'z', down)  17.7 us
    all_to_all x1, waiting for transfers between devices, body(): back = lax.all_to_all(sent, ('y', 'c'), 0, 0, tiled=True)  12 us
    all_to_all x1, waiting for transfers between devices, body(): part = lax.all_to_all(part, ('x', 'c'), 0, 0, tiled=True)  11.4 us
    all_to_all x2, starting transfers between devices, spread(): return lax.all_to_all(copies, axes, 0, 0, tiled=True)  10.7 us
    ppermute x3, starting transfers between devices, ring(): right = lax.ppermute(right, 'z', up)  8.66 us
    ppermute x3, waiting for transfers between devices, ring(): right = lax.ppermute(right, 'z', up)  7.03 us
    all_to_all x2, waiting for transfers between devices, spread(): return lax.all_to_all(copies, axes, 0, 0, tiled=True)  5.77 us
  transfers between devices with their start and end apart: 12, of which 6 were waited for; matrix products, arithmetic and copies ran while one was open for 3% of the time, Pallas kernels for 4%

profile of v4, /device:TPU:1, one launch (start us, length us, event | category | flops | bytes accessed | tf_op | source)
XLA Modules:
  0.0 137.7 jit_solution(17536812830159167389)
XLA Ops:
  0.6 4.8 %collective-permute-start = (bf16[500,640]{1,0:T(8,128)(2,1)}, bf16[500,640]{1,0:T(8,128)(2,1)S(1)}, u32[]{:S(2)}, u32[]{:S(2)}) collective-permute-start(bf16[500,640]{1,0:T(8,128)(2,1)} %bitcast.39), channel_id=1, source_target_pairs={{0,64},{64,128},{128,192},{192,256},{256,320},{320,384},{384,448},... | collective-permute-start | bytes 1920008 | tf_op jit(solution)/shard_map/ppermute | solution.py:186
  5.5 8.6 %collective-permute-start.1 = (bf16[500,640]{1,0:T(8,128)(2,1)}, bf16[500,640]{1,0:T(8,128)(2,1)S(1)}, u32[]{:S(2)}, u32[]{:S(2)}) collective-permute-start(bf16[500,640]{1,0:T(8,128)(2,1)} %bitcast.40), channel_id=1, source_target_pairs={{0,448},{64,0},{128,64},{192,128},{256,192},{320,256},{384,320},{4... | collective-permute-start | bytes 1920008 | tf_op jit(solution)/shard_map/ppermute | solution.py:187
  14.1 3.0 %pick.1 = bf16[12,1408]{1,0:T(8,128)(2,1)} custom-call(s32[2,6]{1,0:T(2,128)} %slots_ref.1, s32[256]{0:T(256)} %targets_ref.1, bf16[2,256,1280]{2,1,0:T(8,128)(2,1)} %hidden_ref.1), custom_call_target="tpu_custom_call" | custom-call | tf_op jit(solution)/shard_map/pick/pallas_call | solution.py:53
  17.1 2.7 %all-gather.1 = bf16[2,12,1408]{2,1,0:T(8,128)(2,1)S(1)} all-gather(bf16[1,12,1408]{2,1,0:T(8,128)(2,1)} %bitcast.49), channel_id=1, replica_groups=mesh['z'=8,'y'=8,'c'=2,'x'=4] {'c'}, dimensions={0}, use_global_device_ids=true | all-gather | bytes 101376 | tf_op jit(solution)/shard_map/all_gather | solution.py:208
  19.8 0.7 broadcast_in_dim.6
  20.6 6.6 %all-to-all-start = ((bf16[8,24,768]{2,1,0:T(8,128)(2,1)}), bf16[8,24,768]{2,1,0:T(8,128)(2,1)S(1)}, u32[]{:S(2)}, u32[]{:S(2)}) async-start(bf16[8,24,768]{2,1,0:T(8,128)(2,1)} %broadcast_in_dim.6), calls=%async_computation | async-start | bytes 589824 | tf_op jit(solution)/shard_map/all_to_all | solution.py:177
  27.2 1.9 %collective-permute-start.2 = (bf16[500,640]{1,0:T(8,128)(2,1)S(1)}, bf16[500,640]{1,0:T(8,128)(2,1)S(1)}, u32[]{:S(2)}, u32[]{:S(2)}) collective-permute-start(bf16[500,640]{1,0:T(8,128)(2,1)S(1)} %collective-permute-done.rest_1_), channel_id=1, source_target_pairs={{0,64},{64,128},{128,192},{192,256},{256,320},{320,384},{384,448},... | collective-permute-start | bytes 1920008 | tf_op jit(solution)/shard_map/ppermute | solution.py:186
  29.1 4.6 %collective-permute-start.3 = (bf16[500,640]{1,0:T(8,128)(2,1)S(1)}, bf16[500,640]{1,0:T(8,128)(2,1)}, u32[]{:S(2)}, u32[]{:S(2)}) collective-permute-start(bf16[500,640]{1,0:T(8,128)(2,1)S(1)} %collective-permute-done.1.rest_2_), channel_id=1, source_target_pairs={{0,448},{64,0},{128,64},{192,128},{256,192},{320,256},{384,320},{4... | collective-permute-start | bytes 1920008 | tf_op jit(solution)/shard_map/ppermute | solution.py:187
  33.9 5.8 %all-to-all-done = bf16[8,24,768]{2,1,0:T(8,128)(2,1)S(1)} async-done(((bf16[8,24,768]{2,1,0:T(8,128)(2,1)}), bf16[8,24,768]{2,1,0:T(8,128)(2,1)S(1)}, u32[]{:S(2)}, u32[]{:S(2)}) %all-to-all-start) | async-done | bytes 294944 | tf_op jit(solution)/shard_map/all_to_all | solution.py:177
  40.3 0.8 broadcast_in_dim.7
  41.1 4.1 %all-to-all-start.1 = ((bf16[4,72,640]{2,1,0:T(8,128)(2,1)}), bf16[4,72,640]{2,1,0:T(8,128)(2,1)}, u32[]{:S(2)}, u32[]{:S(2)}) async-start(bf16[4,72,640]{2,1,0:T(8,128)(2,1)} %broadcast_in_dim.7), calls=%async_computation.1 | async-start | bytes 737280 | tf_op jit(solution)/shard_map/all_to_all | solution.py:177
  45.2 0.5 collective-permute-done.2.rest_3_
  45.7 1.9 %collective-permute-start.4 = (bf16[500,640]{1,0:T(8,128)(2,1)S(1)}, bf16[500,640]{1,0:T(8,128)(2,1)S(1)}, u32[]{:S(2)}, u32[]{:S(2)}) collective-permute-start(bf16[500,640]{1,0:T(8,128)(2,1)S(1)} %collective-permute-done.2.rest_3_), channel_id=1, source_target_pairs={{0,64},{64,128},{128,192},{192,256},{256,320},{320,384},{384,448},... | collective-permute-start | bytes 1920008 | tf_op jit(solution)/shard_map/ppermute | solution.py:186
  47.6 4.6 %collective-permute-start.5 = (bf16[500,640]{1,0:T(8,128)(2,1)}, bf16[500,640]{1,0:T(8,128)(2,1)S(1)}, u32[]{:S(2)}, u32[]{:S(2)}) collective-permute-start(bf16[500,640]{1,0:T(8,128)(2,1)} %collective-permute-done.3.rest_4_), channel_id=1, source_target_pairs={{0,448},{64,0},{128,64},{192,128},{256,192},{320,256},{384,320},{4... | collective-permute-start | bytes 1920008 | tf_op jit(solution)/shard_map/ppermute | solution.py:187
  52.3 4.2 %all-gather = bf16[8,72,640]{2,1,0:T(8,128)(2,1)S(1)} all-gather(bf16[4,72,640]{2,1,0:T(8,128)(2,1)} %all-to-all-done.1), channel_id=2, replica_groups=mesh['z'=8,'y'=8,'c'=2,'x'=4] {'c'}, dimensions={0}, use_global_device_ids=true | all-gather | bytes 1105920 | tf_op jit(solution)/shard_map/all_gather | solution.py:226
  56.8 6.5 %collective-permute-done.4.rest_5_ = bf16[500,640]{1,0:T(8,128)(2,1)S(1)} collective-permute-done((bf16[500,640]{1,0:T(8,128)(2,1)S(1)}, bf16[500,640]{1,0:T(8,128)(2,1)S(1)}, u32[]{:S(2)}, u32[]{:S(2)}) %collective-permute-start.4) | collective-permute-done | bytes 640032 | tf_op jit(solution)/shard_map/ppermute | solution.py:186
  63.3 1.9 %collective-permute-start.6 = (bf16[264,640]{1,0:T(8,128)(2,1)S(1)}, bf16[264,640]{1,0:T(8,128)(2,1)S(1)}, u32[]{:S(2)}, u32[]{:S(2)}) collective-permute-start(bf16[264,640]{1,0:T(8,128)(2,1)S(1)} %slice.49), channel_id=1, source_target_pairs={{0,64},{64,128},{128,192},{192,256},{256,320},{320,384},{384,448},... | collective-permute-start | bytes 1013768 | tf_op jit(solution)/shard_map/ppermute | solution.py:189
  65.3 4.6 %collective-permute-start.7 = (bf16[236,640]{1,0:T(8,128)(2,1)S(1)}, bf16[236,640]{1,0:T(8,128)(2,1)S(1)}, u32[]{:S(2)}, u32[]{:S(2)}) collective-permute-start(bf16[236,640]{1,0:T(8,128)(2,1)S(1)} %slice.50), channel_id=1, source_target_pairs={{0,448},{64,0},{128,64},{192,128},{256,192},{320,256},{384,320},{4... | collective-permute-start | bytes 906248 | tf_op jit(solution)/shard_map/ppermute | solution.py:190
  70.2 2.5 %logits_early.1.first_ref = f32[500,72]{1,0:T(8,128)S(1)} custom-call(s32[10]{0:T(128)S(1)} %stack.43.meta_ref, bf16[2,4,72,640]{3,2,1,0:T(8,128)(2,1)S(1)} %fusion.2.normed_ref, bf16[500,640]{1,0:T(8,128)(2,1)S(1)} %bitcast.41, bf16[500,640]{1,0:T(8,128)(2,1)S(1)} %collective-permute-done.rest_1_, bf16[500,640]{1,0:T(8,128)(2,1)S(1)} %collective-permute-done.1.rest_2_, ...), custom_call_target="tpu_custom_call" | custom-call | flops 322560000 | bytes 4480000 | tf_op jit(solution)/shard_map/logits_early/pallas_call | solution.py:101
  72.6 1.0 collective-permute-done.7.rest_1_.rest_8_
  73.7 1.0 logits.1
  74.7 5.2 %all-gather.2 = f32[2,4,72]{2,1,0:T(4,128)S(1)} all-gather(f32[1,4,72]{2,1,0:T(4,128)S(1)} %bitcast.43), channel_id=1, replica_groups=mesh['z'=8,'y'=8,'c'=2,'x'=4] {'c'}, dimensions={0}, use_global_device_ids=true | all-gather | bytes 3456 | tf_op jit(solution)/shard_map/all_gather | solution.py:235
  79.9 18.2 %all_to_all.25.stats_ref = f32[32,8,72]{2,1,0:T(8,128)S(1)} all-to-all(f32[32,8,72]{2,1,0:T(8,128)S(1)} %broadcast_in_dim.8), channel_id=1, replica_groups=mesh['z'=8,'y'=8,'c'=2,'x'=4] {'y','x'}, dimensions={0} | all-to-all | bytes 147456 | tf_op jit(solution)/shard_map/all_to_all | solution.py:177
  98.1 2.3 %back.1 = (bf16[8,72,640]{2,1,0:T(8,128)(2,1)S(1)}, f32[1,72]{1,0:T(1,128)S(1)}, f32[2,1]{1,0:T(2,128)S(1)}) custom-call(s32[10]{0:T(128)S(1)} %stack.43.meta_ref, f32[32,8,72]{2,1,0:T(8,128)S(1)} %all_to_all.25.stats_ref, f32[500,72]{1,0:T(8,128)S(1)} %get-tuple-element.8.logits_ref, s32[1,72]{1,0:T(1,128)S(1)} %get-tuple-element.25.label_ref, ...), custom_call_target="tpu_custom_call" | custom-call | tf_op jit(solution)/shard_map/back/pallas_call | solution.py:161
  100.5 0.9 copy-done.1
  101.3 5.5 %all-to-all-start.3 = ((bf16[8,72,640]{2,1,0:T(8,128)(2,1)}), bf16[8,72,640]{2,1,0:T(8,128)(2,1)S(1)}, u32[]{:S(2)}, u32[]{:S(2)}) async-start(bf16[8,72,640]{2,1,0:T(8,128)(2,1)} %copy-done.1), calls=%async_computation.3 | async-start | bytes 1474560 | tf_op jit(solution)/shard_map/all_to_all | solution.py:239
  107.2 11.4 %all-to-all-done.3 = bf16[8,72,640]{2,1,0:T(8,128)(2,1)S(1)} async-done(((bf16[8,72,640]{2,1,0:T(8,128)(2,1)}), bf16[8,72,640]{2,1,0:T(8,128)(2,1)S(1)}, u32[]{:S(2)}, u32[]{:S(2)}) %all-to-all-start.3) | async-done | bytes 737312 | tf_op jit(solution)/shard_map/all_to_all | solution.py:239
  118.7 0.9 convolution_convert_fusion
  119.6 4.2 %all-to-all-start.4 = ((bf16[16,16,640]{2,1,0:T(8,128)(2,1)}), bf16[16,16,640]{2,1,0:T(8,128)(2,1)S(1)}, u32[]{:S(2)}, u32[]{:S(2)}) async-start(bf16[16,16,640]{2,1,0:T(8,128)(2,1)} %bitcast.21), calls=%async_computation.4 | async-start | bytes 655360 | tf_op jit(solution)/shard_map/all_to_all | solution.py:243
  124.1 0.6 copy.29
  124.9 12.0 %all-to-all-done.4 = bf16[16,16,640]{2,1,0:T(8,128)(2,1)S(1)} async-done(((bf16[16,16,640]{2,1,0:T(8,128)(2,1)}), bf16[16,16,640]{2,1,0:T(8,128)(2,1)S(1)}, u32[]{:S(2)}, u32[]{:S(2)}) %all-to-all-start.4) | async-done | bytes 327712 | tf_op jit(solution)/shard_map/all_to_all | solution.py:243
  137.1 0.6 copy.28
  (50 shorter events, 2.5 us)
Async XLA Ops:
  0.6 26.5 %collective-permute-start = (bf16[500,640]{1,0:T(8,128)(2,1)}, bf16[500,640]{1,0:T(8,128)(2,1)S(1)}, u32[]{:S(2)}, u32[]{:S(2)}) collective-permute-start(bf16[500,640]{1,0:T(8,128)(2,1)} %bitcast.39), channel_id=1, source_target_pairs={{0,64},{64,128},{128,192},{192,256},{256,320},{320,384},{384,448},... | collective-permute-start | bytes 1920008 | tf_op jit(solution)/shard_map/ppermute | solution.py:186
  5.5 23.6 %collective-permute-start.1 = (bf16[500,640]{1,0:T(8,128)(2,1)}, bf16[500,640]{1,0:T(8,128)(2,1)S(1)}, u32[]{:S(2)}, u32[]{:S(2)}) collective-permute-start(bf16[500,640]{1,0:T(8,128)(2,1)} %bitcast.40), channel_id=1, source_target_pairs={{0,448},{64,0},{128,64},{192,128},{256,192},{320,256},{384,320},{4... | collective-permute-start | bytes 1920008 | tf_op jit(solution)/shard_map/ppermute | solution.py:187
  14.1 19.6 %copy-start.3 = (bf16[5120]{0:T(1024)(128)(2,1)S(1)}, bf16[5120]{0:T(1024)(128)(2,1)}, u32[]{:S(2)}) copy-start(bf16[5120]{0:T(1024)(128)(2,1)} %param.6) | copy-start | bytes 30724
  20.6 19.1 %all-to-all-start = ((bf16[8,24,768]{2,1,0:T(8,128)(2,1)}), bf16[8,24,768]{2,1,0:T(8,128)(2,1)S(1)}, u32[]{:S(2)}, u32[]{:S(2)}) async-start(bf16[8,24,768]{2,1,0:T(8,128)(2,1)} %broadcast_in_dim.6), calls=%async_computation | async-start | bytes 589824 | tf_op jit(solution)/shard_map/all_to_all | solution.py:177
  27.2 18.5 %collective-permute-start.2 = (bf16[500,640]{1,0:T(8,128)(2,1)S(1)}, bf16[500,640]{1,0:T(8,128)(2,1)S(1)}, u32[]{:S(2)}, u32[]{:S(2)}) collective-permute-start(bf16[500,640]{1,0:T(8,128)(2,1)S(1)} %collective-permute-done.rest_1_), channel_id=1, source_target_pairs={{0,64},{64,128},{128,192},{192,256},{256,320},{320,384},{384,448},... | collective-permute-start | bytes 1920008 | tf_op jit(solution)/shard_map/ppermute | solution.py:186
  29.1 18.5 %collective-permute-start.3 = (bf16[500,640]{1,0:T(8,128)(2,1)S(1)}, bf16[500,640]{1,0:T(8,128)(2,1)}, u32[]{:S(2)}, u32[]{:S(2)}) collective-permute-start(bf16[500,640]{1,0:T(8,128)(2,1)S(1)} %collective-permute-done.1.rest_2_), channel_id=1, source_target_pairs={{0,448},{64,0},{128,64},{192,128},{256,192},{320,256},{384,320},{4... | collective-permute-start | bytes 1920008 | tf_op jit(solution)/shard_map/ppermute | solution.py:187
  41.1 11.2 %all-to-all-start.1 = ((bf16[4,72,640]{2,1,0:T(8,128)(2,1)}), bf16[4,72,640]{2,1,0:T(8,128)(2,1)}, u32[]{:S(2)}, u32[]{:S(2)}) async-start(bf16[4,72,640]{2,1,0:T(8,128)(2,1)} %broadcast_in_dim.7), calls=%async_computation.1 | async-start | bytes 737280 | tf_op jit(solution)/shard_map/all_to_all | solution.py:177
  45.7 17.6 %collective-permute-start.4 = (bf16[500,640]{1,0:T(8,128)(2,1)S(1)}, bf16[500,640]{1,0:T(8,128)(2,1)S(1)}, u32[]{:S(2)}, u32[]{:S(2)}) collective-permute-start(bf16[500,640]{1,0:T(8,128)(2,1)S(1)} %collective-permute-done.2.rest_3_), channel_id=1, source_target_pairs={{0,64},{64,128},{128,192},{192,256},{256,320},{320,384},{384,448},... | collective-permute-start | bytes 1920008 | tf_op jit(solution)/shard_map/ppermute | solution.py:186
  47.6 17.6 %collective-permute-start.5 = (bf16[500,640]{1,0:T(8,128)(2,1)}, bf16[500,640]{1,0:T(8,128)(2,1)S(1)}, u32[]{:S(2)}, u32[]{:S(2)}) collective-permute-start(bf16[500,640]{1,0:T(8,128)(2,1)} %collective-permute-done.3.rest_4_), channel_id=1, source_target_pairs={{0,448},{64,0},{128,64},{192,128},{256,192},{320,256},{384,320},{4... | collective-permute-start | bytes 1920008 | tf_op jit(solution)/shard_map/ppermute | solution.py:187
  56.8 13.4 %copy-start = (bf16[640,500]{0,1:T(8,128)(2,1)S(1)}, bf16[640,500]{0,1:T(8,128)(2,1)}, u32[]{:S(2)}) copy-start(bf16[640,500]{0,1:T(8,128)(2,1)} %param.7) | copy-start | bytes 1920004
  63.3 10.3 %collective-permute-start.6 = (bf16[264,640]{1,0:T(8,128)(2,1)S(1)}, bf16[264,640]{1,0:T(8,128)(2,1)S(1)}, u32[]{:S(2)}, u32[]{:S(2)}) collective-permute-start(bf16[264,640]{1,0:T(8,128)(2,1)S(1)} %slice.49), channel_id=1, source_target_pairs={{0,64},{64,128},{128,192},{192,256},{256,320},{320,384},{384,448},... | collective-permute-start | bytes 1013768 | tf_op jit(solution)/shard_map/ppermute | solution.py:189
  65.3 8.4 %collective-permute-start.7 = (bf16[236,640]{1,0:T(8,128)(2,1)S(1)}, bf16[236,640]{1,0:T(8,128)(2,1)S(1)}, u32[]{:S(2)}, u32[]{:S(2)}) collective-permute-start(bf16[236,640]{1,0:T(8,128)(2,1)S(1)} %slice.50), channel_id=1, source_target_pairs={{0,448},{64,0},{128,64},{192,128},{256,192},{320,256},{384,320},{4... | collective-permute-start | bytes 906248 | tf_op jit(solution)/shard_map/ppermute | solution.py:190
  100.4 0.9 copy-start.1
  101.3 17.3 %all-to-all-start.3 = ((bf16[8,72,640]{2,1,0:T(8,128)(2,1)}), bf16[8,72,640]{2,1,0:T(8,128)(2,1)S(1)}, u32[]{:S(2)}, u32[]{:S(2)}) async-start(bf16[8,72,640]{2,1,0:T(8,128)(2,1)} %copy-done.1), calls=%async_computation.3 | async-start | bytes 1474560 | tf_op jit(solution)/shard_map/all_to_all | solution.py:239
  106.8 17.0 %copy-start.2 = (bf16[12,1408]{1,0:T(8,128)(2,1)S(1)}, bf16[12,1408]{1,0:T(8,128)(2,1)}, u32[]{:S(2)}) copy-start(bf16[12,1408]{1,0:T(8,128)(2,1)} %pick.1) | copy-start | bytes 101380
  119.6 17.2 %all-to-all-start.4 = ((bf16[16,16,640]{2,1,0:T(8,128)(2,1)}), bf16[16,16,640]{2,1,0:T(8,128)(2,1)S(1)}, u32[]{:S(2)}, u32[]{:S(2)}) async-start(bf16[16,16,640]{2,1,0:T(8,128)(2,1)} %bitcast.21), calls=%async_computation.4 | async-start | bytes 655360 | tf_op jit(solution)/shard_map/all_to_all | solution.py:243

commit v5 on v4

--- a/solution.py
+++ b/solution.py
@@ -10,8 +10,7 @@
 EPS = 1e-05
 LIVE = 72
 SPAN = 500
-PART = 264
-NEAR = 7
+RING = 3
 WIDTH = 640
 FACTS = 128
 F32 = jnp.float32
@@ -70,97 +69,123 @@
     return lax.dot_general(head, normed, (((1,), (1,)), ((), ())), preferred_element_type=F32)
 
 
-def first_kernel(meta_ref, normed_ref, *rest):
+def early_kernel(meta_ref, normed_ref, *rest):
     *refs, logits_ref = rest
-    total = jnp.zeros((SPAN, LIVE), F32)
-    for place, ref in enumerate(refs):
-        total += scores(meta_ref[2 + place], normed_ref, ref[...])
-    logits_ref[...] = total
-
-
-def logits_kernel(meta_ref, normed_ref, label_ref, first_ref, *rest):
-    *refs, logits_ref, stats_ref = rest
-    parts = [scores(meta_ref[9], normed_ref, ref[...]) for ref in refs]
-    logits = first_ref[...] + jnp.concatenate(parts, axis=0)
-    logits_ref[...] = logits
+    mine = other = jnp.zeros((SPAN, LIVE), F32)
+    for i, ref in enumerate(refs):
+        part = scores(meta_ref[2 + (i + 1) // 2], normed_ref, ref[...])
+        if i == 0 or i % 2 == 1:
+            mine += part
+        else:
+            other += part
+    logits_ref[0] = mine
+    logits_ref[1] = other
+
+
+def far_kernel(meta_ref, normed_ref, begun_ref, far_ref, logits_ref):
+    logits_ref[0] = begun_ref[0] + scores(meta_ref[2 + RING + 1], normed_ref, far_ref[...])
+    logits_ref[1] = begun_ref[1]
+
+
+def sum_kernel(meta_ref, label_ref, own_ref, came_ref, logits_ref, stats_ref):
     column = lax.broadcasted_iota(jnp.int32, (SPAN, LIVE), 0)
-    hits = column + meta_ref[0] == label_ref[...]
-    peak = jnp.max(logits, axis=0, keepdims=True)
-    shifted = jnp.exp(logits - peak)
-    stats_ref[0:1, :] = peak
-    stats_ref[1:2, :] = jnp.sum(shifted, axis=0, keepdims=True)
-    stats_ref[2:3, :] = jnp.sum(shifted * (logits - peak), axis=0, keepdims=True)
-    stats_ref[3:4, :] = jnp.sum(jnp.where(hits, logits, 0.0), axis=0, keepdims=True)
+    parts = [own_ref[i] + came_ref[1 - i] for i in range(2)]
+    peak = jnp.max(jnp.maximum(*parts), axis=0, keepdims=True)
+    mass = mean = aimed = jnp.zeros((1, LIVE), F32)
+    for i, logits in enumerate(parts):
+        logits_ref[i] = logits
+        hits = column + meta_ref[i] == label_ref[...]
+        shifted = jnp.exp(logits - peak)
+        mass += jnp.sum(shifted, axis=0, keepdims=True)
+        mean += jnp.sum(shifted * (logits - peak), axis=0, keepdims=True)
+        aimed += jnp.sum(jnp.where(hits, logits, 0.0), axis=0, keepdims=True)
+    for i, value in enumerate((peak, mass, mean, aimed)):
+        stats_ref[i : i + 1, :] = value
 
 
 VMEM = pl.BlockSpec(memory_space=pltpu.VMEM)
 SMEM = pl.BlockSpec(memory_space=pltpu.SMEM)
 
 
-def local_logits(meta, normed, label, near):
-    first = pl.pallas_call(
-        first_kernel,
-        in_specs=[SMEM, VMEM, *[VMEM] * NEAR],
+BOTH = jax.ShapeDtypeStruct((2, SPAN, LIVE), F32)
+
+
+def early_logits(meta, normed, near):
+    count = len(near)
+    return pl.pallas_call(
+        early_kernel,
+        in_specs=[SMEM, *[VMEM] * (1 + count)],
         out_specs=VMEM,
-        out_shape=jax.ShapeDtypeStruct((SPAN, LIVE), F32),
+        out_shape=BOTH,
         compiler_params=params(),
         cost_estimate=pl.CostEstimate(
-            flops=2 * NEAR * SPAN * LIVE * WIDTH,
-            bytes_accessed=2 * NEAR * SPAN * WIDTH,
+            flops=2 * count * SPAN * LIVE * WIDTH,
+            bytes_accessed=2 * count * SPAN * WIDTH,
             transcendentals=0,
         ),
         name="logits_early",
-    )(meta, normed, *near[:NEAR])
-    return pl.pallas_call(
-        logits_kernel,
-        in_specs=[SMEM, VMEM, VMEM, VMEM, *[VMEM] * (9 - NEAR)],
+    )(meta, normed, *near)
+
+
+def far_logits(meta, normed, begun, far):
+    return pl.pallas_call(
+        far_kernel,
+        in_specs=[SMEM, VMEM, VMEM, VMEM],
+        out_specs=VMEM,
+        out_shape=BOTH,
+        compiler_params=params(),
+        name="logits_far",
+    )(meta, normed, begun, far)
+
+
+def sum_logits(meta, label, own, came):
+    return pl.pallas_call(
+        sum_kernel,
+        in_specs=[SMEM, VMEM, VMEM, VMEM],
         out_specs=[VMEM, VMEM],
-        out_shape=[
-            jax.ShapeDtypeStruct((SPAN, LIVE), F32),
-            jax.ShapeDtypeStruct((4, LIVE), F32),
-        ],
+        out_shape=[BOTH, jax.ShapeDtypeStruct((4, LIVE), F32)],
         compiler_params=params(),
         name="logits",
-    )(meta, normed, label, first, *near[NEAR:])
+    )(meta, label, own, came)
+
+
+def slope_of(logits, first, label, peak, mass):
+    column = lax.broadcasted_iota(jnp.int32, (SPAN, LIVE), 0)
+    hits = (column + first == label).astype(F32)
+    return (jnp.exp(logits - peak) / mass - hits).T.astype(BF16)
 
 
 def back_kernel(meta_ref, stats_ref, logits_ref, label_ref, layer_ref, *rest):
     *refs, part_ref, row_ref, loss_ref = rest
     stats = stats_ref[...]
-    peaks = [stats[:, 4 * c, :] for c in range(2)]
-    peak = jnp.max(jnp.maximum(peaks[0], peaks[1]), axis=0, keepdims=True)
-    mass = mean = aimed = jnp.zeros((1, LIVE), F32)
-    for c in range(2):
-        weight = jnp.exp(peaks[c] - peak)
-        own = stats[:, 4 * c + 1, :]
-        mass += jnp.sum(weight * own, axis=0, keepdims=True)
-        moved = stats[:, 4 * c + 2, :] + (peaks[c] - peak) * own
-        mean += jnp.sum(weight * moved, axis=0, keepdims=True)
-        aimed += jnp.sum(stats[:, 4 * c + 3, :], axis=0, keepdims=True)
+    peaks, own = stats[:, 0, :], stats[:, 1, :]
+    peak = jnp.max(peaks, axis=0, keepdims=True)
+    weight = jnp.exp(peaks - peak)
+    mass = jnp.sum(weight * own, axis=0, keepdims=True)
+    mean = jnp.sum(weight * (stats[:, 2, :] + (peaks - peak) * own), axis=0, keepdims=True)
+    aimed = jnp.sum(stats[:, 3, :], axis=0, keepdims=True)
     row_ref[...] = mean / mass + (peak - aimed)
     loss = jnp.log(mass) + (peak - aimed)
     for layer in range(2):
         mine = (layer_ref[...] == layer).astype(F32)
         total = jnp.sum(loss * mine, axis=1, keepdims=True)
         loss_ref[layer : layer + 1, :] = total / jnp.sum(mine, axis=1, keepdims=True)
-    logits = logits_ref[...]
-    column = lax.broadcasted_iota(jnp.int32, (SPAN, LIVE), 0)
-    hits = (column + meta_ref[0] == label_ref[...]).astype(F32)
-    slope = (jnp.exp(logits - peak) / mass - hits).T.astype(BF16)
-    for place in range(8):
-        shard = meta_ref[2 + place]
-        if place < 7:
-            part = jnp.dot(slope, refs[place][...], preferred_element_type=F32)
-        else:
-            part = jnp.dot(slope[:, :PART], refs[7][...], preferred_element_type=F32)
-            part += jnp.dot(slope[:, PART:], refs[8][...], preferred_element_type=F32)
-        part_ref[shard] = part.astype(BF16)
+    label = label_ref[...]
+    mine = slope_of(logits_ref[0], meta_ref[0], label, peak, mass)
+    other = slope_of(logits_ref[1], meta_ref[1], label, peak, mass)
+    part_ref[...] = jnp.zeros_like(part_ref)
+    for place in range(RING + 2):
+        own = 0 if place == 0 else 2 * place - 1
+        part = jnp.dot(mine, refs[own][...], preferred_element_type=F32)
+        if 0 < place <= RING:
+            part += jnp.dot(other, refs[own + 1][...], preferred_element_type=F32)
+        part_ref[meta_ref[2 + place]] = part.astype(BF16)
 
 
 def local_back(meta, stats, logits, label, layer, near):
     return pl.pallas_call(
         back_kernel,
-        in_specs=[SMEM, VMEM, VMEM, VMEM, VMEM, *[VMEM] * 9],
+        in_specs=[SMEM, *[VMEM] * (4 + len(near))],
         out_specs=[VMEM] * 3,
         out_shape=[
             jax.ShapeDtypeStruct((8, LIVE, WIDTH), BF16),
@@ -177,18 +202,24 @@
     return lax.all_to_all(copies, axes, 0, 0, tiled=True)
 
 
+def swap_core(values):
+    return lax.ppermute(values, "c", [(0, 1), (1, 0)])
+
+
+def after(values, *others):
+    return lax.optimization_barrier((values, *others))[0]
+
+
 def ring(own):
-    up = [(i, (i + 1) % 8) for i in range(8)]
-    down = [(i, (i - 1) % 8) for i in range(8)]
-    right = left = own
+    onward = [(2 * i + c, 2 * ((i + 1 - 2 * c) % 8) + c) for i in range(8) for c in range(2)]
+    mine = own
+    other = swapped = swap_core(own)
     near = [own]
-    for _ in range(3):
-        right = lax.ppermute(right, "z", up)
-        left = lax.ppermute(left, "z", down)
-        near += [right, left]
-    near.append(lax.ppermute(right[:PART], "z", up))
-    near.append(lax.ppermute(left[PART:], "z", down))
-    return near
+    for _ in range(RING):
+        mine = lax.ppermute(mine, ("z", "c"), onward)
+        other = lax.ppermute(other, ("z", "c"), onward)
+        near += [mine, other]
+    return swapped, [*near, lax.ppermute(mine, ("z", "c"), onward)]
 
 
 def body(hidden, gain, head, exit_slots, targets):
@@ -198,18 +229,21 @@
     width = gain.shape[0]
     half = part_width // 2
     z, y, c, x = (lax.axis_index(name) for name in ("z", "y", "c", "x"))
-    shards = [lax.rem(z + s, 8) for s in (0, 7, 1, 6, 2, 5, 3, 4)]
+    shards = [lax.rem(z + 8 + (2 * c - 1) * s, 8) for s in range(RING + 2)]
     first = ((y * 2 + c) * 4 + x) * SPAN
-    meta = jnp.stack([first, c, *shards]).astype(jnp.int32)
-    near = ring(head.T)
+    first_other = ((y * 2 + 1 - c) * 4 + x) * SPAN
+    meta = jnp.stack([first, first_other, *shards]).astype(jnp.int32)
+    swapped, near = ring(head.T)
 
     packed = pick(exit_slots, targets, hidden)
     picked = packed[:, :part_width]
     pair = lax.all_gather(packed, "c", axis=0, tiled=True)
     pair_half = lax.dynamic_slice_in_dim(pair, c * half, half, 1)
     slots = jnp.concatenate([pair_half, pair[:, part_width:]], axis=1)
+    slots = after(slots, near[1], near[2])
     slots = spread(slots, "y", 8).reshape(16 * own, half + 128)
 
+    slots = after(slots, near[3], near[4])
     total = slots.shape[0]
     flag = slots[:, half].astype(F32)
     below = (jnp.arange(total)[:, None] < jnp.arange(total)[None, :]).astype(F32)
@@ -223,6 +257,7 @@
     label_row = (fact[1] * 256 + fact[2]).reshape(1, LIVE)
     layer_row = fact[3].reshape(1, LIVE)
     rows = spread(compact[:, :half].astype(BF16), "x", 4)
+    rows = after(rows, near[5], near[6])
     rows = lax.all_gather(rows, "c", axis=0)
 
     values = rows.astype(F32)
@@ -231,8 +266,9 @@
     gain_rows = gain_f.reshape(4, 2, 1, half).transpose(1, 0, 2, 3)
     normed = (values * scale[:, None] * gain_rows).astype(BF16)
 
-    logits, stats = local_logits(meta, normed, label_row, near)
-    stats = lax.all_gather(stats, "c", axis=0, tiled=True)
+    logits = early_logits(meta, normed, near[:-1])
+    logits = far_logits(meta, normed, logits, near[-1])
+    logits, stats = sum_logits(meta, label_row, logits, swap_core(logits))
     stats = spread(stats, ("y", "x"), 32)
     part, gap, group_loss = local_back(meta, stats, logits, label_row, layer_row, near)
 

time: 139 us -> 137 us (0.986)
  blocking collectives: 30.3 us -> 17.6 us
  waiting for transfers between devices: 37.3 us -> 43.8 us
  Pallas kernels: 8.78 us -> 11.2 us
  starting transfers between devices: 53.3 us -> 54.7 us
    all_to_all x2, waiting for transfers between devices: 5.77 us -> 16.1 us  [spread(): return lax.all_to_all(copies, axes, 0, 0, tiled=True)]
    all_to_all x1, blocking collectives: 18.2 us -> 12.9 us  [spread(): return lax.all_to_all(copies, axes, 0, 0, tiled=True)]
    all_gather x1 -> x0, blocking collectives: 5.17 us -> none  [body(): stats = lax.all_gather(stats, 'c', axis=0, tiled=True)]
    ppermute x8 -> x9, waiting for transfers between devices: 8.07 us -> 4.22 us  [the longest x3 1.9 us: ring(): other = lax.ppermute(other, ('z', 'c'), onward)]
    pallas_call x3 -> x4, Pallas kernels: 5.81 us -> 8.34 us  [the longest x1 2.65 us: early_logits(): pl.pallas_call(early_kernel, in_specs=[SMEM, *[VMEM] * (1 + count)], out_...]
    all_gather x1, blocking collectives: 4.23 us -> 2.66 us  [body(): rows = lax.all_gather(rows, 'c', axis=0)]
    ppermute x8 -> x9, starting transfers between devices: 32.9 us -> 34.2 us  [the longest x3 12.1 us: ring(): mine = lax.ppermute(mine, ('z', 'c'), onward)]
    unnamed x12 -> x18, local copies, waits for them, and re-layouts: 2.2 us -> 2.95 us
  transfers between devices with their start and end apart: 12 -> 13, of which waited for: 6 -> 7; matrix products, arithmetic and copies ran while one was open for 3% -> 3% of each run, Pallas kernels for 4% -> 4%
where the time goes in v5:
time: 137 us; the launch traced here: 136 us
  starting transfers between devices  54.7 us (40%)
  waiting for transfers between devices  43.8 us (32%)
  blocking collectives  17.6 us (13%)
  Pallas kernels  11.2 us (8%)
  local copies, waits for them, and re-layouts  4.99 us (4%)
  other arithmetic  1.51 us (1%)
    all_to_all x2, waiting for transfers between devices, spread(): return lax.all_to_all(copies, axes, 0, 0, tiled=True)  16.1 us
    all_to_all x1, blocking collectives, spread(): return lax.all_to_all(copies, axes, 0, 0, tiled=True)  12.9 us
    ppermute x3, starting transfers between devices, ring(): mine = lax.ppermute(mine, ('z', 'c'), onward)  12.1 us
    all_to_all x1, waiting for transfers between devices, body(): back = lax.all_to_all(sent, ('y', 'c'), 0, 0, tiled=True)  12 us
    all_to_all x1, waiting for transfers between devices, body(): part = lax.all_to_all(part, ('x', 'c'), 0, 0, tiled=True)  11.4 us
    ppermute x2, starting transfers between devices, swap_core(): return lax.ppermute(values, 'c', [(0, 1), (1, 0)])  11.1 us
    all_to_all x2, starting transfers between devices, spread(): return lax.all_to_all(copies, axes, 0, 0, tiled=True)  11.1 us
    ppermute x3, starting transfers between devices, ring(): other = lax.ppermute(other, ('z', 'c'), onward)  9.12 us
  transfers between devices with their start and end apart: 13, of which 7 were waited for; matrix products, arithmetic and copies ran while one was open for 3% of the time, Pallas kernels for 4%

profile of v5, /device:TPU:1, one launch (start us, length us, event | category | flops | bytes accessed | tf_op | source)
XLA Modules:
  0.0 136.1 jit_solution(14292333887105541851)
XLA Ops:
  0.6 8.8 %collective-permute-start.1 = (bf16[500,640]{1,0:T(8,128)(2,1)}, bf16[500,640]{1,0:T(8,128)(2,1)S(1)}, u32[]{:S(2)}, u32[]{:S(2)}) collective-permute-start(bf16[500,640]{1,0:T(8,128)(2,1)} %bitcast.34), channel_id=1, source_target_pairs={{0,4},{4,0},{1,5},{5,1},{2,6},{6,2},{3,7},{7,3},{8,12},{12,8},{9,1... | collective-permute-start | bytes 1920008 | tf_op jit(solution)/shard_map/ppermute | solution.py:206
  9.4 5.3 %collective-permute-start = (bf16[500,640]{1,0:T(8,128)(2,1)}, bf16[500,640]{1,0:T(8,128)(2,1)S(1)}, u32[]{:S(2)}, u32[]{:S(2)}) collective-permute-start(bf16[500,640]{1,0:T(8,128)(2,1)} %bitcast.35), channel_id=1, source_target_pairs={{0,64},{4,452},{64,128},{68,4},{128,192},{132,68},{192,256},{196,1... | collective-permute-start | bytes 1920008 | tf_op jit(solution)/shard_map/ppermute | solution.py:219
  14.7 2.2 %collective-permute-start.2 = (bf16[500,640]{1,0:T(8,128)(2,1)S(1)}, bf16[500,640]{1,0:T(8,128)(2,1)S(1)}, u32[]{:S(2)}, u32[]{:S(2)}) collective-permute-start(bf16[500,640]{1,0:T(8,128)(2,1)S(1)} %collective-permute-done.1), channel_id=1, source_target_pairs={{0,64},{4,452},{64,128},{68,4},{128,192},{132,68},{192,256},{196,1... | collective-permute-start | bytes 1920008 | tf_op jit(solution)/shard_map/ppermute | solution.py:220
  16.9 2.8 %pick.1 = bf16[12,1408]{1,0:T(8,128)(2,1)} custom-call(s32[2,6]{1,0:T(2,128)} %slots_ref.1, s32[256]{0:T(256)} %targets_ref.1, bf16[2,256,1280]{2,1,0:T(8,128)(2,1)} %hidden_ref.1), custom_call_target="tpu_custom_call" | custom-call | tf_op jit(solution)/shard_map/pick/pallas_call | solution.py:52
  19.8 2.1 %all-gather.1 = bf16[2,12,1408]{2,1,0:T(8,128)(2,1)S(1)} all-gather(bf16[1,12,1408]{2,1,0:T(8,128)(2,1)} %bitcast.43), channel_id=1, replica_groups=mesh['z'=8,'y'=8,'c'=2,'x'=4] {'c'}, dimensions={0}, use_global_device_ids=true | all-gather | bytes 101376 | tf_op jit(solution)/shard_map/all_gather | solution.py:240
  22.4 4.9 %collective-permute-start.3 = (bf16[500,640]{1,0:T(8,128)(2,1)S(1)}, bf16[500,640]{1,0:T(8,128)(2,1)S(1)}, u32[]{:S(2)}, u32[]{:S(2)}) collective-permute-start(bf16[500,640]{1,0:T(8,128)(2,1)S(1)} %collective-permute-done.rest_1_), channel_id=1, source_target_pairs={{0,64},{4,452},{64,128},{68,4},{128,192},{132,68},{192,256},{196,1... | collective-permute-start | bytes 1920008 | tf_op jit(solution)/shard_map/ppermute | solution.py:219
  27.4 1.9 %collective-permute-done.2.rest_2_ = bf16[500,640]{1,0:T(8,128)(2,1)S(1)} collective-permute-done((bf16[500,640]{1,0:T(8,128)(2,1)S(1)}, bf16[500,640]{1,0:T(8,128)(2,1)S(1)}, u32[]{:S(2)}, u32[]{:S(2)}) %collective-permute-start.2) | collective-permute-done | bytes 640032 | tf_op jit(solution)/shard_map/ppermute | solution.py:220
  29.3 5.0 %collective-permute-start.4 = (bf16[500,640]{1,0:T(8,128)(2,1)S(1)}, bf16[500,640]{1,0:T(8,128)(2,1)S(1)}, u32[]{:S(2)}, u32[]{:S(2)}) collective-permute-start(bf16[500,640]{1,0:T(8,128)(2,1)S(1)} %collective-permute-done.2.rest_2_), channel_id=1, source_target_pairs={{0,64},{4,452},{64,128},{68,4},{128,192},{132,68},{192,256},{196,1... | collective-permute-start | bytes 1920008 | tf_op jit(solution)/shard_map/ppermute | solution.py:220
  34.3 0.7 broadcast_in_dim.6
  35.0 7.0 %all-to-all-start = ((bf16[8,24,768]{2,1,0:T(8,128)(2,1)}), bf16[8,24,768]{2,1,0:T(8,128)(2,1)S(1)}, u32[]{:S(2)}, u32[]{:S(2)}) async-start(bf16[8,24,768]{2,1,0:T(8,128)(2,1)} %broadcast_in_dim.6), calls=%async_computation | async-start | bytes 589824 | tf_op jit(solution)/shard_map/all_to_all | solution.py:202
  42.0 1.9 %collective-permute-start.5 = (bf16[500,640]{1,0:T(8,128)(2,1)S(1)}, bf16[500,640]{1,0:T(8,128)(2,1)}, u32[]{:S(2)}, u32[]{:S(2)}) collective-permute-start(bf16[500,640]{1,0:T(8,128)(2,1)S(1)} %collective-permute-done.3.rest_3_), channel_id=1, source_target_pairs={{0,64},{4,452},{64,128},{68,4},{128,192},{132,68},{192,256},{196,1... | collective-permute-start | bytes 1920008 | tf_op jit(solution)/shard_map/ppermute | solution.py:219
  43.9 9.9 %all-to-all-done = bf16[8,24,768]{2,1,0:T(8,128)(2,1)S(1)} async-done(((bf16[8,24,768]{2,1,0:T(8,128)(2,1)}), bf16[8,24,768]{2,1,0:T(8,128)(2,1)S(1)}, u32[]{:S(2)}, u32[]{:S(2)}) %all-to-all-start) | async-done | bytes 294944 | tf_op jit(solution)/shard_map/all_to_all | solution.py:202
  53.9 1.9 %collective-permute-start.6 = (bf16[500,640]{1,0:T(8,128)(2,1)S(1)}, bf16[500,640]{1,0:T(8,128)(2,1)}, u32[]{:S(2)}, u32[]{:S(2)}) collective-permute-start(bf16[500,640]{1,0:T(8,128)(2,1)S(1)} %collective-permute-done.4.rest_4_), channel_id=1, source_target_pairs={{0,64},{4,452},{64,128},{68,4},{128,192},{132,68},{192,256},{196,1... | collective-permute-start | bytes 1920008 | tf_op jit(solution)/shard_map/ppermute | solution.py:220
  56.4 0.8 broadcast_in_dim.7
  57.2 4.1 %all-to-all-start.1 = ((bf16[4,72,640]{2,1,0:T(8,128)(2,1)}), bf16[4,72,640]{2,1,0:T(8,128)(2,1)}, u32[]{:S(2)}, u32[]{:S(2)}) async-start(bf16[4,72,640]{2,1,0:T(8,128)(2,1)} %broadcast_in_dim.7), calls=%async_computation.1 | async-start | bytes 737280 | tf_op jit(solution)/shard_map/all_to_all | solution.py:202
  61.5 1.9 %collective-permute-start.7 = (bf16[500,640]{1,0:T(8,128)(2,1)}, bf16[500,640]{1,0:T(8,128)(2,1)S(1)}, u32[]{:S(2)}, u32[]{:S(2)}) collective-permute-start(bf16[500,640]{1,0:T(8,128)(2,1)} %collective-permute-done.5.rest_5_), channel_id=1, source_target_pairs={{0,64},{4,452},{64,128},{68,4},{128,192},{132,68},{192,256},{196,1... | collective-permute-start | bytes 1920008 | tf_op jit(solution)/shard_map/ppermute | solution.py:222
  63.4 6.2 %all-to-all-done.1 = bf16[4,72,640]{2,1,0:T(8,128)(2,1)} async-done(((bf16[4,72,640]{2,1,0:T(8,128)(2,1)}), bf16[4,72,640]{2,1,0:T(8,128)(2,1)}, u32[]{:S(2)}, u32[]{:S(2)}) %all-to-all-start.1) | async-done | bytes 368672 | tf_op jit(solution)/shard_map/all_to_all | solution.py:202
  69.7 2.7 %all-gather = bf16[8,72,640]{2,1,0:T(8,128)(2,1)S(1)} all-gather(bf16[4,72,640]{2,1,0:T(8,128)(2,1)} %all-to-all-done.1), channel_id=2, replica_groups=mesh['z'=8,'y'=8,'c'=2,'x'=4] {'c'}, dimensions={0}, use_global_device_ids=true | all-gather | bytes 1105920 | tf_op jit(solution)/shard_map/all_gather | solution.py:261
  73.6 2.6 %logits_early.1.begun_ref = f32[2,500,72]{2,1,0:T(8,128)S(1)} custom-call(s32[7]{0:T(128)S(1)} %stack.31.meta_ref, bf16[2,4,72,640]{3,2,1,0:T(8,128)(2,1)S(1)} %fusion.2.normed_ref, bf16[500,640]{1,0:T(8,128)(2,1)S(1)} %bitcast.36, bf16[500,640]{1,0:T(8,128)(2,1)S(1)} %collective-permute-done.rest_1_, bf16[500,640]{1,0:T(8,128)(2,1)S(1)} %collective-permute-done.2.rest_2_, ...), custom_call_target="tpu_custom_call" | custom-call | flops 322560000 | bytes 4480000 | tf_op jit(solution)/shard_map/logits_early/pallas_call | solution.py:115
  76.3 1.7 %logits_far.1.own_ref = f32[2,500,72]{2,1,0:T(8,128)} custom-call(s32[7]{0:T(128)S(1)} %stack.31.meta_ref, bf16[2,4,72,640]{3,2,1,0:T(8,128)(2,1)S(1)} %fusion.2.normed_ref, f32[2,500,72]{2,1,0:T(8,128)S(1)} %logits_early.1.begun_ref, bf16[500,640]{1,0:T(8,128)(2,1)S(1)} %collective-permute-done.7.far_ref.rest_7_), custom_call_target="tpu_custom_call" | custom-call | tf_op jit(solution)/shard_map/logits_far/pallas_call | solution.py:131
  77.9 2.3 %collective-permute-start.8 = (f32[2,500,72]{2,1,0:T(8,128)}, f32[2,500,72]{2,1,0:T(8,128)}, u32[]{:S(2)}, u32[]{:S(2)}) collective-permute-start(f32[2,500,72]{2,1,0:T(8,128)} %logits_far.1.own_ref), channel_id=1, source_target_pairs={{0,4},{4,0},{1,5},{5,1},{2,6},{6,2},{3,7},{7,3},{8,12},{12,8},{9,1... | collective-permute-start | bytes 864008 | tf_op jit(solution)/shard_map/ppermute | solution.py:206
  80.3 1.7 %collective-permute-done.8.came_ref = f32[2,500,72]{2,1,0:T(8,128)} collective-permute-done((f32[2,500,72]{2,1,0:T(8,128)}, f32[2,500,72]{2,1,0:T(8,128)}, u32[]{:S(2)}, u32[]{:S(2)}) %collective-permute-start.8) | collective-permute-done | bytes 288032 | tf_op jit(solution)/shard_map/ppermute | solution.py:206
  82.0 1.6 %logits.1 = (f32[2,500,72]{2,1,0:T(8,128)S(1)}, f32[4,72]{1,0:T(4,128)S(1)}) custom-call(s32[7]{0:T(128)S(1)} %stack.31.meta_ref, s32[1,72]{1,0:T(1,128)S(1)} %get-tuple-element.31.label_ref, f32[2,500,72]{2,1,0:T(8,128)} %logits_far.1.own_ref, f32[2,500,72]{2,1,0:T(8,128)} %collective-permute-done.8.came_ref), custom_call_target="tpu_custom_call" | custom-call | tf_op jit(solution)/shard_map/logits/pallas_call | solution.py:142
  83.6 12.9 %all_to_all.25.stats_ref = f32[32,4,72]{2,1,0:T(4,128)S(1)} all-to-all(f32[32,4,72]{2,1,0:T(4,128)S(1)} %broadcast_in_dim.8), channel_id=1, replica_groups=mesh['z'=8,'y'=8,'c'=2,'x'=4] {'y','x'}, dimensions={0} | all-to-all | bytes 73728 | tf_op jit(solution)/shard_map/all_to_all | solution.py:202
  96.5 2.5 %back.1 = (bf16[8,72,640]{2,1,0:T(8,128)(2,1)S(1)}, f32[1,72]{1,0:T(1,128)S(1)}, f32[2,1]{1,0:T(2,128)S(1)}) custom-call(s32[7]{0:T(128)S(1)} %stack.31.meta_ref, f32[32,4,72]{2,1,0:T(4,128)S(1)} %all_to_all.25.stats_ref, f32[2,500,72]{2,1,0:T(8,128)S(1)} %get-tuple-element.14.logits_ref, s32[1,72]{1,0:T(1,128)S(1)} %get-tuple-element.31.label_ref, ...), custom_call_target="tpu_custom_call" | custom-call | tf_op jit(solution)/shard_map/back/pallas_call | solution.py:186
  99.0 0.9 copy-done.4
  99.9 5.3 %all-to-all-start.3 = ((bf16[8,72,640]{2,1,0:T(8,128)(2,1)}), bf16[8,72,640]{2,1,0:T(8,128)(2,1)S(1)}, u32[]{:S(2)}, u32[]{:S(2)}) async-start(bf16[8,72,640]{2,1,0:T(8,128)(2,1)} %copy-done.4), calls=%async_computation.3 | async-start | bytes 1474560 | tf_op jit(solution)/shard_map/all_to_all | solution.py:275
  105.5 11.4 %all-to-all-done.3 = bf16[8,72,640]{2,1,0:T(8,128)(2,1)S(1)} async-done(((bf16[8,72,640]{2,1,0:T(8,128)(2,1)}), bf16[8,72,640]{2,1,0:T(8,128)(2,1)S(1)}, u32[]{:S(2)}, u32[]{:S(2)}) %all-to-all-start.3) | async-done | bytes 737312 | tf_op jit(solution)/shard_map/all_to_all | solution.py:275
  117.0 1.0 convolution_convert_fusion
  118.0 4.2 %all-to-all-start.4 = ((bf16[16,16,640]{2,1,0:T(8,128)(2,1)}), bf16[16,16,640]{2,1,0:T(8,128)(2,1)S(1)}, u32[]{:S(2)}, u32[]{:S(2)}) async-start(bf16[16,16,640]{2,1,0:T(8,128)(2,1)} %bitcast.16), calls=%async_computation.4 | async-start | bytes 655360 | tf_op jit(solution)/shard_map/all_to_all | solution.py:279
  123.2 12.0 %all-to-all-done.4 = bf16[16,16,640]{2,1,0:T(8,128)(2,1)S(1)} async-done(((bf16[16,16,640]{2,1,0:T(8,128)(2,1)}), bf16[16,16,640]{2,1,0:T(8,128)(2,1)S(1)}, u32[]{:S(2)}, u32[]{:S(2)}) %all-to-all-start.4) | async-done | bytes 327712 | tf_op jit(solution)/shard_map/all_to_all | solution.py:279
  135.4 0.6 copy.28
  (56 shorter events, 4.4 us)
Async XLA Ops:
  0.6 14.1 %collective-permute-start.1 = (bf16[500,640]{1,0:T(8,128)(2,1)}, bf16[500,640]{1,0:T(8,128)(2,1)S(1)}, u32[]{:S(2)}, u32[]{:S(2)}) collective-permute-start(bf16[500,640]{1,0:T(8,128)(2,1)} %bitcast.34), channel_id=1, source_target_pairs={{0,4},{4,0},{1,5},{5,1},{2,6},{6,2},{3,7},{7,3},{8,12},{12,8},{9,1... | collective-permute-start | bytes 1920008 | tf_op jit(solution)/shard_map/ppermute | solution.py:206
  9.4 13.0 %collective-permute-start = (bf16[500,640]{1,0:T(8,128)(2,1)}, bf16[500,640]{1,0:T(8,128)(2,1)S(1)}, u32[]{:S(2)}, u32[]{:S(2)}) collective-permute-start(bf16[500,640]{1,0:T(8,128)(2,1)} %bitcast.35), channel_id=1, source_target_pairs={{0,64},{4,452},{64,128},{68,4},{128,192},{132,68},{192,256},{196,1... | collective-permute-start | bytes 1920008 | tf_op jit(solution)/shard_map/ppermute | solution.py:219
  14.7 14.5 %collective-permute-start.2 = (bf16[500,640]{1,0:T(8,128)(2,1)S(1)}, bf16[500,640]{1,0:T(8,128)(2,1)S(1)}, u32[]{:S(2)}, u32[]{:S(2)}) collective-permute-start(bf16[500,640]{1,0:T(8,128)(2,1)S(1)} %collective-permute-done.1), channel_id=1, source_target_pairs={{0,64},{4,452},{64,128},{68,4},{128,192},{132,68},{192,256},{196,1... | collective-permute-start | bytes 1920008 | tf_op jit(solution)/shard_map/ppermute | solution.py:220
  22.4 19.6 %collective-permute-start.3 = (bf16[500,640]{1,0:T(8,128)(2,1)S(1)}, bf16[500,640]{1,0:T(8,128)(2,1)S(1)}, u32[]{:S(2)}, u32[]{:S(2)}) collective-permute-start(bf16[500,640]{1,0:T(8,128)(2,1)S(1)} %collective-permute-done.rest_1_), channel_id=1, source_target_pairs={{0,64},{4,452},{64,128},{68,4},{128,192},{132,68},{192,256},{196,1... | collective-permute-start | bytes 1920008 | tf_op jit(solution)/shard_map/ppermute | solution.py:219
  29.3 24.6 %collective-permute-start.4 = (bf16[500,640]{1,0:T(8,128)(2,1)S(1)}, bf16[500,640]{1,0:T(8,128)(2,1)S(1)}, u32[]{:S(2)}, u32[]{:S(2)}) collective-permute-start(bf16[500,640]{1,0:T(8,128)(2,1)S(1)} %collective-permute-done.2.rest_2_), channel_id=1, source_target_pairs={{0,64},{4,452},{64,128},{68,4},{128,192},{132,68},{192,256},{196,1... | collective-permute-start | bytes 1920008 | tf_op jit(solution)/shard_map/ppermute | solution.py:220
  35.0 26.3 %copy-start.6 = (bf16[5120]{0:T(1024)(128)(2,1)S(1)}, bf16[5120]{0:T(1024)(128)(2,1)}, u32[]{:S(2)}) copy-start(bf16[5120]{0:T(1024)(128)(2,1)} %param.6) | copy-start | bytes 30724
  35.0 18.8 %all-to-all-start = ((bf16[8,24,768]{2,1,0:T(8,128)(2,1)}), bf16[8,24,768]{2,1,0:T(8,128)(2,1)S(1)}, u32[]{:S(2)}, u32[]{:S(2)}) async-start(bf16[8,24,768]{2,1,0:T(8,128)(2,1)} %broadcast_in_dim.6), calls=%async_computation | async-start | bytes 589824 | tf_op jit(solution)/shard_map/all_to_all | solution.py:202
  42.0 19.5 %collective-permute-start.5 = (bf16[500,640]{1,0:T(8,128)(2,1)S(1)}, bf16[500,640]{1,0:T(8,128)(2,1)}, u32[]{:S(2)}, u32[]{:S(2)}) collective-permute-start(bf16[500,640]{1,0:T(8,128)(2,1)S(1)} %collective-permute-done.3.rest_3_), channel_id=1, source_target_pairs={{0,64},{4,452},{64,128},{68,4},{128,192},{132,68},{192,256},{196,1... | collective-permute-start | bytes 1920008 | tf_op jit(solution)/shard_map/ppermute | solution.py:219
  53.8 15.8 %copy-start.1 = (bf16[500,640]{1,0:T(8,128)(2,1)}, bf16[500,640]{1,0:T(8,128)(2,1)S(1)}, u32[]{:S(2)}) copy-start(bf16[500,640]{1,0:T(8,128)(2,1)S(1)} %collective-permute-done.4.rest_4_) | copy-start | bytes 1920004
  53.9 15.7 %collective-permute-start.6 = (bf16[500,640]{1,0:T(8,128)(2,1)S(1)}, bf16[500,640]{1,0:T(8,128)(2,1)}, u32[]{:S(2)}, u32[]{:S(2)}) collective-permute-start(bf16[500,640]{1,0:T(8,128)(2,1)S(1)} %collective-permute-done.4.rest_4_), channel_id=1, source_target_pairs={{0,64},{4,452},{64,128},{68,4},{128,192},{132,68},{192,256},{196,1... | collective-permute-start | bytes 1920008 | tf_op jit(solution)/shard_map/ppermute | solution.py:220
  57.2 12.4 %all-to-all-start.1 = ((bf16[4,72,640]{2,1,0:T(8,128)(2,1)}), bf16[4,72,640]{2,1,0:T(8,128)(2,1)}, u32[]{:S(2)}, u32[]{:S(2)}) async-start(bf16[4,72,640]{2,1,0:T(8,128)(2,1)} %broadcast_in_dim.7), calls=%async_computation.1 | async-start | bytes 737280 | tf_op jit(solution)/shard_map/all_to_all | solution.py:202
  61.5 14.8 %collective-permute-start.7 = (bf16[500,640]{1,0:T(8,128)(2,1)}, bf16[500,640]{1,0:T(8,128)(2,1)S(1)}, u32[]{:S(2)}, u32[]{:S(2)}) collective-permute-start(bf16[500,640]{1,0:T(8,128)(2,1)} %collective-permute-done.5.rest_5_), channel_id=1, source_target_pairs={{0,64},{4,452},{64,128},{68,4},{128,192},{132,68},{192,256},{196,1... | collective-permute-start | bytes 1920008 | tf_op jit(solution)/shard_map/ppermute | solution.py:222
  72.3 1.1 copy-start
  72.3 1.3 copy-start.2
  77.9 4.1 %collective-permute-start.8 = (f32[2,500,72]{2,1,0:T(8,128)}, f32[2,500,72]{2,1,0:T(8,128)}, u32[]{:S(2)}, u32[]{:S(2)}) collective-permute-start(f32[2,500,72]{2,1,0:T(8,128)} %logits_far.1.own_ref), channel_id=1, source_target_pairs={{0,4},{4,0},{1,5},{5,1},{2,6},{6,2},{3,7},{7,3},{8,12},{12,8},{9,1... | collective-permute-start | bytes 864008 | tf_op jit(solution)/shard_map/ppermute | solution.py:206
  80.3 16.2 %copy-start.3 = (bf16[500,640]{1,0:T(8,128)(2,1)S(1)}, bf16[500,640]{1,0:T(8,128)(2,1)}, u32[]{:S(2)}) copy-start(bf16[500,640]{1,0:T(8,128)(2,1)} %copy-done.1) | copy-start | bytes 1920004
  99.0 0.9 copy-start.4
  99.9 17.0 %all-to-all-start.3 = ((bf16[8,72,640]{2,1,0:T(8,128)(2,1)}), bf16[8,72,640]{2,1,0:T(8,128)(2,1)S(1)}, u32[]{:S(2)}, u32[]{:S(2)}) async-start(bf16[8,72,640]{2,1,0:T(8,128)(2,1)} %copy-done.4), calls=%async_computation.3 | async-start | bytes 1474560 | tf_op jit(solution)/shard_map/all_to_all | solution.py:275
  105.1 17.1 %copy-start.5 = (bf16[12,1408]{1,0:T(8,128)(2,1)S(1)}, bf16[12,1408]{1,0:T(8,128)(2,1)}, u32[]{:S(2)}) copy-start(bf16[12,1408]{1,0:T(8,128)(2,1)} %pick.1) | copy-start | bytes 101380
  118.0 17.2 %all-to-all-start.4 = ((bf16[16,16,640]{2,1,0:T(8,128)(2,1)}), bf16[16,16,640]{2,1,0:T(8,128)(2,1)S(1)}, u32[]{:S(2)}, u32[]{:S(2)}) async-start(bf16[16,16,640]{2,1,0:T(8,128)(2,1)} %bitcast.16), calls=%async_computation.4 | async-start | bytes 655360 | tf_op jit(solution)/shard_map/all_to_all | solution.py:279

commit v6 on v5

--- a/solution.py
+++ b/solution.py
@@ -70,7 +70,7 @@
 
 
 def early_kernel(meta_ref, normed_ref, *rest):
-    *refs, logits_ref = rest
+    *refs, mine_ref, other_ref = rest
     mine = other = jnp.zeros((SPAN, LIVE), F32)
     for i, ref in enumerate(refs):
         part = scores(meta_ref[2 + (i + 1) // 2], normed_ref, ref[...])
@@ -78,18 +78,17 @@
             mine += part
         else:
             other += part
-    logits_ref[0] = mine
-    logits_ref[1] = other
+    mine_ref[...] = mine
+    other_ref[...] = other
 
 
 def far_kernel(meta_ref, normed_ref, begun_ref, far_ref, logits_ref):
-    logits_ref[0] = begun_ref[0] + scores(meta_ref[2 + RING + 1], normed_ref, far_ref[...])
-    logits_ref[1] = begun_ref[1]
-
-
-def sum_kernel(meta_ref, label_ref, own_ref, came_ref, logits_ref, stats_ref):
+    logits_ref[...] = begun_ref[...] + scores(meta_ref[2 + RING + 1], normed_ref, far_ref[...])
+
+
+def sum_kernel(meta_ref, label_ref, mine_ref, more_ref, other_ref, rest_ref, logits_ref, stats_ref):
     column = lax.broadcasted_iota(jnp.int32, (SPAN, LIVE), 0)
-    parts = [own_ref[i] + came_ref[1 - i] for i in range(2)]
+    parts = [mine_ref[...] + more_ref[...], other_ref[...] + rest_ref[...]]
     peak = jnp.max(jnp.maximum(*parts), axis=0, keepdims=True)
     mass = mean = aimed = jnp.zeros((1, LIVE), F32)
     for i, logits in enumerate(parts):
@@ -107,6 +106,7 @@
 SMEM = pl.BlockSpec(memory_space=pltpu.SMEM)
 
 
+ONE = jax.ShapeDtypeStruct((SPAN, LIVE), F32)
 BOTH = jax.ShapeDtypeStruct((2, SPAN, LIVE), F32)
 
 
@@ -115,8 +115,8 @@
     return pl.pallas_call(
         early_kernel,
         in_specs=[SMEM, *[VMEM] * (1 + count)],
-        out_specs=VMEM,
-        out_shape=BOTH,
+        out_specs=[VMEM, VMEM],
+        out_shape=[ONE, ONE],
         compiler_params=params(),
         cost_estimate=pl.CostEstimate(
             flops=2 * count * SPAN * LIVE * WIDTH,
@@ -132,21 +132,21 @@
         far_kernel,
         in_specs=[SMEM, VMEM, VMEM, VMEM],
         out_specs=VMEM,
-        out_shape=BOTH,
+        out_shape=ONE,
         compiler_params=params(),
         name="logits_far",
     )(meta, normed, begun, far)
 
 
-def sum_logits(meta, label, own, came):
+def sum_logits(meta, label, mine, more, other, rest):
     return pl.pallas_call(
         sum_kernel,
-        in_specs=[SMEM, VMEM, VMEM, VMEM],
+        in_specs=[SMEM, *[VMEM] * 5],
         out_specs=[VMEM, VMEM],
         out_shape=[BOTH, jax.ShapeDtypeStruct((4, LIVE), F32)],
         compiler_params=params(),
         name="logits",
-    )(meta, label, own, came)
+    )(meta, label, mine, more, other, rest)
 
 
 def slope_of(logits, first, label, peak, mass):
@@ -173,7 +173,8 @@
     label = label_ref[...]
     mine = slope_of(logits_ref[0], meta_ref[0], label, peak, mass)
     other = slope_of(logits_ref[1], meta_ref[1], label, peak, mass)
-    part_ref[...] = jnp.zeros_like(part_ref)
+    for i in range(RING):
+        part_ref[meta_ref[4 + RING + i]] = jnp.zeros((LIVE, WIDTH), BF16)
     for place in range(RING + 2):
         own = 0 if place == 0 else 2 * place - 1
         part = jnp.dot(mine, refs[own][...], preferred_element_type=F32)
@@ -232,7 +233,8 @@
     shards = [lax.rem(z + 8 + (2 * c - 1) * s, 8) for s in range(RING + 2)]
     first = ((y * 2 + c) * 4 + x) * SPAN
     first_other = ((y * 2 + 1 - c) * 4 + x) * SPAN
-    meta = jnp.stack([first, first_other, *shards]).astype(jnp.int32)
+    absent = [lax.rem(z + 8 - (2 * c - 1) * s, 8) for s in range(1, RING + 1)]
+    meta = jnp.stack([first, first_other, *shards, *absent]).astype(jnp.int32)
     swapped, near = ring(head.T)
 
     packed = pick(exit_slots, targets, hidden)
@@ -266,9 +268,10 @@
     gain_rows = gain_f.reshape(4, 2, 1, half).transpose(1, 0, 2, 3)
     normed = (values * scale[:, None] * gain_rows).astype(BF16)
 
-    logits = early_logits(meta, normed, near[:-1])
-    logits = far_logits(meta, normed, logits, near[-1])
-    logits, stats = sum_logits(meta, label_row, logits, swap_core(logits))
+    mine, other = early_logits(meta, normed, near[:-1])
+    more = swap_core(other)
+    mine = far_logits(meta, normed, mine, near[-1])
+    logits, stats = sum_logits(meta, label_row, mine, more, other, swap_core(mine))
     stats = spread(stats, ("y", "x"), 32)
     part, gap, group_loss = local_back(meta, stats, logits, label_row, layer_row, near)
 

time: 137 us -> 137 us (level)
  starting transfers between devices: 54.7 us -> 56.8 us
    ppermute x2 -> x3, starting transfers between devices: 11.1 us -> 13.1 us  [swap_core(): return lax.ppermute(values, 'c', [(0, 1), (1, 0)])]
    unnamed x18 -> x14, local copies, waits for them, and re-layouts: 2.95 us -> 3.42 us
  transfers between devices with their start and end apart: 13 -> 14, of which waited for: 7 -> 7; matrix products, arithmetic and copies ran while one was open for 3% -> 4% of each run, Pallas kernels for 4% -> 5%
where the time goes in v6:
time: 137 us; the launch traced here: 136 us
  starting transfers between devices  56.8 us (41%)
  waiting for transfers between devices  42.5 us (31%)
  blocking collectives  16.5 us (12%)
  Pallas kernels  10.1 us (7%)
  local copies, waits for them, and re-layouts  5.48 us (4%)
  other arithmetic  2.28 us (2%)
    all_to_all x2, waiting for transfers between devices, spread(): return lax.all_to_all(copies, axes, 0, 0, tiled=True)  15.2 us
    ppermute x3, starting transfers between devices, swap_core(): return lax.ppermute(values, 'c', [(0, 1), (1, 0)])  13.1 us
    ppermute x3, starting transfers between devices, ring(): mine = lax.ppermute(mine, ('z', 'c'), onward)  12.1 us
    all_to_all x1, waiting for transfers between devices, body(): back = lax.all_to_all(sent, ('y', 'c'), 0, 0, tiled=True)  12 us
    all_to_all x1, blocking collectives, spread(): return lax.all_to_all(copies, axes, 0, 0, tiled=True)  11.8 us
    all_to_all x1, waiting for transfers between devices, body(): part = lax.all_to_all(part, ('x', 'c'), 0, 0, tiled=True)  11.4 us
    all_to_all x2, starting transfers between devices, spread(): return lax.all_to_all(copies, axes, 0, 0, tiled=True)  11.1 us
    ppermute x3, starting transfers between devices, ring(): other = lax.ppermute(other, ('z', 'c'), onward)  9.12 us
  transfers between devices with their start and end apart: 14, of which 7 were waited for; matrix products, arithmetic and copies ran while one was open for 4% of the time, Pallas kernels for 5%

profile of v6, /device:TPU:1, one launch (start us, length us, event | category | flops | bytes accessed | tf_op | source)
XLA Modules:
  0.0 135.9 jit_solution(18105584403206601771)
XLA Ops:
  0.6 8.8 %collective-permute-start.1 = (bf16[500,640]{1,0:T(8,128)(2,1)}, bf16[500,640]{1,0:T(8,128)(2,1)S(1)}, u32[]{:S(2)}, u32[]{:S(2)}) collective-permute-start(bf16[500,640]{1,0:T(8,128)(2,1)} %bitcast.37), channel_id=1, source_target_pairs={{0,4},{4,0},{1,5},{5,1},{2,6},{6,2},{3,7},{7,3},{8,12},{12,8},{9,1... | collective-permute-start | bytes 1920008 | tf_op jit(solution)/shard_map/ppermute | solution.py:207
  9.4 5.3 %collective-permute-start = (bf16[500,640]{1,0:T(8,128)(2,1)}, bf16[500,640]{1,0:T(8,128)(2,1)S(1)}, u32[]{:S(2)}, u32[]{:S(2)}) collective-permute-start(bf16[500,640]{1,0:T(8,128)(2,1)} %bitcast.38), channel_id=1, source_target_pairs={{0,64},{4,452},{64,128},{68,4},{128,192},{132,68},{192,256},{196,1... | collective-permute-start | bytes 1920008 | tf_op jit(solution)/shard_map/ppermute | solution.py:220
  14.7 2.2 %collective-permute-start.2 = (bf16[500,640]{1,0:T(8,128)(2,1)S(1)}, bf16[500,640]{1,0:T(8,128)(2,1)S(1)}, u32[]{:S(2)}, u32[]{:S(2)}) collective-permute-start(bf16[500,640]{1,0:T(8,128)(2,1)S(1)} %collective-permute-done.1), channel_id=1, source_target_pairs={{0,64},{4,452},{64,128},{68,4},{128,192},{132,68},{192,256},{196,1... | collective-permute-start | bytes 1920008 | tf_op jit(solution)/shard_map/ppermute | solution.py:221
  16.9 2.8 %pick.1 = bf16[12,1408]{1,0:T(8,128)(2,1)} custom-call(s32[2,6]{1,0:T(2,128)} %slots_ref.1, s32[256]{0:T(256)} %targets_ref.1, bf16[2,256,1280]{2,1,0:T(8,128)(2,1)} %hidden_ref.1), custom_call_target="tpu_custom_call" | custom-call | tf_op jit(solution)/shard_map/pick/pallas_call | solution.py:52
  19.8 2.1 %all-gather.1 = bf16[2,12,1408]{2,1,0:T(8,128)(2,1)S(1)} all-gather(bf16[1,12,1408]{2,1,0:T(8,128)(2,1)} %bitcast.46), channel_id=1, replica_groups=mesh['z'=8,'y'=8,'c'=2,'x'=4] {'c'}, dimensions={0}, use_global_device_ids=true | all-gather | bytes 101376 | tf_op jit(solution)/shard_map/all_gather | solution.py:242
  22.4 4.9 %collective-permute-start.3 = (bf16[500,640]{1,0:T(8,128)(2,1)S(1)}, bf16[500,640]{1,0:T(8,128)(2,1)S(1)}, u32[]{:S(2)}, u32[]{:S(2)}) collective-permute-start(bf16[500,640]{1,0:T(8,128)(2,1)S(1)} %collective-permute-done.rest_1_), channel_id=1, source_target_pairs={{0,64},{4,452},{64,128},{68,4},{128,192},{132,68},{192,256},{196,1... | collective-permute-start | bytes 1920008 | tf_op jit(solution)/shard_map/ppermute | solution.py:220
  27.4 1.9 %collective-permute-done.2.rest_2_ = bf16[500,640]{1,0:T(8,128)(2,1)S(1)} collective-permute-done((bf16[500,640]{1,0:T(8,128)(2,1)S(1)}, bf16[500,640]{1,0:T(8,128)(2,1)S(1)}, u32[]{:S(2)}, u32[]{:S(2)}) %collective-permute-start.2) | collective-permute-done | bytes 640032 | tf_op jit(solution)/shard_map/ppermute | solution.py:221
  29.3 5.0 %collective-permute-start.4 = (bf16[500,640]{1,0:T(8,128)(2,1)S(1)}, bf16[500,640]{1,0:T(8,128)(2,1)S(1)}, u32[]{:S(2)}, u32[]{:S(2)}) collective-permute-start(bf16[500,640]{1,0:T(8,128)(2,1)S(1)} %collective-permute-done.2.rest_2_), channel_id=1, source_target_pairs={{0,64},{4,452},{64,128},{68,4},{128,192},{132,68},{192,256},{196,1... | collective-permute-start | bytes 1920008 | tf_op jit(solution)/shard_map/ppermute | solution.py:221
  35.0 7.0 %all-to-all-start = ((bf16[8,24,768]{2,1,0:T(8,128)(2,1)}), bf16[8,24,768]{2,1,0:T(8,128)(2,1)S(1)}, u32[]{:S(2)}, u32[]{:S(2)}) async-start(bf16[8,24,768]{2,1,0:T(8,128)(2,1)} %broadcast_in_dim.6), calls=%async_computation | async-start | bytes 589824 | tf_op jit(solution)/shard_map/all_to_all | solution.py:203
  42.0 1.9 %collective-permute-start.5 = (bf16[500,640]{1,0:T(8,128)(2,1)S(1)}, bf16[500,640]{1,0:T(8,128)(2,1)S(1)}, u32[]{:S(2)}, u32[]{:S(2)}) collective-permute-start(bf16[500,640]{1,0:T(8,128)(2,1)S(1)} %collective-permute-done.3.rest_3_), channel_id=1, source_target_pairs={{0,64},{4,452},{64,128},{68,4},{128,192},{132,68},{192,256},{196,1... | collective-permute-start | bytes 1920008 | tf_op jit(solution)/shard_map/ppermute | solution.py:220
  43.9 9.9 %all-to-all-done = bf16[8,24,768]{2,1,0:T(8,128)(2,1)S(1)} async-done(((bf16[8,24,768]{2,1,0:T(8,128)(2,1)}), bf16[8,24,768]{2,1,0:T(8,128)(2,1)S(1)}, u32[]{:S(2)}, u32[]{:S(2)}) %all-to-all-start) | async-done | bytes 294944 | tf_op jit(solution)/shard_map/all_to_all | solution.py:203
  53.9 1.9 %collective-permute-start.6 = (bf16[500,640]{1,0:T(8,128)(2,1)S(1)}, bf16[500,640]{1,0:T(8,128)(2,1)}, u32[]{:S(2)}, u32[]{:S(2)}) collective-permute-start(bf16[500,640]{1,0:T(8,128)(2,1)S(1)} %collective-permute-done.4.rest_4_), channel_id=1, source_target_pairs={{0,64},{4,452},{64,128},{68,4},{128,192},{132,68},{192,256},{196,1... | collective-permute-start | bytes 1920008 | tf_op jit(solution)/shard_map/ppermute | solution.py:221
  57.1 0.8 broadcast_in_dim.7
  57.9 4.1 %all-to-all-start.1 = ((bf16[4,72,640]{2,1,0:T(8,128)(2,1)}), bf16[4,72,640]{2,1,0:T(8,128)(2,1)}, u32[]{:S(2)}, u32[]{:S(2)}) async-start(bf16[4,72,640]{2,1,0:T(8,128)(2,1)} %broadcast_in_dim.7), calls=%async_computation.1 | async-start | bytes 737280 | tf_op jit(solution)/shard_map/all_to_all | solution.py:203
  62.2 0.8 slice_convert_fusion.2
  63.0 1.9 %collective-permute-start.7 = (bf16[500,640]{1,0:T(8,128)(2,1)S(1)}, bf16[500,640]{1,0:T(8,128)(2,1)}, u32[]{:S(2)}, u32[]{:S(2)}) collective-permute-start(bf16[500,640]{1,0:T(8,128)(2,1)S(1)} %collective-permute-done.5.rest_5_), channel_id=1, source_target_pairs={{0,64},{4,452},{64,128},{68,4},{128,192},{132,68},{192,256},{196,1... | collective-permute-start | bytes 1920008 | tf_op jit(solution)/shard_map/ppermute | solution.py:223
  65.0 5.4 %all-to-all-done.1 = bf16[4,72,640]{2,1,0:T(8,128)(2,1)} async-done(((bf16[4,72,640]{2,1,0:T(8,128)(2,1)}), bf16[4,72,640]{2,1,0:T(8,128)(2,1)}, u32[]{:S(2)}, u32[]{:S(2)}) %all-to-all-start.1) | async-done | bytes 368672 | tf_op jit(solution)/shard_map/all_to_all | solution.py:203
  70.3 2.7 %all-gather = bf16[8,72,640]{2,1,0:T(8,128)(2,1)S(1)} all-gather(bf16[4,72,640]{2,1,0:T(8,128)(2,1)} %all-to-all-done.1), channel_id=2, replica_groups=mesh['z'=8,'y'=8,'c'=2,'x'=4] {'c'}, dimensions={0}, use_global_device_ids=true | all-gather | bytes 1105920 | tf_op jit(solution)/shard_map/all_gather | solution.py:263
  74.1 2.5 %logits_early.1 = (f32[500,72]{1,0:T(8,128)S(1)}, f32[500,72]{1,0:T(8,128)S(1)}) custom-call(s32[10]{0:T(128)S(1)} %stack.43.meta_ref, bf16[2,4,72,640]{3,2,1,0:T(8,128)(2,1)S(1)} %fusion.2.normed_ref, bf16[500,640]{1,0:T(8,128)(2,1)S(1)} %bitcast.39, bf16[500,640]{1,0:T(8,128)(2,1)S(1)} %collective-permute-done.rest_1_, ...), custom_call_target="tpu_custom_call" | custom-call | flops 322560000 | bytes 4480000 | tf_op jit(solution)/shard_map/logits_early/pallas_call | solution.py:115
  76.6 2.3 %collective-permute-start.8 = (f32[500,72]{1,0:T(8,128)S(1)}, f32[500,72]{1,0:T(8,128)S(1)}, u32[]{:S(2)}, u32[]{:S(2)}) collective-permute-start(f32[500,72]{1,0:T(8,128)S(1)} %get-tuple-element.16.other_ref), channel_id=1, source_target_pairs={{0,4},{4,0},{1,5},{5,1},{2,6},{6,2},{3,7},{7,3},{8,12},{12,8},{9,1... | collective-permute-start | bytes 432008 | tf_op jit(solution)/shard_map/ppermute | solution.py:207
  78.9 1.4 %logits_far.1.mine_ref = f32[500,72]{1,0:T(8,128)S(1)} custom-call(s32[10]{0:T(128)S(1)} %stack.43.meta_ref, bf16[2,4,72,640]{3,2,1,0:T(8,128)(2,1)S(1)} %fusion.2.normed_ref, f32[500,72]{1,0:T(8,128)S(1)} %get-tuple-element.15.begun_ref, bf16[500,640]{1,0:T(8,128)(2,1)} %collective-permute-done.7.far_ref.rest_7_), custom_call_target="tpu_custom_call" | custom-call | tf_op jit(solution)/shard_map/logits_far/pallas_call | solution.py:131
  80.3 2.0 %collective-permute-start.9 = (f32[500,72]{1,0:T(8,128)S(1)}, f32[500,72]{1,0:T(8,128)S(1)}, u32[]{:S(2)}, u32[]{:S(2)}) collective-permute-start(f32[500,72]{1,0:T(8,128)S(1)} %logits_far.1.mine_ref), channel_id=1, source_target_pairs={{0,4},{4,0},{1,5},{5,1},{2,6},{6,2},{3,7},{7,3},{8,12},{12,8},{9,1... | collective-permute-start | bytes 432008 | tf_op jit(solution)/shard_map/ppermute | solution.py:207
  82.4 1.3 collective-permute-done.9.rest_ref
  83.7 0.9 logits.1
  84.6 11.8 %all_to_all.25.stats_ref = f32[32,4,72]{2,1,0:T(4,128)S(1)} all-to-all(f32[32,4,72]{2,1,0:T(4,128)S(1)} %broadcast_in_dim.8), channel_id=1, replica_groups=mesh['z'=8,'y'=8,'c'=2,'x'=4] {'y','x'}, dimensions={0} | all-to-all | bytes 73728 | tf_op jit(solution)/shard_map/all_to_all | solution.py:203
  96.4 2.5 %back.1 = (bf16[8,72,640]{2,1,0:T(8,128)(2,1)S(1)}, f32[1,72]{1,0:T(1,128)S(1)}, f32[2,1]{1,0:T(2,128)S(1)}) custom-call(s32[10]{0:T(128)S(1)} %stack.43.meta_ref, f32[32,4,72]{2,1,0:T(4,128)S(1)} %all_to_all.25.stats_ref, f32[2,500,72]{2,1,0:T(8,128)S(1)} %get-tuple-element.18.logits_ref, s32[1,72]{1,0:T(1,128)S(1)} %get-tuple-element.35.label_ref, ...), custom_call_target="tpu_custom_call" | custom-call | tf_op jit(solution)/shard_map/back/pallas_call | solution.py:187
  98.9 0.9 copy-done.1
  99.7 5.2 %all-to-all-start.3 = ((bf16[8,72,640]{2,1,0:T(8,128)(2,1)}), bf16[8,72,640]{2,1,0:T(8,128)(2,1)S(1)}, u32[]{:S(2)}, u32[]{:S(2)}) async-start(bf16[8,72,640]{2,1,0:T(8,128)(2,1)} %copy-done.1), calls=%async_computation.3 | async-start | bytes 1474560 | tf_op jit(solution)/shard_map/all_to_all | solution.py:278
  105.4 11.4 %all-to-all-done.3 = bf16[8,72,640]{2,1,0:T(8,128)(2,1)S(1)} async-done(((bf16[8,72,640]{2,1,0:T(8,128)(2,1)}), bf16[8,72,640]{2,1,0:T(8,128)(2,1)S(1)}, u32[]{:S(2)}, u32[]{:S(2)}) %all-to-all-start.3) | async-done | bytes 737312 | tf_op jit(solution)/shard_map/all_to_all | solution.py:278
  116.9 1.0 convolution_convert_fusion
  117.8 4.2 %all-to-all-start.4 = ((bf16[16,16,640]{2,1,0:T(8,128)(2,1)}), bf16[16,16,640]{2,1,0:T(8,128)(2,1)S(1)}, u32[]{:S(2)}, u32[]{:S(2)}) async-start(bf16[16,16,640]{2,1,0:T(8,128)(2,1)} %bitcast.19), calls=%async_computation.4 | async-start | bytes 655360 | tf_op jit(solution)/shard_map/all_to_all | solution.py:282
  123.1 12.0 %all-to-all-done.4 = bf16[16,16,640]{2,1,0:T(8,128)(2,1)S(1)} async-done(((bf16[16,16,640]{2,1,0:T(8,128)(2,1)}), bf16[16,16,640]{2,1,0:T(8,128)(2,1)S(1)}, u32[]{:S(2)}, u32[]{:S(2)}) %all-to-all-start.4) | async-done | bytes 327712 | tf_op jit(solution)/shard_map/all_to_all | solution.py:282
  (54 shorter events, 6.2 us)
Async XLA Ops:
  0.6 14.1 %collective-permute-start.1 = (bf16[500,640]{1,0:T(8,128)(2,1)}, bf16[500,640]{1,0:T(8,128)(2,1)S(1)}, u32[]{:S(2)}, u32[]{:S(2)}) collective-permute-start(bf16[500,640]{1,0:T(8,128)(2,1)} %bitcast.37), channel_id=1, source_target_pairs={{0,4},{4,0},{1,5},{5,1},{2,6},{6,2},{3,7},{7,3},{8,12},{12,8},{9,1... | collective-permute-start | bytes 1920008 | tf_op jit(solution)/shard_map/ppermute | solution.py:207
  9.4 13.0 %collective-permute-start = (bf16[500,640]{1,0:T(8,128)(2,1)}, bf16[500,640]{1,0:T(8,128)(2,1)S(1)}, u32[]{:S(2)}, u32[]{:S(2)}) collective-permute-start(bf16[500,640]{1,0:T(8,128)(2,1)} %bitcast.38), channel_id=1, source_target_pairs={{0,64},{4,452},{64,128},{68,4},{128,192},{132,68},{192,256},{196,1... | collective-permute-start | bytes 1920008 | tf_op jit(solution)/shard_map/ppermute | solution.py:220
  14.7 14.5 %collective-permute-start.2 = (bf16[500,640]{1,0:T(8,128)(2,1)S(1)}, bf16[500,640]{1,0:T(8,128)(2,1)S(1)}, u32[]{:S(2)}, u32[]{:S(2)}) collective-permute-start(bf16[500,640]{1,0:T(8,128)(2,1)S(1)} %collective-permute-done.1), channel_id=1, source_target_pairs={{0,64},{4,452},{64,128},{68,4},{128,192},{132,68},{192,256},{196,1... | collective-permute-start | bytes 1920008 | tf_op jit(solution)/shard_map/ppermute | solution.py:221
  22.4 19.6 %collective-permute-start.3 = (bf16[500,640]{1,0:T(8,128)(2,1)S(1)}, bf16[500,640]{1,0:T(8,128)(2,1)S(1)}, u32[]{:S(2)}, u32[]{:S(2)}) collective-permute-start(bf16[500,640]{1,0:T(8,128)(2,1)S(1)} %collective-permute-done.rest_1_), channel_id=1, source_target_pairs={{0,64},{4,452},{64,128},{68,4},{128,192},{132,68},{192,256},{196,1... | collective-permute-start | bytes 1920008 | tf_op jit(solution)/shard_map/ppermute | solution.py:220
  29.3 24.6 %collective-permute-start.4 = (bf16[500,640]{1,0:T(8,128)(2,1)S(1)}, bf16[500,640]{1,0:T(8,128)(2,1)S(1)}, u32[]{:S(2)}, u32[]{:S(2)}) collective-permute-start(bf16[500,640]{1,0:T(8,128)(2,1)S(1)} %collective-permute-done.2.rest_2_), channel_id=1, source_target_pairs={{0,64},{4,452},{64,128},{68,4},{128,192},{132,68},{192,256},{196,1... | collective-permute-start | bytes 1920008 | tf_op jit(solution)/shard_map/ppermute | solution.py:221
  35.0 27.0 %copy-start.4 = (bf16[5120]{0:T(1024)(128)(2,1)S(1)}, bf16[5120]{0:T(1024)(128)(2,1)}, u32[]{:S(2)}) copy-start(bf16[5120]{0:T(1024)(128)(2,1)} %param.6) | copy-start | bytes 30724
  35.0 18.8 %all-to-all-start = ((bf16[8,24,768]{2,1,0:T(8,128)(2,1)}), bf16[8,24,768]{2,1,0:T(8,128)(2,1)S(1)}, u32[]{:S(2)}, u32[]{:S(2)}) async-start(bf16[8,24,768]{2,1,0:T(8,128)(2,1)} %broadcast_in_dim.6), calls=%async_computation | async-start | bytes 589824 | tf_op jit(solution)/shard_map/all_to_all | solution.py:203
  42.0 21.0 %collective-permute-start.5 = (bf16[500,640]{1,0:T(8,128)(2,1)S(1)}, bf16[500,640]{1,0:T(8,128)(2,1)S(1)}, u32[]{:S(2)}, u32[]{:S(2)}) collective-permute-start(bf16[500,640]{1,0:T(8,128)(2,1)S(1)} %collective-permute-done.3.rest_3_), channel_id=1, source_target_pairs={{0,64},{4,452},{64,128},{68,4},{128,192},{132,68},{192,256},{196,1... | collective-permute-start | bytes 1920008 | tf_op jit(solution)/shard_map/ppermute | solution.py:220
  53.9 16.4 %collective-permute-start.6 = (bf16[500,640]{1,0:T(8,128)(2,1)S(1)}, bf16[500,640]{1,0:T(8,128)(2,1)}, u32[]{:S(2)}, u32[]{:S(2)}) collective-permute-start(bf16[500,640]{1,0:T(8,128)(2,1)S(1)} %collective-permute-done.4.rest_4_), channel_id=1, source_target_pairs={{0,64},{4,452},{64,128},{68,4},{128,192},{132,68},{192,256},{196,1... | collective-permute-start | bytes 1920008 | tf_op jit(solution)/shard_map/ppermute | solution.py:221
  56.4 0.7 copy-start.2
  57.9 12.4 %all-to-all-start.1 = ((bf16[4,72,640]{2,1,0:T(8,128)(2,1)}), bf16[4,72,640]{2,1,0:T(8,128)(2,1)}, u32[]{:S(2)}, u32[]{:S(2)}) async-start(bf16[4,72,640]{2,1,0:T(8,128)(2,1)} %broadcast_in_dim.7), calls=%async_computation.1 | async-start | bytes 737280 | tf_op jit(solution)/shard_map/all_to_all | solution.py:203
  63.0 15.8 %collective-permute-start.7 = (bf16[500,640]{1,0:T(8,128)(2,1)S(1)}, bf16[500,640]{1,0:T(8,128)(2,1)}, u32[]{:S(2)}, u32[]{:S(2)}) collective-permute-start(bf16[500,640]{1,0:T(8,128)(2,1)S(1)} %collective-permute-done.5.rest_5_), channel_id=1, source_target_pairs={{0,64},{4,452},{64,128},{68,4},{128,192},{132,68},{192,256},{196,1... | collective-permute-start | bytes 1920008 | tf_op jit(solution)/shard_map/ppermute | solution.py:223
  73.0 1.1 copy-start
  76.6 5.8 %collective-permute-start.8 = (f32[500,72]{1,0:T(8,128)S(1)}, f32[500,72]{1,0:T(8,128)S(1)}, u32[]{:S(2)}, u32[]{:S(2)}) collective-permute-start(f32[500,72]{1,0:T(8,128)S(1)} %get-tuple-element.16.other_ref), channel_id=1, source_target_pairs={{0,4},{4,0},{1,5},{5,1},{2,6},{6,2},{3,7},{7,3},{8,12},{12,8},{9,1... | collective-permute-start | bytes 432008 | tf_op jit(solution)/shard_map/ppermute | solution.py:207
  80.3 3.4 %collective-permute-start.9 = (f32[500,72]{1,0:T(8,128)S(1)}, f32[500,72]{1,0:T(8,128)S(1)}, u32[]{:S(2)}, u32[]{:S(2)}) collective-permute-start(f32[500,72]{1,0:T(8,128)S(1)} %logits_far.1.mine_ref), channel_id=1, source_target_pairs={{0,4},{4,0},{1,5},{5,1},{2,6},{6,2},{3,7},{7,3},{8,12},{12,8},{9,1... | collective-permute-start | bytes 432008 | tf_op jit(solution)/shard_map/ppermute | solution.py:207
  98.9 0.9 copy-start.1
  99.7 17.0 %all-to-all-start.3 = ((bf16[8,72,640]{2,1,0:T(8,128)(2,1)}), bf16[8,72,640]{2,1,0:T(8,128)(2,1)S(1)}, u32[]{:S(2)}, u32[]{:S(2)}) async-start(bf16[8,72,640]{2,1,0:T(8,128)(2,1)} %copy-done.1), calls=%async_computation.3 | async-start | bytes 1474560 | tf_op jit(solution)/shard_map/all_to_all | solution.py:278
  105.0 17.1 %copy-start.3 = (bf16[12,1408]{1,0:T(8,128)(2,1)S(1)}, bf16[12,1408]{1,0:T(8,128)(2,1)}, u32[]{:S(2)}) copy-start(bf16[12,1408]{1,0:T(8,128)(2,1)} %pick.1) | copy-start | bytes 101380
  117.8 17.2 %all-to-all-start.4 = ((bf16[16,16,640]{2,1,0:T(8,128)(2,1)}), bf16[16,16,640]{2,1,0:T(8,128)(2,1)S(1)}, u32[]{:S(2)}, u32[]{:S(2)}) async-start(bf16[16,16,640]{2,1,0:T(8,128)(2,1)} %bitcast.19), calls=%async_computation.4 | async-start | bytes 655360 | tf_op jit(solution)/shard_map/all_to_all | solution.py:282

commit v7 on v6

--- a/solution.py
+++ b/solution.py
@@ -62,6 +62,44 @@
         compiler_params=params(56),
         name="pick",
     )(slots, targets, hidden)
+
+
+def compact_kernel(slots_ref, rows_ref, place_ref, label_ref, layer_ref):
+    total, lanes = slots_ref.shape
+    half = lanes - FACTS
+    facts = slots_ref[:, half:].astype(F32).T
+    flag = facts[0:1, :]
+    below = lax.broadcasted_iota(jnp.int32, (total, total), 0)
+    below = (below < lax.broadcasted_iota(jnp.int32, (total, total), 1)).astype(F32)
+    rank = jnp.dot(flag, below, preferred_element_type=F32)
+    row = lax.broadcasted_iota(jnp.int32, (LIVE, total), 0)
+    place = ((row == rank.astype(jnp.int32)) & (flag > 0)).astype(F32).astype(BF16)
+    place_ref[...] = place
+    rows = jnp.dot(place, slots_ref[:, :half], preferred_element_type=F32).astype(BF16)
+    for i in range(rows_ref.shape[0]):
+        rows_ref[i] = rows
+    known = lax.dot_general(
+        facts[0:8, :].astype(BF16), place, (((1,), (1,)), ((), ())), preferred_element_type=F32
+    ).astype(jnp.int32)
+    label_ref[...] = known[1:2, :] * 256 + known[2:3, :]
+    layer_ref[...] = known[3:4, :]
+
+
+def compact(slots):
+    total, lanes = slots.shape
+    return pl.pallas_call(
+        compact_kernel,
+        in_specs=[VMEM],
+        out_specs=[VMEM] * 4,
+        out_shape=[
+            jax.ShapeDtypeStruct((4, LIVE, lanes - FACTS), BF16),
+            jax.ShapeDtypeStruct((LIVE, total), BF16),
+            jax.ShapeDtypeStruct((1, LIVE), jnp.int32),
+            jax.ShapeDtypeStruct((1, LIVE), jnp.int32),
+        ],
+        compiler_params=params(),
+        name="compact",
+    )(slots)
 
 
 def scores(shard, normed_ref, head):
@@ -211,16 +249,19 @@
     return lax.optimization_barrier((values, *others))[0]
 
 
-def ring(own):
-    onward = [(2 * i + c, 2 * ((i + 1 - 2 * c) % 8) + c) for i in range(8) for c in range(2)]
-    mine = own
-    other = swapped = swap_core(own)
-    near = [own]
-    for _ in range(RING):
-        mine = lax.ppermute(mine, ("z", "c"), onward)
-        other = lax.ppermute(other, ("z", "c"), onward)
+def onward(values):
+    pairs = [(2 * i + c, 2 * ((i + 1 - 2 * c) % 8) + c) for i in range(8) for c in range(2)]
+    return lax.ppermute(values, ("z", "c"), pairs)
+
+
+def ring(own, swapped, first):
+    mine, other = onward(own), onward(swapped)
+    near = [own, mine, other]
+    mine = after(mine, first)
+    for _ in range(RING - 1):
+        mine, other = onward(mine), onward(other)
         near += [mine, other]
-    return swapped, [*near, lax.ppermute(mine, ("z", "c"), onward)]
+    return [*near, onward(mine)]
 
 
 def body(hidden, gain, head, exit_slots, targets):
@@ -235,30 +276,20 @@
     first_other = ((y * 2 + 1 - c) * 4 + x) * SPAN
     absent = [lax.rem(z + 8 - (2 * c - 1) * s, 8) for s in range(1, RING + 1)]
     meta = jnp.stack([first, first_other, *shards, *absent]).astype(jnp.int32)
-    swapped, near = ring(head.T)
-
     packed = pick(exit_slots, targets, hidden)
     picked = packed[:, :part_width]
     pair = lax.all_gather(packed, "c", axis=0, tiled=True)
+    near = ring(head.T, swap_core(head.T), pair)
     pair_half = lax.dynamic_slice_in_dim(pair, c * half, half, 1)
     slots = jnp.concatenate([pair_half, pair[:, part_width:]], axis=1)
     slots = after(slots, near[1], near[2])
     slots = spread(slots, "y", 8).reshape(16 * own, half + 128)
 
     slots = after(slots, near[3], near[4])
-    total = slots.shape[0]
-    flag = slots[:, half].astype(F32)
-    below = (jnp.arange(total)[:, None] < jnp.arange(total)[None, :]).astype(F32)
-    rank = jnp.sum(below * flag[:, None], axis=0)
-    place = (rank[None, :] == jnp.arange(LIVE, dtype=F32)[:, None]) & (flag > 0)[None, :]
-    place = place.astype(BF16)
+    rows, place, label_row, layer_row = compact(slots)
     place_out = jnp.pad(place.reshape(LIVE, 16, own), ((0, 0), (0, 0), (0, 16 - own)))
     place_out = place_out.reshape(LIVE, 256)
-    compact = jnp.dot(place, slots, preferred_element_type=F32)
-    fact = compact[:, half : half + 4].astype(jnp.int32).T
-    label_row = (fact[1] * 256 + fact[2]).reshape(1, LIVE)
-    layer_row = fact[3].reshape(1, LIVE)
-    rows = spread(compact[:, :half].astype(BF16), "x", 4)
+    rows = lax.all_to_all(rows, "x", 0, 0, tiled=True)
     rows = after(rows, near[5], near[6])
     rows = lax.all_gather(rows, "c", axis=0)
 

time: 137 us -> 136 us (level)
  waiting for transfers between devices: 42.5 us -> 39.7 us
  starting transfers between devices: 56.8 us -> 58.9 us
  blocking collectives: 16.5 us -> 18 us
  other arithmetic: 2.28 us -> 0.89 us
    all_to_all x2 -> x1, waiting for transfers between devices: 15.2 us -> 5.59 us  [spread(): return lax.all_to_all(copies, axes, 0, 0, tiled=True)]
    all_to_all x0 -> x1, waiting for transfers between devices: none -> 6.23 us  [body(): rows = lax.all_to_all(rows, 'x', 0, 0, tiled=True)]
    all_to_all x2 -> x1, starting transfers between devices: 11.1 us -> 6.82 us  [spread(): return lax.all_to_all(copies, axes, 0, 0, tiled=True)]
    all_to_all x0 -> x1, starting transfers between devices: none -> 4.12 us  [body(): rows = lax.all_to_all(rows, 'x', 0, 0, tiled=True)]
    ppermute x7, starting transfers between devices: 23.2 us -> 25.5 us  [onward(): return lax.ppermute(values, ('z', 'c'), pairs)]
    all_to_all x1, blocking collectives: 11.8 us -> 13.2 us  [spread(): return lax.all_to_all(copies, axes, 0, 0, tiled=True)]
    unnamed x14 -> x17, local copies, waits for them, and re-layouts: 3.42 us -> 4.02 us
  transfers between devices with their start and end apart: 14 -> 14, of which waited for: 7 -> 7; matrix products, arithmetic and copies ran while one was open for 4% -> 2% of each run, Pallas kernels for 5% -> 4%
where the time goes in v7:
time: 136 us; the launch traced here: 135 us
  starting transfers between devices  58.9 us (43%)
  waiting for transfers between devices  39.7 us (29%)
  blocking collectives  18 us (13%)
  Pallas kernels  10.2 us (7%)
  local copies, waits for them, and re-layouts  5.21 us (4%)
    ppermute x7, starting transfers between devices, onward(): return lax.ppermute(values, ('z', 'c'), pairs)  25.5 us
    all_to_all x1, blocking collectives, spread(): return lax.all_to_all(copies, axes, 0, 0, tiled=True)  13.2 us
    ppermute x3, starting transfers between devices, swap_core(): return lax.ppermute(values, 'c', [(0, 1), (1, 0)])  13.1 us
    all_to_all x1, waiting for transfers between devices, body(): back = lax.all_to_all(sent, ('y', 'c'), 0, 0, tiled=True)  12.3 us
    all_to_all x1, waiting for transfers between devices, body(): part = lax.all_to_all(part, ('x', 'c'), 0, 0, tiled=True)  11.5 us
    all_to_all x1, starting transfers between devices, spread(): return lax.all_to_all(copies, axes, 0, 0, tiled=True)  6.82 us
    all_to_all x1, waiting for transfers between devices, body(): rows = lax.all_to_all(rows, 'x', 0, 0, tiled=True)  6.23 us
    all_to_all x1, waiting for transfers between devices, spread(): return lax.all_to_all(copies, axes, 0, 0, tiled=True)  5.59 us
  transfers between devices with their start and end apart: 14, of which 7 were waited for; matrix products, arithmetic and copies ran while one was open for 2% of the time, Pallas kernels for 4%

profile of v7, /device:TPU:1, one launch (start us, length us, event | category | flops | bytes accessed | tf_op | source)
XLA Modules:
  0.0 134.7 jit_solution(4228711825511758781)
XLA Ops:
  0.6 8.8 %collective-permute-start.1 = (bf16[500,640]{1,0:T(8,128)(2,1)}, bf16[500,640]{1,0:T(8,128)(2,1)S(1)}, u32[]{:S(2)}, u32[]{:S(2)}) collective-permute-start(bf16[500,640]{1,0:T(8,128)(2,1)} %bitcast.37), channel_id=1, source_target_pairs={{0,4},{4,0},{1,5},{5,1},{2,6},{6,2},{3,7},{7,3},{8,12},{12,8},{9,1... | collective-permute-start | bytes 1920008 | tf_op jit(solution)/shard_map/ppermute | solution.py:245
  9.4 5.3 %collective-permute-start = (bf16[500,640]{1,0:T(8,128)(2,1)}, bf16[500,640]{1,0:T(8,128)(2,1)S(1)}, u32[]{:S(2)}, u32[]{:S(2)}) collective-permute-start(bf16[500,640]{1,0:T(8,128)(2,1)} %bitcast.38), channel_id=1, source_target_pairs={{0,64},{4,452},{64,128},{68,4},{128,192},{132,68},{192,256},{196,1... | collective-permute-start | bytes 1920008 | tf_op jit(solution)/shard_map/ppermute | solution.py:254
  14.7 2.2 %collective-permute-start.2 = (bf16[500,640]{1,0:T(8,128)(2,1)S(1)}, bf16[500,640]{1,0:T(8,128)(2,1)S(1)}, u32[]{:S(2)}, u32[]{:S(2)}) collective-permute-start(bf16[500,640]{1,0:T(8,128)(2,1)S(1)} %collective-permute-done.1), channel_id=1, source_target_pairs={{0,64},{4,452},{64,128},{68,4},{128,192},{132,68},{192,256},{196,1... | collective-permute-start | bytes 1920008 | tf_op jit(solution)/shard_map/ppermute | solution.py:254
  16.9 2.6 %pick.1 = bf16[12,1408]{1,0:T(8,128)(2,1)} custom-call(s32[2,6]{1,0:T(2,128)} %slots_ref.1, s32[256]{0:T(256)} %targets_ref.1, bf16[2,256,1280]{2,1,0:T(8,128)(2,1)} %hidden_ref.1), custom_call_target="tpu_custom_call" | custom-call | tf_op jit(solution)/shard_map/pick/pallas_call | solution.py:52
  19.5 2.1 %all-gather.1 = bf16[2,12,1408]{2,1,0:T(8,128)(2,1)S(1)} all-gather(bf16[1,12,1408]{2,1,0:T(8,128)(2,1)} %bitcast.44), channel_id=1, replica_groups=mesh['z'=8,'y'=8,'c'=2,'x'=4] {'c'}, dimensions={0}, use_global_device_ids=true | all-gather | bytes 101376 | tf_op jit(solution)/shard_map/all_gather | solution.py:281
  21.6 0.8 collective-permute-done.rest_1_
  22.4 4.9 %collective-permute-start.3 = (bf16[500,640]{1,0:T(8,128)(2,1)S(1)}, bf16[500,640]{1,0:T(8,128)(2,1)S(1)}, u32[]{:S(2)}, u32[]{:S(2)}) collective-permute-start(bf16[500,640]{1,0:T(8,128)(2,1)S(1)} %collective-permute-done.rest_1_), channel_id=1, source_target_pairs={{0,64},{4,452},{64,128},{68,4},{128,192},{132,68},{192,256},{196,1... | collective-permute-start | bytes 1920008 | tf_op jit(solution)/shard_map/ppermute | solution.py:254
  27.4 1.9 %collective-permute-done.2.rest_2_ = bf16[500,640]{1,0:T(8,128)(2,1)S(1)} collective-permute-done((bf16[500,640]{1,0:T(8,128)(2,1)S(1)}, bf16[500,640]{1,0:T(8,128)(2,1)S(1)}, u32[]{:S(2)}, u32[]{:S(2)}) %collective-permute-start.2) | collective-permute-done | bytes 640032 | tf_op jit(solution)/shard_map/ppermute | solution.py:254
  29.3 5.0 %collective-permute-start.4 = (bf16[500,640]{1,0:T(8,128)(2,1)S(1)}, bf16[500,640]{1,0:T(8,128)(2,1)S(1)}, u32[]{:S(2)}, u32[]{:S(2)}) collective-permute-start(bf16[500,640]{1,0:T(8,128)(2,1)S(1)} %collective-permute-done.2.rest_2_), channel_id=1, source_target_pairs={{0,64},{4,452},{64,128},{68,4},{128,192},{132,68},{192,256},{196,1... | collective-permute-start | bytes 1920008 | tf_op jit(solution)/shard_map/ppermute | solution.py:254
  34.3 0.7 broadcast_in_dim.4
  35.1 6.8 %all-to-all-start = ((bf16[8,24,768]{2,1,0:T(8,128)(2,1)}), bf16[8,24,768]{2,1,0:T(8,128)(2,1)S(1)}, u32[]{:S(2)}, u32[]{:S(2)}) async-start(bf16[8,24,768]{2,1,0:T(8,128)(2,1)} %broadcast_in_dim.4), calls=%async_computation | async-start | bytes 589824 | tf_op jit(solution)/shard_map/all_to_all | solution.py:241
  41.9 1.9 %collective-permute-start.5 = (bf16[500,640]{1,0:T(8,128)(2,1)S(1)}, bf16[500,640]{1,0:T(8,128)(2,1)S(1)}, u32[]{:S(2)}, u32[]{:S(2)}) collective-permute-start(bf16[500,640]{1,0:T(8,128)(2,1)S(1)} %collective-permute-done.3.rest_3_), channel_id=1, source_target_pairs={{0,64},{4,452},{64,128},{68,4},{128,192},{132,68},{192,256},{196,1... | collective-permute-start | bytes 1920008 | tf_op jit(solution)/shard_map/ppermute | solution.py:254
  43.8 4.3 %collective-permute-start.6 = (bf16[500,640]{1,0:T(8,128)(2,1)S(1)}, bf16[500,640]{1,0:T(8,128)(2,1)}, u32[]{:S(2)}, u32[]{:S(2)}) collective-permute-start(bf16[500,640]{1,0:T(8,128)(2,1)S(1)} %collective-permute-done.4.rest_4_), channel_id=1, source_target_pairs={{0,64},{4,452},{64,128},{68,4},{128,192},{132,68},{192,256},{196,1... | collective-permute-start | bytes 1920008 | tf_op jit(solution)/shard_map/ppermute | solution.py:254
  48.1 5.6 %all-to-all-done = bf16[8,24,768]{2,1,0:T(8,128)(2,1)S(1)} async-done(((bf16[8,24,768]{2,1,0:T(8,128)(2,1)}), bf16[8,24,768]{2,1,0:T(8,128)(2,1)S(1)}, u32[]{:S(2)}, u32[]{:S(2)}) %all-to-all-start) | async-done | bytes 294944 | tf_op jit(solution)/shard_map/all_to_all | solution.py:241
  55.4 4.1 %all-to-all-start.1 = ((bf16[4,72,640]{2,1,0:T(8,128)(2,1)}), bf16[4,72,640]{2,1,0:T(8,128)(2,1)}, u32[]{:S(2)}, u32[]{:S(2)}) async-start(bf16[4,72,640]{2,1,0:T(8,128)(2,1)} %copy-done.2), calls=%async_computation.1 | async-start | bytes 737280 | tf_op jit(solution)/shard_map/all_to_all | solution.py:292
  59.7 1.9 %collective-permute-start.7 = (bf16[500,640]{1,0:T(8,128)(2,1)S(1)}, bf16[500,640]{1,0:T(8,128)(2,1)}, u32[]{:S(2)}, u32[]{:S(2)}) collective-permute-start(bf16[500,640]{1,0:T(8,128)(2,1)S(1)} %collective-permute-done.5.rest_5_), channel_id=1, source_target_pairs={{0,64},{4,452},{64,128},{68,4},{128,192},{132,68},{192,256},{196,1... | collective-permute-start | bytes 1920008 | tf_op jit(solution)/shard_map/ppermute | solution.py:254
  61.6 6.2 %all-to-all-done.1 = bf16[4,72,640]{2,1,0:T(8,128)(2,1)} async-done(((bf16[4,72,640]{2,1,0:T(8,128)(2,1)}), bf16[4,72,640]{2,1,0:T(8,128)(2,1)}, u32[]{:S(2)}, u32[]{:S(2)}) %all-to-all-start.1) | async-done | bytes 368672 | tf_op jit(solution)/shard_map/all_to_all | solution.py:292
  67.8 2.6 %all-gather = bf16[8,72,640]{2,1,0:T(8,128)(2,1)S(1)} all-gather(bf16[4,72,640]{2,1,0:T(8,128)(2,1)} %all-to-all-done.1), channel_id=2, replica_groups=mesh['z'=8,'y'=8,'c'=2,'x'=4] {'c'}, dimensions={0}, use_global_device_ids=true | all-gather | bytes 1105920 | tf_op jit(solution)/shard_map/all_gather | solution.py:294
  71.6 2.5 %logits_early.1 = (f32[500,72]{1,0:T(8,128)S(1)}, f32[500,72]{1,0:T(8,128)S(1)}) custom-call(s32[10]{0:T(128)S(1)} %stack.43.meta_ref, bf16[2,4,72,640]{3,2,1,0:T(8,128)(2,1)S(1)} %fusion.2.normed_ref, bf16[500,640]{1,0:T(8,128)(2,1)S(1)} %bitcast.39, bf16[500,640]{1,0:T(8,128)(2,1)S(1)} %collective-permute-done.rest_1_, ...), custom_call_target="tpu_custom_call" | custom-call | flops 322560000 | bytes 4480000 | tf_op jit(solution)/shard_map/logits_early/pallas_call | solution.py:153
  74.0 1.4 %logits_far.1.mine_ref = f32[500,72]{1,0:T(8,128)S(1)} custom-call(s32[10]{0:T(128)S(1)} %stack.43.meta_ref, bf16[2,4,72,640]{3,2,1,0:T(8,128)(2,1)S(1)} %fusion.2.normed_ref, f32[500,72]{1,0:T(8,128)S(1)} %get-tuple-element.24.begun_ref, bf16[500,640]{1,0:T(8,128)(2,1)} %collective-permute-done.7.far_ref.rest_7_), custom_call_target="tpu_custom_call" | custom-call | tf_op jit(solution)/shard_map/logits_far/pallas_call | solution.py:169
  75.5 2.3 %collective-permute-start.9 = (f32[500,72]{1,0:T(8,128)S(1)}, f32[500,72]{1,0:T(8,128)S(1)}, u32[]{:S(2)}, u32[]{:S(2)}) collective-permute-start(f32[500,72]{1,0:T(8,128)S(1)} %logits_far.1.mine_ref), channel_id=1, source_target_pairs={{0,4},{4,0},{1,5},{5,1},{2,6},{6,2},{3,7},{7,3},{8,12},{12,8},{9,1... | collective-permute-start | bytes 432008 | tf_op jit(solution)/shard_map/ppermute | solution.py:245
  77.8 2.0 %collective-permute-start.8 = (f32[500,72]{1,0:T(8,128)S(1)}, f32[500,72]{1,0:T(8,128)S(1)}, u32[]{:S(2)}, u32[]{:S(2)}) collective-permute-start(f32[500,72]{1,0:T(8,128)S(1)} %get-tuple-element.25.other_ref), channel_id=1, source_target_pairs={{0,4},{4,0},{1,5},{5,1},{2,6},{6,2},{3,7},{7,3},{8,12},{12,8},{9,1... | collective-permute-start | bytes 432008 | tf_op jit(solution)/shard_map/ppermute | solution.py:245
  79.8 1.4 %collective-permute-done.8.more_ref = f32[500,72]{1,0:T(8,128)S(1)} collective-permute-done((f32[500,72]{1,0:T(8,128)S(1)}, f32[500,72]{1,0:T(8,128)S(1)}, u32[]{:S(2)}, u32[]{:S(2)}) %collective-permute-start.8) | collective-permute-done | bytes 144032 | tf_op jit(solution)/shard_map/ppermute | solution.py:245
  81.2 0.9 logits.1
  82.1 13.2 %all_to_all.25.stats_ref = f32[32,4,72]{2,1,0:T(4,128)S(1)} all-to-all(f32[32,4,72]{2,1,0:T(4,128)S(1)} %broadcast_in_dim.5), channel_id=1, replica_groups=mesh['z'=8,'y'=8,'c'=2,'x'=4] {'y','x'}, dimensions={0} | all-to-all | bytes 73728 | tf_op jit(solution)/shard_map/all_to_all | solution.py:241
  95.3 2.5 %back.1 = (bf16[8,72,640]{2,1,0:T(8,128)(2,1)S(1)}, f32[1,72]{1,0:T(1,128)S(1)}, f32[2,1]{1,0:T(2,128)S(1)}) custom-call(s32[10]{0:T(128)S(1)} %stack.43.meta_ref, f32[32,4,72]{2,1,0:T(4,128)S(1)} %all_to_all.25.stats_ref, f32[2,500,72]{2,1,0:T(8,128)S(1)} %get-tuple-element.27.logits_ref, s32[1,72]{1,0:T(1,128)S(1)} %get-tuple-element.23.label_ref, ...), custom_call_target="tpu_custom_call" | custom-call | tf_op jit(solution)/shard_map/back/pallas_call | solution.py:225
  97.8 0.9 copy-done.1
  98.7 5.1 %all-to-all-start.3 = ((bf16[8,72,640]{2,1,0:T(8,128)(2,1)}), bf16[8,72,640]{2,1,0:T(8,128)(2,1)S(1)}, u32[]{:S(2)}, u32[]{:S(2)}) async-start(bf16[8,72,640]{2,1,0:T(8,128)(2,1)} %copy-done.1), calls=%async_computation.3 | async-start | bytes 1474560 | tf_op jit(solution)/shard_map/all_to_all | solution.py:309
  104.1 11.5 %all-to-all-done.3 = bf16[8,72,640]{2,1,0:T(8,128)(2,1)S(1)} async-done(((bf16[8,72,640]{2,1,0:T(8,128)(2,1)}), bf16[8,72,640]{2,1,0:T(8,128)(2,1)S(1)}, u32[]{:S(2)}, u32[]{:S(2)}) %all-to-all-start.3) | async-done | bytes 737312 | tf_op jit(solution)/shard_map/all_to_all | solution.py:309
  115.7 0.9 convolution_convert_fusion
  116.6 4.2 %all-to-all-start.4 = ((bf16[16,16,640]{2,1,0:T(8,128)(2,1)}), bf16[16,16,640]{2,1,0:T(8,128)(2,1)S(1)}, u32[]{:S(2)}, u32[]{:S(2)}) async-start(bf16[16,16,640]{2,1,0:T(8,128)(2,1)} %bitcast.18), calls=%async_computation.4 | async-start | bytes 655360 | tf_op jit(solution)/shard_map/all_to_all | solution.py:313
  121.6 12.3 %all-to-all-done.4 = bf16[16,16,640]{2,1,0:T(8,128)(2,1)S(1)} async-done(((bf16[16,16,640]{2,1,0:T(8,128)(2,1)}), bf16[16,16,640]{2,1,0:T(8,128)(2,1)S(1)}, u32[]{:S(2)}, u32[]{:S(2)}) %all-to-all-start.4) | async-done | bytes 327712 | tf_op jit(solution)/shard_map/all_to_all | solution.py:313
  (48 shorter events, 4.9 us)
Async XLA Ops:
  0.6 14.1 %collective-permute-start.1 = (bf16[500,640]{1,0:T(8,128)(2,1)}, bf16[500,640]{1,0:T(8,128)(2,1)S(1)}, u32[]{:S(2)}, u32[]{:S(2)}) collective-permute-start(bf16[500,640]{1,0:T(8,128)(2,1)} %bitcast.37), channel_id=1, source_target_pairs={{0,4},{4,0},{1,5},{5,1},{2,6},{6,2},{3,7},{7,3},{8,12},{12,8},{9,1... | collective-permute-start | bytes 1920008 | tf_op jit(solution)/shard_map/ppermute | solution.py:245
  9.4 13.0 %collective-permute-start = (bf16[500,640]{1,0:T(8,128)(2,1)}, bf16[500,640]{1,0:T(8,128)(2,1)S(1)}, u32[]{:S(2)}, u32[]{:S(2)}) collective-permute-start(bf16[500,640]{1,0:T(8,128)(2,1)} %bitcast.38), channel_id=1, source_target_pairs={{0,64},{4,452},{64,128},{68,4},{128,192},{132,68},{192,256},{196,1... | collective-permute-start | bytes 1920008 | tf_op jit(solution)/shard_map/ppermute | solution.py:254
  14.7 14.5 %collective-permute-start.2 = (bf16[500,640]{1,0:T(8,128)(2,1)S(1)}, bf16[500,640]{1,0:T(8,128)(2,1)S(1)}, u32[]{:S(2)}, u32[]{:S(2)}) collective-permute-start(bf16[500,640]{1,0:T(8,128)(2,1)S(1)} %collective-permute-done.1), channel_id=1, source_target_pairs={{0,64},{4,452},{64,128},{68,4},{128,192},{132,68},{192,256},{196,1... | collective-permute-start | bytes 1920008 | tf_op jit(solution)/shard_map/ppermute | solution.py:254
  19.5 40.0 %copy-start.6 = (bf16[5120]{0:T(1024)(128)(2,1)S(1)}, bf16[5120]{0:T(1024)(128)(2,1)}, u32[]{:S(2)}) copy-start(bf16[5120]{0:T(1024)(128)(2,1)} %param.6) | copy-start | bytes 30724
  22.4 19.4 %collective-permute-start.3 = (bf16[500,640]{1,0:T(8,128)(2,1)S(1)}, bf16[500,640]{1,0:T(8,128)(2,1)S(1)}, u32[]{:S(2)}, u32[]{:S(2)}) collective-permute-start(bf16[500,640]{1,0:T(8,128)(2,1)S(1)} %collective-permute-done.rest_1_), channel_id=1, source_target_pairs={{0,64},{4,452},{64,128},{68,4},{128,192},{132,68},{192,256},{196,1... | collective-permute-start | bytes 1920008 | tf_op jit(solution)/shard_map/ppermute | solution.py:254
  29.3 14.6 %collective-permute-start.4 = (bf16[500,640]{1,0:T(8,128)(2,1)S(1)}, bf16[500,640]{1,0:T(8,128)(2,1)S(1)}, u32[]{:S(2)}, u32[]{:S(2)}) collective-permute-start(bf16[500,640]{1,0:T(8,128)(2,1)S(1)} %collective-permute-done.2.rest_2_), channel_id=1, source_target_pairs={{0,64},{4,452},{64,128},{68,4},{128,192},{132,68},{192,256},{196,1... | collective-permute-start | bytes 1920008 | tf_op jit(solution)/shard_map/ppermute | solution.py:254
  35.1 18.6 %all-to-all-start = ((bf16[8,24,768]{2,1,0:T(8,128)(2,1)}), bf16[8,24,768]{2,1,0:T(8,128)(2,1)S(1)}, u32[]{:S(2)}, u32[]{:S(2)}) async-start(bf16[8,24,768]{2,1,0:T(8,128)(2,1)} %broadcast_in_dim.4), calls=%async_computation | async-start | bytes 589824 | tf_op jit(solution)/shard_map/all_to_all | solution.py:241
  41.9 17.8 %collective-permute-start.5 = (bf16[500,640]{1,0:T(8,128)(2,1)S(1)}, bf16[500,640]{1,0:T(8,128)(2,1)S(1)}, u32[]{:S(2)}, u32[]{:S(2)}) collective-permute-start(bf16[500,640]{1,0:T(8,128)(2,1)S(1)} %collective-permute-done.3.rest_3_), channel_id=1, source_target_pairs={{0,64},{4,452},{64,128},{68,4},{128,192},{132,68},{192,256},{196,1... | collective-permute-start | bytes 1920008 | tf_op jit(solution)/shard_map/ppermute | solution.py:254
  43.8 24.0 %collective-permute-start.6 = (bf16[500,640]{1,0:T(8,128)(2,1)S(1)}, bf16[500,640]{1,0:T(8,128)(2,1)}, u32[]{:S(2)}, u32[]{:S(2)}) collective-permute-start(bf16[500,640]{1,0:T(8,128)(2,1)S(1)} %collective-permute-done.4.rest_4_), channel_id=1, source_target_pairs={{0,64},{4,452},{64,128},{68,4},{128,192},{132,68},{192,256},{196,1... | collective-permute-start | bytes 1920008 | tf_op jit(solution)/shard_map/ppermute | solution.py:254
  54.0 0.7 copy-start.2
  54.8 0.6 copy-start.3
  55.4 12.5 %all-to-all-start.1 = ((bf16[4,72,640]{2,1,0:T(8,128)(2,1)}), bf16[4,72,640]{2,1,0:T(8,128)(2,1)}, u32[]{:S(2)}, u32[]{:S(2)}) async-start(bf16[4,72,640]{2,1,0:T(8,128)(2,1)} %copy-done.2), calls=%async_computation.1 | async-start | bytes 737280 | tf_op jit(solution)/shard_map/all_to_all | solution.py:292
  59.7 14.4 %collective-permute-start.7 = (bf16[500,640]{1,0:T(8,128)(2,1)S(1)}, bf16[500,640]{1,0:T(8,128)(2,1)}, u32[]{:S(2)}, u32[]{:S(2)}) collective-permute-start(bf16[500,640]{1,0:T(8,128)(2,1)S(1)} %collective-permute-done.5.rest_5_), channel_id=1, source_target_pairs={{0,64},{4,452},{64,128},{68,4},{128,192},{132,68},{192,256},{196,1... | collective-permute-start | bytes 1920008 | tf_op jit(solution)/shard_map/ppermute | solution.py:254
  70.5 1.1 copy-start
  75.5 4.3 %collective-permute-start.9 = (f32[500,72]{1,0:T(8,128)S(1)}, f32[500,72]{1,0:T(8,128)S(1)}, u32[]{:S(2)}, u32[]{:S(2)}) collective-permute-start(f32[500,72]{1,0:T(8,128)S(1)} %logits_far.1.mine_ref), channel_id=1, source_target_pairs={{0,4},{4,0},{1,5},{5,1},{2,6},{6,2},{3,7},{7,3},{8,12},{12,8},{9,1... | collective-permute-start | bytes 432008 | tf_op jit(solution)/shard_map/ppermute | solution.py:245
  77.8 3.4 %collective-permute-start.8 = (f32[500,72]{1,0:T(8,128)S(1)}, f32[500,72]{1,0:T(8,128)S(1)}, u32[]{:S(2)}, u32[]{:S(2)}) collective-permute-start(f32[500,72]{1,0:T(8,128)S(1)} %get-tuple-element.25.other_ref), channel_id=1, source_target_pairs={{0,4},{4,0},{1,5},{5,1},{2,6},{6,2},{3,7},{7,3},{8,12},{12,8},{9,1... | collective-permute-start | bytes 432008 | tf_op jit(solution)/shard_map/ppermute | solution.py:245
  97.8 0.9 copy-start.1
  98.7 5.2 %copy-start.4 = (bf16[72,192]{1,0:T(8,128)(2,1)S(1)}, bf16[72,192]{1,0:T(8,128)(2,1)}, u32[]{:S(2)}) copy-start(bf16[72,192]{1,0:T(8,128)(2,1)} %copy-done.3) | copy-start | bytes 82948
  98.7 16.9 %all-to-all-start.3 = ((bf16[8,72,640]{2,1,0:T(8,128)(2,1)}), bf16[8,72,640]{2,1,0:T(8,128)(2,1)S(1)}, u32[]{:S(2)}, u32[]{:S(2)}) async-start(bf16[8,72,640]{2,1,0:T(8,128)(2,1)} %copy-done.1), calls=%async_computation.3 | async-start | bytes 1474560 | tf_op jit(solution)/shard_map/all_to_all | solution.py:309
  103.8 17.0 %copy-start.5 = (bf16[12,1408]{1,0:T(8,128)(2,1)S(1)}, bf16[12,1408]{1,0:T(8,128)(2,1)}, u32[]{:S(2)}) copy-start(bf16[12,1408]{1,0:T(8,128)(2,1)} %pick.1) | copy-start | bytes 101380
  116.6 17.3 %all-to-all-start.4 = ((bf16[16,16,640]{2,1,0:T(8,128)(2,1)}), bf16[16,16,640]{2,1,0:T(8,128)(2,1)S(1)}, u32[]{:S(2)}, u32[]{:S(2)}) async-start(bf16[16,16,640]{2,1,0:T(8,128)(2,1)} %bitcast.18), calls=%async_computation.4 | async-start | bytes 655360 | tf_op jit(solution)/shard_map/all_to_all | solution.py:313

commit v8 on v7

--- a/solution.py
+++ b/solution.py
@@ -302,6 +302,7 @@
     mine, other = early_logits(meta, normed, near[:-1])
     more = swap_core(other)
     mine = far_logits(meta, normed, mine, near[-1])
+    more, mine = lax.optimization_barrier((more, mine))
     logits, stats = sum_logits(meta, label_row, mine, more, other, swap_core(mine))
     stats = spread(stats, ("y", "x"), 32)
     part, gap, group_loss = local_back(meta, stats, logits, label_row, layer_row, near)

time: 136 us -> 134 us (0.985)
  blocking collectives: 18 us -> 16.6 us
  transfers between devices with their start and end apart: 14 -> 14, of which waited for: 7 -> 7; matrix products, arithmetic and copies ran while one was open for 2% -> 2% of each run, Pallas kernels for 4% -> 5%
where the time goes in v8:
time: 134 us; the launch traced here: 133 us
  starting transfers between devices  58.7 us (44%)
  waiting for transfers between devices  39.4 us (29%)
  blocking collectives  16.6 us (12%)
  Pallas kernels  10.5 us (8%)
  local copies, waits for them, and re-layouts  5.21 us (4%)
    ppermute x7, starting transfers between devices, onward(): return lax.ppermute(values, ('z', 'c'), pairs)  25.5 us
    ppermute x3, starting transfers between devices, swap_core(): return lax.ppermute(values, 'c', [(0, 1), (1, 0)])  13.1 us
    all_to_all x1, waiting for transfers between devices, body(): back = lax.all_to_all(sent, ('y', 'c'), 0, 0, tiled=True)  12.3 us
    all_to_all x1, blocking collectives, spread(): return lax.all_to_all(copies, axes, 0, 0, tiled=True)  11.9 us
    all_to_all x1, waiting for transfers between devices, body(): part = lax.all_to_all(part, ('x', 'c'), 0, 0, tiled=True)  11.5 us
    all_to_all x1, starting transfers between devices, spread(): return lax.all_to_all(copies, axes, 0, 0, tiled=True)  6.82 us
    all_to_all x1, waiting for transfers between devices, body(): rows = lax.all_to_all(rows, 'x', 0, 0, tiled=True)  6.23 us
    all_to_all x1, waiting for transfers between devices, spread(): return lax.all_to_all(copies, axes, 0, 0, tiled=True)  5.59 us
  transfers between devices with their start and end apart: 14, of which 7 were waited for; matrix products, arithmetic and copies ran while one was open for 2% of the time, Pallas kernels for 5%

profile of v8, /device:TPU:1, one launch (start us, length us, event | category | flops | bytes accessed | tf_op | source)
XLA Modules:
  0.0 133.2 jit_solution(4538973529662589359)
XLA Ops:
  0.6 8.8 %collective-permute-start.1 = (bf16[500,640]{1,0:T(8,128)(2,1)}, bf16[500,640]{1,0:T(8,128)(2,1)S(1)}, u32[]{:S(2)}, u32[]{:S(2)}) collective-permute-start(bf16[500,640]{1,0:T(8,128)(2,1)} %bitcast.37), channel_id=1, source_target_pairs={{0,4},{4,0},{1,5},{5,1},{2,6},{6,2},{3,7},{7,3},{8,12},{12,8},{9,1... | collective-permute-start | bytes 1920008 | tf_op jit(solution)/shard_map/ppermute | solution.py:245
  9.4 5.3 %collective-permute-start = (bf16[500,640]{1,0:T(8,128)(2,1)}, bf16[500,640]{1,0:T(8,128)(2,1)S(1)}, u32[]{:S(2)}, u32[]{:S(2)}) collective-permute-start(bf16[500,640]{1,0:T(8,128)(2,1)} %bitcast.38), channel_id=1, source_target_pairs={{0,64},{4,452},{64,128},{68,4},{128,192},{132,68},{192,256},{196,1... | collective-permute-start | bytes 1920008 | tf_op jit(solution)/shard_map/ppermute | solution.py:254
  14.7 2.2 %collective-permute-start.2 = (bf16[500,640]{1,0:T(8,128)(2,1)S(1)}, bf16[500,640]{1,0:T(8,128)(2,1)S(1)}, u32[]{:S(2)}, u32[]{:S(2)}) collective-permute-start(bf16[500,640]{1,0:T(8,128)(2,1)S(1)} %collective-permute-done.1), channel_id=1, source_target_pairs={{0,64},{4,452},{64,128},{68,4},{128,192},{132,68},{192,256},{196,1... | collective-permute-start | bytes 1920008 | tf_op jit(solution)/shard_map/ppermute | solution.py:254
  16.9 2.8 %pick.1 = bf16[12,1408]{1,0:T(8,128)(2,1)} custom-call(s32[2,6]{1,0:T(2,128)} %slots_ref.1, s32[256]{0:T(256)} %targets_ref.1, bf16[2,256,1280]{2,1,0:T(8,128)(2,1)} %hidden_ref.1), custom_call_target="tpu_custom_call" | custom-call | tf_op jit(solution)/shard_map/pick/pallas_call | solution.py:52
  19.8 2.1 %all-gather.1 = bf16[2,12,1408]{2,1,0:T(8,128)(2,1)S(1)} all-gather(bf16[1,12,1408]{2,1,0:T(8,128)(2,1)} %bitcast.44), channel_id=1, replica_groups=mesh['z'=8,'y'=8,'c'=2,'x'=4] {'c'}, dimensions={0}, use_global_device_ids=true | all-gather | bytes 101376 | tf_op jit(solution)/shard_map/all_gather | solution.py:281
  22.4 4.9 %collective-permute-start.3 = (bf16[500,640]{1,0:T(8,128)(2,1)S(1)}, bf16[500,640]{1,0:T(8,128)(2,1)S(1)}, u32[]{:S(2)}, u32[]{:S(2)}) collective-permute-start(bf16[500,640]{1,0:T(8,128)(2,1)S(1)} %collective-permute-done.rest_1_), channel_id=1, source_target_pairs={{0,64},{4,452},{64,128},{68,4},{128,192},{132,68},{192,256},{196,1... | collective-permute-start | bytes 1920008 | tf_op jit(solution)/shard_map/ppermute | solution.py:254
  27.4 1.9 %collective-permute-done.2.rest_2_ = bf16[500,640]{1,0:T(8,128)(2,1)S(1)} collective-permute-done((bf16[500,640]{1,0:T(8,128)(2,1)S(1)}, bf16[500,640]{1,0:T(8,128)(2,1)S(1)}, u32[]{:S(2)}, u32[]{:S(2)}) %collective-permute-start.2) | collective-permute-done | bytes 640032 | tf_op jit(solution)/shard_map/ppermute | solution.py:254
  29.3 5.0 %collective-permute-start.4 = (bf16[500,640]{1,0:T(8,128)(2,1)S(1)}, bf16[500,640]{1,0:T(8,128)(2,1)S(1)}, u32[]{:S(2)}, u32[]{:S(2)}) collective-permute-start(bf16[500,640]{1,0:T(8,128)(2,1)S(1)} %collective-permute-done.2.rest_2_), channel_id=1, source_target_pairs={{0,64},{4,452},{64,128},{68,4},{128,192},{132,68},{192,256},{196,1... | collective-permute-start | bytes 1920008 | tf_op jit(solution)/shard_map/ppermute | solution.py:254
  34.3 0.7 broadcast_in_dim.4
  35.1 6.8 %all-to-all-start = ((bf16[8,24,768]{2,1,0:T(8,128)(2,1)}), bf16[8,24,768]{2,1,0:T(8,128)(2,1)S(1)}, u32[]{:S(2)}, u32[]{:S(2)}) async-start(bf16[8,24,768]{2,1,0:T(8,128)(2,1)} %broadcast_in_dim.4), calls=%async_computation | async-start | bytes 589824 | tf_op jit(solution)/shard_map/all_to_all | solution.py:241
  41.9 1.9 %collective-permute-start.5 = (bf16[500,640]{1,0:T(8,128)(2,1)S(1)}, bf16[500,640]{1,0:T(8,128)(2,1)S(1)}, u32[]{:S(2)}, u32[]{:S(2)}) collective-permute-start(bf16[500,640]{1,0:T(8,128)(2,1)S(1)} %collective-permute-done.3.rest_3_), channel_id=1, source_target_pairs={{0,64},{4,452},{64,128},{68,4},{128,192},{132,68},{192,256},{196,1... | collective-permute-start | bytes 1920008 | tf_op jit(solution)/shard_map/ppermute | solution.py:254
  43.8 4.3 %collective-permute-start.6 = (bf16[500,640]{1,0:T(8,128)(2,1)S(1)}, bf16[500,640]{1,0:T(8,128)(2,1)}, u32[]{:S(2)}, u32[]{:S(2)}) collective-permute-start(bf16[500,640]{1,0:T(8,128)(2,1)S(1)} %collective-permute-done.4.rest_4_), channel_id=1, source_target_pairs={{0,64},{4,452},{64,128},{68,4},{128,192},{132,68},{192,256},{196,1... | collective-permute-start | bytes 1920008 | tf_op jit(solution)/shard_map/ppermute | solution.py:254
  48.1 5.6 %all-to-all-done = bf16[8,24,768]{2,1,0:T(8,128)(2,1)S(1)} async-done(((bf16[8,24,768]{2,1,0:T(8,128)(2,1)}), bf16[8,24,768]{2,1,0:T(8,128)(2,1)S(1)}, u32[]{:S(2)}, u32[]{:S(2)}) %all-to-all-start) | async-done | bytes 294944 | tf_op jit(solution)/shard_map/all_to_all | solution.py:241
  54.1 0.7 copy-done.2
  55.4 4.1 %all-to-all-start.1 = ((bf16[4,72,640]{2,1,0:T(8,128)(2,1)}), bf16[4,72,640]{2,1,0:T(8,128)(2,1)}, u32[]{:S(2)}, u32[]{:S(2)}) async-start(bf16[4,72,640]{2,1,0:T(8,128)(2,1)} %copy-done.2), calls=%async_computation.1 | async-start | bytes 737280 | tf_op jit(solution)/shard_map/all_to_all | solution.py:292
  59.7 1.9 %collective-permute-start.8 = (bf16[500,640]{1,0:T(8,128)(2,1)S(1)}, bf16[500,640]{1,0:T(8,128)(2,1)}, u32[]{:S(2)}, u32[]{:S(2)}) collective-permute-start(bf16[500,640]{1,0:T(8,128)(2,1)S(1)} %collective-permute-done.5.rest_5_), channel_id=1, source_target_pairs={{0,64},{4,452},{64,128},{68,4},{128,192},{132,68},{192,256},{196,1... | collective-permute-start | bytes 1920008 | tf_op jit(solution)/shard_map/ppermute | solution.py:254
  61.6 6.2 %all-to-all-done.1 = bf16[4,72,640]{2,1,0:T(8,128)(2,1)} async-done(((bf16[4,72,640]{2,1,0:T(8,128)(2,1)}), bf16[4,72,640]{2,1,0:T(8,128)(2,1)}, u32[]{:S(2)}, u32[]{:S(2)}) %all-to-all-start.1) | async-done | bytes 368672 | tf_op jit(solution)/shard_map/all_to_all | solution.py:292
  67.8 2.6 %all-gather = bf16[8,72,640]{2,1,0:T(8,128)(2,1)S(1)} all-gather(bf16[4,72,640]{2,1,0:T(8,128)(2,1)} %all-to-all-done.1), channel_id=2, replica_groups=mesh['z'=8,'y'=8,'c'=2,'x'=4] {'c'}, dimensions={0}, use_global_device_ids=true | all-gather | bytes 1105920 | tf_op jit(solution)/shard_map/all_gather | solution.py:294
  71.6 2.5 %logits_early.1 = (f32[500,72]{1,0:T(8,128)S(1)}, f32[500,72]{1,0:T(8,128)S(1)}) custom-call(s32[10]{0:T(128)S(1)} %stack.43.meta_ref, bf16[2,4,72,640]{3,2,1,0:T(8,128)(2,1)S(1)} %fusion.2.normed_ref, bf16[500,640]{1,0:T(8,128)(2,1)S(1)} %bitcast.39, bf16[500,640]{1,0:T(8,128)(2,1)S(1)} %collective-permute-done.rest_1_, ...), custom_call_target="tpu_custom_call" | custom-call | flops 322560000 | bytes 4480000 | tf_op jit(solution)/shard_map/logits_early/pallas_call | solution.py:153
  74.0 2.3 %collective-permute-start.7 = (f32[500,72]{1,0:T(8,128)S(1)}, f32[500,72]{1,0:T(8,128)S(1)}, u32[]{:S(2)}, u32[]{:S(2)}) collective-permute-start(f32[500,72]{1,0:T(8,128)S(1)} %get-tuple-element.26.other_ref), channel_id=1, source_target_pairs={{0,4},{4,0},{1,5},{5,1},{2,6},{6,2},{3,7},{7,3},{8,12},{12,8},{9,1... | collective-permute-start | bytes 432008 | tf_op jit(solution)/shard_map/ppermute | solution.py:245
  76.3 1.4 %logits_far.1.mine_ref = f32[500,72]{1,0:T(8,128)S(1)} custom-call(s32[10]{0:T(128)S(1)} %stack.43.meta_ref, bf16[2,4,72,640]{3,2,1,0:T(8,128)(2,1)S(1)} %fusion.2.normed_ref, f32[500,72]{1,0:T(8,128)S(1)} %get-tuple-element.27.begun_ref, bf16[500,640]{1,0:T(8,128)(2,1)} %collective-permute-done.8.far_ref.rest_7_), custom_call_target="tpu_custom_call" | custom-call | tf_op jit(solution)/shard_map/logits_far/pallas_call | solution.py:169
  77.8 2.0 %collective-permute-start.9 = (f32[500,72]{1,0:T(8,128)S(1)}, f32[500,72]{1,0:T(8,128)S(1)}, u32[]{:S(2)}, u32[]{:S(2)}) collective-permute-start(f32[500,72]{1,0:T(8,128)S(1)} %logits_far.1.mine_ref), channel_id=1, source_target_pairs={{0,4},{4,0},{1,5},{5,1},{2,6},{6,2},{3,7},{7,3},{8,12},{12,8},{9,1... | collective-permute-start | bytes 432008 | tf_op jit(solution)/shard_map/ppermute | solution.py:245
  79.8 1.4 %collective-permute-done.9.rest_ref = f32[500,72]{1,0:T(8,128)S(1)} collective-permute-done((f32[500,72]{1,0:T(8,128)S(1)}, f32[500,72]{1,0:T(8,128)S(1)}, u32[]{:S(2)}, u32[]{:S(2)}) %collective-permute-start.9) | collective-permute-done | bytes 144032 | tf_op jit(solution)/shard_map/ppermute | solution.py:245
  81.2 0.9 logits.1
  82.1 11.9 %all_to_all.25.stats_ref = f32[32,4,72]{2,1,0:T(4,128)S(1)} all-to-all(f32[32,4,72]{2,1,0:T(4,128)S(1)} %broadcast_in_dim.5), channel_id=1, replica_groups=mesh['z'=8,'y'=8,'c'=2,'x'=4] {'y','x'}, dimensions={0} | all-to-all | bytes 73728 | tf_op jit(solution)/shard_map/all_to_all | solution.py:241
  94.0 2.5 %back.1 = (bf16[8,72,640]{2,1,0:T(8,128)(2,1)S(1)}, f32[1,72]{1,0:T(1,128)S(1)}, f32[2,1]{1,0:T(2,128)S(1)}) custom-call(s32[10]{0:T(128)S(1)} %stack.43.meta_ref, f32[32,4,72]{2,1,0:T(4,128)S(1)} %all_to_all.25.stats_ref, f32[2,500,72]{2,1,0:T(8,128)S(1)} %get-tuple-element.31.logits_ref, s32[1,72]{1,0:T(1,128)S(1)} %get-tuple-element.25.label_ref, ...), custom_call_target="tpu_custom_call" | custom-call | tf_op jit(solution)/shard_map/back/pallas_call | solution.py:225
  96.5 0.9 copy-done.1
  97.4 4.9 %all-to-all-start.3 = ((bf16[8,72,640]{2,1,0:T(8,128)(2,1)}), bf16[8,72,640]{2,1,0:T(8,128)(2,1)S(1)}, u32[]{:S(2)}, u32[]{:S(2)}) async-start(bf16[8,72,640]{2,1,0:T(8,128)(2,1)} %copy-done.1), calls=%async_computation.3 | async-start | bytes 1474560 | tf_op jit(solution)/shard_map/all_to_all | solution.py:310
  102.6 11.5 %all-to-all-done.3 = bf16[8,72,640]{2,1,0:T(8,128)(2,1)S(1)} async-done(((bf16[8,72,640]{2,1,0:T(8,128)(2,1)}), bf16[8,72,640]{2,1,0:T(8,128)(2,1)S(1)}, u32[]{:S(2)}, u32[]{:S(2)}) %all-to-all-start.3) | async-done | bytes 737312 | tf_op jit(solution)/shard_map/all_to_all | solution.py:310
  114.2 0.9 convolution_convert_fusion
  115.1 4.2 %all-to-all-start.4 = ((bf16[16,16,640]{2,1,0:T(8,128)(2,1)}), bf16[16,16,640]{2,1,0:T(8,128)(2,1)S(1)}, u32[]{:S(2)}, u32[]{:S(2)}) async-start(bf16[16,16,640]{2,1,0:T(8,128)(2,1)} %bitcast.18), calls=%async_computation.4 | async-start | bytes 655360 | tf_op jit(solution)/shard_map/all_to_all | solution.py:314
  120.1 12.3 %all-to-all-done.4 = bf16[16,16,640]{2,1,0:T(8,128)(2,1)S(1)} async-done(((bf16[16,16,640]{2,1,0:T(8,128)(2,1)}), bf16[16,16,640]{2,1,0:T(8,128)(2,1)S(1)}, u32[]{:S(2)}, u32[]{:S(2)}) %all-to-all-start.4) | async-done | bytes 327712 | tf_op jit(solution)/shard_map/all_to_all | solution.py:314
  (48 shorter events, 4.7 us)
Async XLA Ops:
  0.6 14.1 %collective-permute-start.1 = (bf16[500,640]{1,0:T(8,128)(2,1)}, bf16[500,640]{1,0:T(8,128)(2,1)S(1)}, u32[]{:S(2)}, u32[]{:S(2)}) collective-permute-start(bf16[500,640]{1,0:T(8,128)(2,1)} %bitcast.37), channel_id=1, source_target_pairs={{0,4},{4,0},{1,5},{5,1},{2,6},{6,2},{3,7},{7,3},{8,12},{12,8},{9,1... | collective-permute-start | bytes 1920008 | tf_op jit(solution)/shard_map/ppermute | solution.py:245
  9.4 13.0 %collective-permute-start = (bf16[500,640]{1,0:T(8,128)(2,1)}, bf16[500,640]{1,0:T(8,128)(2,1)S(1)}, u32[]{:S(2)}, u32[]{:S(2)}) collective-permute-start(bf16[500,640]{1,0:T(8,128)(2,1)} %bitcast.38), channel_id=1, source_target_pairs={{0,64},{4,452},{64,128},{68,4},{128,192},{132,68},{192,256},{196,1... | collective-permute-start | bytes 1920008 | tf_op jit(solution)/shard_map/ppermute | solution.py:254
  14.7 14.5 %collective-permute-start.2 = (bf16[500,640]{1,0:T(8,128)(2,1)S(1)}, bf16[500,640]{1,0:T(8,128)(2,1)S(1)}, u32[]{:S(2)}, u32[]{:S(2)}) collective-permute-start(bf16[500,640]{1,0:T(8,128)(2,1)S(1)} %collective-permute-done.1), channel_id=1, source_target_pairs={{0,64},{4,452},{64,128},{68,4},{128,192},{132,68},{192,256},{196,1... | collective-permute-start | bytes 1920008 | tf_op jit(solution)/shard_map/ppermute | solution.py:254
  19.8 39.8 %copy-start.6 = (bf16[5120]{0:T(1024)(128)(2,1)S(1)}, bf16[5120]{0:T(1024)(128)(2,1)}, u32[]{:S(2)}) copy-start(bf16[5120]{0:T(1024)(128)(2,1)} %param.6) | copy-start | bytes 30724
  22.4 19.4 %collective-permute-start.3 = (bf16[500,640]{1,0:T(8,128)(2,1)S(1)}, bf16[500,640]{1,0:T(8,128)(2,1)S(1)}, u32[]{:S(2)}, u32[]{:S(2)}) collective-permute-start(bf16[500,640]{1,0:T(8,128)(2,1)S(1)} %collective-permute-done.rest_1_), channel_id=1, source_target_pairs={{0,64},{4,452},{64,128},{68,4},{128,192},{132,68},{192,256},{196,1... | collective-permute-start | bytes 1920008 | tf_op jit(solution)/shard_map/ppermute | solution.py:254
  29.3 14.6 %collective-permute-start.4 = (bf16[500,640]{1,0:T(8,128)(2,1)S(1)}, bf16[500,640]{1,0:T(8,128)(2,1)S(1)}, u32[]{:S(2)}, u32[]{:S(2)}) collective-permute-start(bf16[500,640]{1,0:T(8,128)(2,1)S(1)} %collective-permute-done.2.rest_2_), channel_id=1, source_target_pairs={{0,64},{4,452},{64,128},{68,4},{128,192},{132,68},{192,256},{196,1... | collective-permute-start | bytes 1920008 | tf_op jit(solution)/shard_map/ppermute | solution.py:254
  35.1 18.6 %all-to-all-start = ((bf16[8,24,768]{2,1,0:T(8,128)(2,1)}), bf16[8,24,768]{2,1,0:T(8,128)(2,1)S(1)}, u32[]{:S(2)}, u32[]{:S(2)}) async-start(bf16[8,24,768]{2,1,0:T(8,128)(2,1)} %broadcast_in_dim.4), calls=%async_computation | async-start | bytes 589824 | tf_op jit(solution)/shard_map/all_to_all | solution.py:241
  41.9 17.8 %collective-permute-start.5 = (bf16[500,640]{1,0:T(8,128)(2,1)S(1)}, bf16[500,640]{1,0:T(8,128)(2,1)S(1)}, u32[]{:S(2)}, u32[]{:S(2)}) collective-permute-start(bf16[500,640]{1,0:T(8,128)(2,1)S(1)} %collective-permute-done.3.rest_3_), channel_id=1, source_target_pairs={{0,64},{4,452},{64,128},{68,4},{128,192},{132,68},{192,256},{196,1... | collective-permute-start | bytes 1920008 | tf_op jit(solution)/shard_map/ppermute | solution.py:254
  43.8 24.0 %collective-permute-start.6 = (bf16[500,640]{1,0:T(8,128)(2,1)S(1)}, bf16[500,640]{1,0:T(8,128)(2,1)}, u32[]{:S(2)}, u32[]{:S(2)}) collective-permute-start(bf16[500,640]{1,0:T(8,128)(2,1)S(1)} %collective-permute-done.4.rest_4_), channel_id=1, source_target_pairs={{0,64},{4,452},{64,128},{68,4},{128,192},{132,68},{192,256},{196,1... | collective-permute-start | bytes 1920008 | tf_op jit(solution)/shard_map/ppermute | solution.py:254
  54.0 0.7 copy-start.2
  54.8 0.6 copy-start.3
  55.4 12.5 %all-to-all-start.1 = ((bf16[4,72,640]{2,1,0:T(8,128)(2,1)}), bf16[4,72,640]{2,1,0:T(8,128)(2,1)}, u32[]{:S(2)}, u32[]{:S(2)}) async-start(bf16[4,72,640]{2,1,0:T(8,128)(2,1)} %copy-done.2), calls=%async_computation.1 | async-start | bytes 737280 | tf_op jit(solution)/shard_map/all_to_all | solution.py:292
  59.7 16.6 %collective-permute-start.8 = (bf16[500,640]{1,0:T(8,128)(2,1)S(1)}, bf16[500,640]{1,0:T(8,128)(2,1)}, u32[]{:S(2)}, u32[]{:S(2)}) collective-permute-start(bf16[500,640]{1,0:T(8,128)(2,1)S(1)} %collective-permute-done.5.rest_5_), channel_id=1, source_target_pairs={{0,64},{4,452},{64,128},{68,4},{128,192},{132,68},{192,256},{196,1... | collective-permute-start | bytes 1920008 | tf_op jit(solution)/shard_map/ppermute | solution.py:254
  70.5 1.1 copy-start
  74.0 3.7 %collective-permute-start.7 = (f32[500,72]{1,0:T(8,128)S(1)}, f32[500,72]{1,0:T(8,128)S(1)}, u32[]{:S(2)}, u32[]{:S(2)}) collective-permute-start(f32[500,72]{1,0:T(8,128)S(1)} %get-tuple-element.26.other_ref), channel_id=1, source_target_pairs={{0,4},{4,0},{1,5},{5,1},{2,6},{6,2},{3,7},{7,3},{8,12},{12,8},{9,1... | collective-permute-start | bytes 432008 | tf_op jit(solution)/shard_map/ppermute | solution.py:245
  77.8 3.4 %collective-permute-start.9 = (f32[500,72]{1,0:T(8,128)S(1)}, f32[500,72]{1,0:T(8,128)S(1)}, u32[]{:S(2)}, u32[]{:S(2)}) collective-permute-start(f32[500,72]{1,0:T(8,128)S(1)} %logits_far.1.mine_ref), channel_id=1, source_target_pairs={{0,4},{4,0},{1,5},{5,1},{2,6},{6,2},{3,7},{7,3},{8,12},{12,8},{9,1... | collective-permute-start | bytes 432008 | tf_op jit(solution)/shard_map/ppermute | solution.py:245
  96.5 0.9 copy-start.1
  97.4 5.0 %copy-start.4 = (bf16[72,192]{1,0:T(8,128)(2,1)S(1)}, bf16[72,192]{1,0:T(8,128)(2,1)}, u32[]{:S(2)}) copy-start(bf16[72,192]{1,0:T(8,128)(2,1)} %copy-done.3) | copy-start | bytes 82948
  97.4 16.7 %all-to-all-start.3 = ((bf16[8,72,640]{2,1,0:T(8,128)(2,1)}), bf16[8,72,640]{2,1,0:T(8,128)(2,1)S(1)}, u32[]{:S(2)}, u32[]{:S(2)}) async-start(bf16[8,72,640]{2,1,0:T(8,128)(2,1)} %copy-done.1), calls=%async_computation.3 | async-start | bytes 1474560 | tf_op jit(solution)/shard_map/all_to_all | solution.py:310
  102.3 17.0 %copy-start.5 = (bf16[12,1408]{1,0:T(8,128)(2,1)S(1)}, bf16[12,1408]{1,0:T(8,128)(2,1)}, u32[]{:S(2)}) copy-start(bf16[12,1408]{1,0:T(8,128)(2,1)} %pick.1) | copy-start | bytes 101380
  115.1 17.3 %all-to-all-start.4 = ((bf16[16,16,640]{2,1,0:T(8,128)(2,1)}), bf16[16,16,640]{2,1,0:T(8,128)(2,1)S(1)}, u32[]{:S(2)}, u32[]{:S(2)}) async-start(bf16[16,16,640]{2,1,0:T(8,128)(2,1)} %bitcast.18), calls=%async_computation.4 | async-start | bytes 655360 | tf_op jit(solution)/shard_map/all_to_all | solution.py:314

commit v9 on v8

--- a/solution.py
+++ b/solution.py
@@ -97,7 +97,7 @@
             jax.ShapeDtypeStruct((1, LIVE), jnp.int32),
             jax.ShapeDtypeStruct((1, LIVE), jnp.int32),
         ],
-        compiler_params=params(),
+        compiler_params=params(56),
         name="compact",
     )(slots)
 

time: 134 us -> 135 us (level)
  Pallas kernels: 10.5 us -> 12.2 us
    pallas_call x1, Pallas kernels: 0.35 us -> 2.06 us  [compact(): pl.pallas_call(compact_kernel, in_specs=[VMEM], out_specs=[VMEM] * 4, out...]
    unnamed x17 -> x19, local copies, waits for them, and re-layouts: 4.02 us -> 3.42 us
  transfers between devices with their start and end apart: 14 -> 14, of which waited for: 7 -> 7; matrix products, arithmetic and copies ran while one was open for 2% -> 2% of each run, Pallas kernels for 5% -> 7%
where the time goes in v9:
time: 135 us; the launch traced here: 134 us
  starting transfers between devices  58.7 us (43%)
  waiting for transfers between devices  39.4 us (29%)
  blocking collectives  16.6 us (12%)
  Pallas kernels  12.2 us (9%)
  local copies, waits for them, and re-layouts  4.63 us (3%)
    ppermute x7, starting transfers between devices, onward(): return lax.ppermute(values, ('z', 'c'), pairs)  25.5 us
    ppermute x3, starting transfers between devices, swap_core(): return lax.ppermute(values, 'c', [(0, 1), (1, 0)])  13.1 us
    all_to_all x1, waiting for transfers between devices, body(): back = lax.all_to_all(sent, ('y', 'c'), 0, 0, tiled=True)  12.3 us
    all_to_all x1, blocking collectives, spread(): return lax.all_to_all(copies, axes, 0, 0, tiled=True)  11.8 us
    all_to_all x1, waiting for transfers between devices, body(): part = lax.all_to_all(part, ('x', 'c'), 0, 0, tiled=True)  11.5 us
    all_to_all x1, starting transfers between devices, spread(): return lax.all_to_all(copies, axes, 0, 0, tiled=True)  6.82 us
    all_to_all x1, waiting for transfers between devices, body(): rows = lax.all_to_all(rows, 'x', 0, 0, tiled=True)  6.22 us
    all_to_all x1, waiting for transfers between devices, spread(): return lax.all_to_all(copies, axes, 0, 0, tiled=True)  5.59 us
  transfers between devices with their start and end apart: 14, of which 7 were waited for; matrix products, arithmetic and copies ran while one was open for 2% of the time, Pallas kernels for 7%

profile of v9, /device:TPU:1, one launch (start us, length us, event | category | flops | bytes accessed | tf_op | source)
XLA Modules:
  0.0 134.3 jit_solution(4867478531835724453)
XLA Ops:
  0.6 8.8 %collective-permute-start.1 = (bf16[500,640]{1,0:T(8,128)(2,1)}, bf16[500,640]{1,0:T(8,128)(2,1)S(1)}, u32[]{:S(2)}, u32[]{:S(2)}) collective-permute-start(bf16[500,640]{1,0:T(8,128)(2,1)} %bitcast.37), channel_id=1, source_target_pairs={{0,4},{4,0},{1,5},{5,1},{2,6},{6,2},{3,7},{7,3},{8,12},{12,8},{9,1... | collective-permute-start | bytes 1920008 | tf_op jit(solution)/shard_map/ppermute | solution.py:245
  9.4 5.3 %collective-permute-start = (bf16[500,640]{1,0:T(8,128)(2,1)}, bf16[500,640]{1,0:T(8,128)(2,1)S(1)}, u32[]{:S(2)}, u32[]{:S(2)}) collective-permute-start(bf16[500,640]{1,0:T(8,128)(2,1)} %bitcast.38), channel_id=1, source_target_pairs={{0,64},{4,452},{64,128},{68,4},{128,192},{132,68},{192,256},{196,1... | collective-permute-start | bytes 1920008 | tf_op jit(solution)/shard_map/ppermute | solution.py:254
  14.7 2.2 %collective-permute-start.2 = (bf16[500,640]{1,0:T(8,128)(2,1)S(1)}, bf16[500,640]{1,0:T(8,128)(2,1)S(1)}, u32[]{:S(2)}, u32[]{:S(2)}) collective-permute-start(bf16[500,640]{1,0:T(8,128)(2,1)S(1)} %collective-permute-done.1), channel_id=1, source_target_pairs={{0,64},{4,452},{64,128},{68,4},{128,192},{132,68},{192,256},{196,1... | collective-permute-start | bytes 1920008 | tf_op jit(solution)/shard_map/ppermute | solution.py:254
  16.9 2.8 %pick.1 = bf16[12,1408]{1,0:T(8,128)(2,1)} custom-call(s32[2,6]{1,0:T(2,128)} %slots_ref.1, s32[256]{0:T(256)} %targets_ref.1, bf16[2,256,1280]{2,1,0:T(8,128)(2,1)} %hidden_ref.1), custom_call_target="tpu_custom_call" | custom-call | tf_op jit(solution)/shard_map/pick/pallas_call | solution.py:52
  19.8 2.1 %all-gather.1 = bf16[2,12,1408]{2,1,0:T(8,128)(2,1)S(1)} all-gather(bf16[1,12,1408]{2,1,0:T(8,128)(2,1)} %bitcast.44), channel_id=1, replica_groups=mesh['z'=8,'y'=8,'c'=2,'x'=4] {'c'}, dimensions={0}, use_global_device_ids=true | all-gather | bytes 101376 | tf_op jit(solution)/shard_map/all_gather | solution.py:281
  22.4 4.9 %collective-permute-start.3 = (bf16[500,640]{1,0:T(8,128)(2,1)S(1)}, bf16[500,640]{1,0:T(8,128)(2,1)S(1)}, u32[]{:S(2)}, u32[]{:S(2)}) collective-permute-start(bf16[500,640]{1,0:T(8,128)(2,1)S(1)} %collective-permute-done.rest_1_), channel_id=1, source_target_pairs={{0,64},{4,452},{64,128},{68,4},{128,192},{132,68},{192,256},{196,1... | collective-permute-start | bytes 1920008 | tf_op jit(solution)/shard_map/ppermute | solution.py:254
  27.4 1.9 %collective-permute-done.2.rest_2_ = bf16[500,640]{1,0:T(8,128)(2,1)S(1)} collective-permute-done((bf16[500,640]{1,0:T(8,128)(2,1)S(1)}, bf16[500,640]{1,0:T(8,128)(2,1)S(1)}, u32[]{:S(2)}, u32[]{:S(2)}) %collective-permute-start.2) | collective-permute-done | bytes 640032 | tf_op jit(solution)/shard_map/ppermute | solution.py:254
  29.3 5.0 %collective-permute-start.4 = (bf16[500,640]{1,0:T(8,128)(2,1)S(1)}, bf16[500,640]{1,0:T(8,128)(2,1)S(1)}, u32[]{:S(2)}, u32[]{:S(2)}) collective-permute-start(bf16[500,640]{1,0:T(8,128)(2,1)S(1)} %collective-permute-done.2.rest_2_), channel_id=1, source_target_pairs={{0,64},{4,452},{64,128},{68,4},{128,192},{132,68},{192,256},{196,1... | collective-permute-start | bytes 1920008 | tf_op jit(solution)/shard_map/ppermute | solution.py:254
  34.3 0.7 broadcast_in_dim.4
  35.1 6.8 %all-to-all-start = ((bf16[8,24,768]{2,1,0:T(8,128)(2,1)}), bf16[8,24,768]{2,1,0:T(8,128)(2,1)S(1)}, u32[]{:S(2)}, u32[]{:S(2)}) async-start(bf16[8,24,768]{2,1,0:T(8,128)(2,1)} %broadcast_in_dim.4), calls=%async_computation | async-start | bytes 589824 | tf_op jit(solution)/shard_map/all_to_all | solution.py:241
  41.9 1.9 %collective-permute-start.5 = (bf16[500,640]{1,0:T(8,128)(2,1)S(1)}, bf16[500,640]{1,0:T(8,128)(2,1)S(1)}, u32[]{:S(2)}, u32[]{:S(2)}) collective-permute-start(bf16[500,640]{1,0:T(8,128)(2,1)S(1)} %collective-permute-done.3.rest_3_), channel_id=1, source_target_pairs={{0,64},{4,452},{64,128},{68,4},{128,192},{132,68},{192,256},{196,1... | collective-permute-start | bytes 1920008 | tf_op jit(solution)/shard_map/ppermute | solution.py:254
  43.8 4.3 %collective-permute-start.6 = (bf16[500,640]{1,0:T(8,128)(2,1)S(1)}, bf16[500,640]{1,0:T(8,128)(2,1)}, u32[]{:S(2)}, u32[]{:S(2)}) collective-permute-start(bf16[500,640]{1,0:T(8,128)(2,1)S(1)} %collective-permute-done.4.rest_4_), channel_id=1, source_target_pairs={{0,64},{4,452},{64,128},{68,4},{128,192},{132,68},{192,256},{196,1... | collective-permute-start | bytes 1920008 | tf_op jit(solution)/shard_map/ppermute | solution.py:254
  48.1 5.6 %all-to-all-done = bf16[8,24,768]{2,1,0:T(8,128)(2,1)S(1)} async-done(((bf16[8,24,768]{2,1,0:T(8,128)(2,1)}), bf16[8,24,768]{2,1,0:T(8,128)(2,1)S(1)}, u32[]{:S(2)}, u32[]{:S(2)}) %all-to-all-start) | async-done | bytes 294944 | tf_op jit(solution)/shard_map/all_to_all | solution.py:241
  54.4 2.1 %compact.1 = (bf16[4,72,640]{2,1,0:T(8,128)(2,1)}, bf16[72,192]{1,0:T(8,128)(2,1)}, s32[1,72]{1,0:T(1,128)}, s32[1,72]{1,0:T(1,128)}) custom-call(bf16[192,768]{1,0:T(8,128)(2,1)} %bitcast.43), custom_call_target="tpu_custom_call" | custom-call | tf_op jit(solution)/shard_map/compact/pallas_call | solution.py:90
  56.5 4.1 %all-to-all-start.1 = ((bf16[4,72,640]{2,1,0:T(8,128)(2,1)}), bf16[4,72,640]{2,1,0:T(8,128)(2,1)}, u32[]{:S(2)}, u32[]{:S(2)}) async-start(bf16[4,72,640]{2,1,0:T(8,128)(2,1)} %get-tuple-element.23), calls=%async_computation.1 | async-start | bytes 737280 | tf_op jit(solution)/shard_map/all_to_all | solution.py:292
  60.7 1.9 %collective-permute-start.8 = (bf16[500,640]{1,0:T(8,128)(2,1)S(1)}, bf16[500,640]{1,0:T(8,128)(2,1)}, u32[]{:S(2)}, u32[]{:S(2)}) collective-permute-start(bf16[500,640]{1,0:T(8,128)(2,1)S(1)} %collective-permute-done.5.rest_5_), channel_id=1, source_target_pairs={{0,64},{4,452},{64,128},{68,4},{128,192},{132,68},{192,256},{196,1... | collective-permute-start | bytes 1920008 | tf_op jit(solution)/shard_map/ppermute | solution.py:254
  62.7 6.2 %all-to-all-done.1 = bf16[4,72,640]{2,1,0:T(8,128)(2,1)} async-done(((bf16[4,72,640]{2,1,0:T(8,128)(2,1)}), bf16[4,72,640]{2,1,0:T(8,128)(2,1)}, u32[]{:S(2)}, u32[]{:S(2)}) %all-to-all-start.1) | async-done | bytes 368672 | tf_op jit(solution)/shard_map/all_to_all | solution.py:292
  68.9 2.7 %all-gather = bf16[8,72,640]{2,1,0:T(8,128)(2,1)S(1)} all-gather(bf16[4,72,640]{2,1,0:T(8,128)(2,1)} %all-to-all-done.1), channel_id=2, replica_groups=mesh['z'=8,'y'=8,'c'=2,'x'=4] {'c'}, dimensions={0}, use_global_device_ids=true | all-gather | bytes 1105920 | tf_op jit(solution)/shard_map/all_gather | solution.py:294
  72.6 2.5 %logits_early.1 = (f32[500,72]{1,0:T(8,128)S(1)}, f32[500,72]{1,0:T(8,128)S(1)}) custom-call(s32[10]{0:T(128)S(1)} %stack.43.meta_ref, bf16[2,4,72,640]{3,2,1,0:T(8,128)(2,1)S(1)} %fusion.2.normed_ref, bf16[500,640]{1,0:T(8,128)(2,1)S(1)} %bitcast.39, bf16[500,640]{1,0:T(8,128)(2,1)S(1)} %collective-permute-done.rest_1_, ...), custom_call_target="tpu_custom_call" | custom-call | flops 322560000 | bytes 4480000 | tf_op jit(solution)/shard_map/logits_early/pallas_call | solution.py:153
  75.1 2.3 %collective-permute-start.7 = (f32[500,72]{1,0:T(8,128)S(1)}, f32[500,72]{1,0:T(8,128)S(1)}, u32[]{:S(2)}, u32[]{:S(2)}) collective-permute-start(f32[500,72]{1,0:T(8,128)S(1)} %get-tuple-element.26.other_ref), channel_id=1, source_target_pairs={{0,4},{4,0},{1,5},{5,1},{2,6},{6,2},{3,7},{7,3},{8,12},{12,8},{9,1... | collective-permute-start | bytes 432008 | tf_op jit(solution)/shard_map/ppermute | solution.py:245
  77.4 1.4 %logits_far.1.mine_ref = f32[500,72]{1,0:T(8,128)S(1)} custom-call(s32[10]{0:T(128)S(1)} %stack.43.meta_ref, bf16[2,4,72,640]{3,2,1,0:T(8,128)(2,1)S(1)} %fusion.2.normed_ref, f32[500,72]{1,0:T(8,128)S(1)} %get-tuple-element.27.begun_ref, bf16[500,640]{1,0:T(8,128)(2,1)} %collective-permute-done.8.far_ref.rest_7_), custom_call_target="tpu_custom_call" | custom-call | tf_op jit(solution)/shard_map/logits_far/pallas_call | solution.py:169
  78.9 2.1 %collective-permute-start.9 = (f32[500,72]{1,0:T(8,128)S(1)}, f32[500,72]{1,0:T(8,128)S(1)}, u32[]{:S(2)}, u32[]{:S(2)}) collective-permute-start(f32[500,72]{1,0:T(8,128)S(1)} %logits_far.1.mine_ref), channel_id=1, source_target_pairs={{0,4},{4,0},{1,5},{5,1},{2,6},{6,2},{3,7},{7,3},{8,12},{12,8},{9,1... | collective-permute-start | bytes 432008 | tf_op jit(solution)/shard_map/ppermute | solution.py:245
  80.9 1.4 %collective-permute-done.9.rest_ref = f32[500,72]{1,0:T(8,128)S(1)} collective-permute-done((f32[500,72]{1,0:T(8,128)S(1)}, f32[500,72]{1,0:T(8,128)S(1)}, u32[]{:S(2)}, u32[]{:S(2)}) %collective-permute-start.9) | collective-permute-done | bytes 144032 | tf_op jit(solution)/shard_map/ppermute | solution.py:245
  82.3 0.9 logits.1
  83.2 11.8 %all_to_all.25.stats_ref = f32[32,4,72]{2,1,0:T(4,128)S(1)} all-to-all(f32[32,4,72]{2,1,0:T(4,128)S(1)} %broadcast_in_dim.5), channel_id=1, replica_groups=mesh['z'=8,'y'=8,'c'=2,'x'=4] {'y','x'}, dimensions={0} | all-to-all | bytes 73728 | tf_op jit(solution)/shard_map/all_to_all | solution.py:241
  95.1 2.5 %back.1 = (bf16[8,72,640]{2,1,0:T(8,128)(2,1)S(1)}, f32[1,72]{1,0:T(1,128)S(1)}, f32[2,1]{1,0:T(2,128)S(1)}) custom-call(s32[10]{0:T(128)S(1)} %stack.43.meta_ref, f32[32,4,72]{2,1,0:T(4,128)S(1)} %all_to_all.25.stats_ref, f32[2,500,72]{2,1,0:T(8,128)S(1)} %get-tuple-element.31.logits_ref, s32[1,72]{1,0:T(1,128)S(1)} %copy-done.2, s32[1,72]{1,0:T(1,128)S(1)} %copy-done.3, ...), custom_call_target="tpu_custom_call" | custom-call | tf_op jit(solution)/shard_map/back/pallas_call | solution.py:225
  97.5 0.9 copy-done.1
  98.4 5.0 %all-to-all-start.3 = ((bf16[8,72,640]{2,1,0:T(8,128)(2,1)}), bf16[8,72,640]{2,1,0:T(8,128)(2,1)S(1)}, u32[]{:S(2)}, u32[]{:S(2)}) async-start(bf16[8,72,640]{2,1,0:T(8,128)(2,1)} %copy-done.1), calls=%async_computation.3 | async-start | bytes 1474560 | tf_op jit(solution)/shard_map/all_to_all | solution.py:310
  103.7 11.5 %all-to-all-done.3 = bf16[8,72,640]{2,1,0:T(8,128)(2,1)S(1)} async-done(((bf16[8,72,640]{2,1,0:T(8,128)(2,1)}), bf16[8,72,640]{2,1,0:T(8,128)(2,1)S(1)}, u32[]{:S(2)}, u32[]{:S(2)}) %all-to-all-start.3) | async-done | bytes 737312 | tf_op jit(solution)/shard_map/all_to_all | solution.py:310
  115.3 1.0 convolution_convert_fusion
  116.2 4.2 %all-to-all-start.4 = ((bf16[16,16,640]{2,1,0:T(8,128)(2,1)}), bf16[16,16,640]{2,1,0:T(8,128)(2,1)S(1)}, u32[]{:S(2)}, u32[]{:S(2)}) async-start(bf16[16,16,640]{2,1,0:T(8,128)(2,1)} %bitcast.18), calls=%async_computation.4 | async-start | bytes 655360 | tf_op jit(solution)/shard_map/all_to_all | solution.py:314
  121.2 12.3 %all-to-all-done.4 = bf16[16,16,640]{2,1,0:T(8,128)(2,1)S(1)} async-done(((bf16[16,16,640]{2,1,0:T(8,128)(2,1)}), bf16[16,16,640]{2,1,0:T(8,128)(2,1)S(1)}, u32[]{:S(2)}, u32[]{:S(2)}) %all-to-all-start.4) | async-done | bytes 327712 | tf_op jit(solution)/shard_map/all_to_all | solution.py:314
  (50 shorter events, 4.5 us)
Async XLA Ops:
  0.6 14.1 %collective-permute-start.1 = (bf16[500,640]{1,0:T(8,128)(2,1)}, bf16[500,640]{1,0:T(8,128)(2,1)S(1)}, u32[]{:S(2)}, u32[]{:S(2)}) collective-permute-start(bf16[500,640]{1,0:T(8,128)(2,1)} %bitcast.37), channel_id=1, source_target_pairs={{0,4},{4,0},{1,5},{5,1},{2,6},{6,2},{3,7},{7,3},{8,12},{12,8},{9,1... | collective-permute-start | bytes 1920008 | tf_op jit(solution)/shard_map/ppermute | solution.py:245
  9.4 13.0 %collective-permute-start = (bf16[500,640]{1,0:T(8,128)(2,1)}, bf16[500,640]{1,0:T(8,128)(2,1)S(1)}, u32[]{:S(2)}, u32[]{:S(2)}) collective-permute-start(bf16[500,640]{1,0:T(8,128)(2,1)} %bitcast.38), channel_id=1, source_target_pairs={{0,64},{4,452},{64,128},{68,4},{128,192},{132,68},{192,256},{196,1... | collective-permute-start | bytes 1920008 | tf_op jit(solution)/shard_map/ppermute | solution.py:254
  14.7 14.5 %collective-permute-start.2 = (bf16[500,640]{1,0:T(8,128)(2,1)S(1)}, bf16[500,640]{1,0:T(8,128)(2,1)S(1)}, u32[]{:S(2)}, u32[]{:S(2)}) collective-permute-start(bf16[500,640]{1,0:T(8,128)(2,1)S(1)} %collective-permute-done.1), channel_id=1, source_target_pairs={{0,64},{4,452},{64,128},{68,4},{128,192},{132,68},{192,256},{196,1... | collective-permute-start | bytes 1920008 | tf_op jit(solution)/shard_map/ppermute | solution.py:254
  19.8 40.8 %copy-start.7 = (bf16[5120]{0:T(1024)(128)(2,1)S(1)}, bf16[5120]{0:T(1024)(128)(2,1)}, u32[]{:S(2)}) copy-start(bf16[5120]{0:T(1024)(128)(2,1)} %param.6) | copy-start | bytes 30724
  22.4 19.4 %collective-permute-start.3 = (bf16[500,640]{1,0:T(8,128)(2,1)S(1)}, bf16[500,640]{1,0:T(8,128)(2,1)S(1)}, u32[]{:S(2)}, u32[]{:S(2)}) collective-permute-start(bf16[500,640]{1,0:T(8,128)(2,1)S(1)} %collective-permute-done.rest_1_), channel_id=1, source_target_pairs={{0,64},{4,452},{64,128},{68,4},{128,192},{132,68},{192,256},{196,1... | collective-permute-start | bytes 1920008 | tf_op jit(solution)/shard_map/ppermute | solution.py:254
  29.3 14.6 %collective-permute-start.4 = (bf16[500,640]{1,0:T(8,128)(2,1)S(1)}, bf16[500,640]{1,0:T(8,128)(2,1)S(1)}, u32[]{:S(2)}, u32[]{:S(2)}) collective-permute-start(bf16[500,640]{1,0:T(8,128)(2,1)S(1)} %collective-permute-done.2.rest_2_), channel_id=1, source_target_pairs={{0,64},{4,452},{64,128},{68,4},{128,192},{132,68},{192,256},{196,1... | collective-permute-start | bytes 1920008 | tf_op jit(solution)/shard_map/ppermute | solution.py:254
  35.1 18.6 %all-to-all-start = ((bf16[8,24,768]{2,1,0:T(8,128)(2,1)}), bf16[8,24,768]{2,1,0:T(8,128)(2,1)S(1)}, u32[]{:S(2)}, u32[]{:S(2)}) async-start(bf16[8,24,768]{2,1,0:T(8,128)(2,1)} %broadcast_in_dim.4), calls=%async_computation | async-start | bytes 589824 | tf_op jit(solution)/shard_map/all_to_all | solution.py:241
  41.9 18.9 %collective-permute-start.5 = (bf16[500,640]{1,0:T(8,128)(2,1)S(1)}, bf16[500,640]{1,0:T(8,128)(2,1)S(1)}, u32[]{:S(2)}, u32[]{:S(2)}) collective-permute-start(bf16[500,640]{1,0:T(8,128)(2,1)S(1)} %collective-permute-done.3.rest_3_), channel_id=1, source_target_pairs={{0,64},{4,452},{64,128},{68,4},{128,192},{132,68},{192,256},{196,1... | collective-permute-start | bytes 1920008 | tf_op jit(solution)/shard_map/ppermute | solution.py:254
  43.8 25.1 %collective-permute-start.6 = (bf16[500,640]{1,0:T(8,128)(2,1)S(1)}, bf16[500,640]{1,0:T(8,128)(2,1)}, u32[]{:S(2)}, u32[]{:S(2)}) collective-permute-start(bf16[500,640]{1,0:T(8,128)(2,1)S(1)} %collective-permute-done.4.rest_4_), channel_id=1, source_target_pairs={{0,64},{4,452},{64,128},{68,4},{128,192},{132,68},{192,256},{196,1... | collective-permute-start | bytes 1920008 | tf_op jit(solution)/shard_map/ppermute | solution.py:254
  53.7 0.7 copy-start.4
  56.5 12.4 %all-to-all-start.1 = ((bf16[4,72,640]{2,1,0:T(8,128)(2,1)}), bf16[4,72,640]{2,1,0:T(8,128)(2,1)}, u32[]{:S(2)}, u32[]{:S(2)}) async-start(bf16[4,72,640]{2,1,0:T(8,128)(2,1)} %get-tuple-element.23), calls=%async_computation.1 | async-start | bytes 737280 | tf_op jit(solution)/shard_map/all_to_all | solution.py:292
  60.7 16.7 %collective-permute-start.8 = (bf16[500,640]{1,0:T(8,128)(2,1)S(1)}, bf16[500,640]{1,0:T(8,128)(2,1)}, u32[]{:S(2)}, u32[]{:S(2)}) collective-permute-start(bf16[500,640]{1,0:T(8,128)(2,1)S(1)} %collective-permute-done.5.rest_5_), channel_id=1, source_target_pairs={{0,64},{4,452},{64,128},{68,4},{128,192},{132,68},{192,256},{196,1... | collective-permute-start | bytes 1920008 | tf_op jit(solution)/shard_map/ppermute | solution.py:254
  71.5 1.1 copy-start
  75.1 7.2 %copy-start.2 = (s32[1,72]{1,0:T(1,128)S(1)}, s32[1,72]{1,0:T(1,128)}, u32[]{:S(2)}) copy-start(s32[1,72]{1,0:T(1,128)} %get-tuple-element.25.label_ref) | copy-start | bytes 868
  75.1 3.7 %collective-permute-start.7 = (f32[500,72]{1,0:T(8,128)S(1)}, f32[500,72]{1,0:T(8,128)S(1)}, u32[]{:S(2)}, u32[]{:S(2)}) collective-permute-start(f32[500,72]{1,0:T(8,128)S(1)} %get-tuple-element.26.other_ref), channel_id=1, source_target_pairs={{0,4},{4,0},{1,5},{5,1},{2,6},{6,2},{3,7},{7,3},{8,12},{12,8},{9,1... | collective-permute-start | bytes 432008 | tf_op jit(solution)/shard_map/ppermute | solution.py:245
  77.4 17.6 %copy-start.3 = (s32[1,72]{1,0:T(1,128)S(1)}, s32[1,72]{1,0:T(1,128)}, u32[]{:S(2)}) copy-start(s32[1,72]{1,0:T(1,128)} %get-tuple-element.32.layer_ref) | copy-start | bytes 868
  78.9 3.4 %collective-permute-start.9 = (f32[500,72]{1,0:T(8,128)S(1)}, f32[500,72]{1,0:T(8,128)S(1)}, u32[]{:S(2)}, u32[]{:S(2)}) collective-permute-start(f32[500,72]{1,0:T(8,128)S(1)} %logits_far.1.mine_ref), channel_id=1, source_target_pairs={{0,4},{4,0},{1,5},{5,1},{2,6},{6,2},{3,7},{7,3},{8,12},{12,8},{9,1... | collective-permute-start | bytes 432008 | tf_op jit(solution)/shard_map/ppermute | solution.py:245
  97.5 0.9 copy-start.1
  98.4 5.1 %copy-start.6 = (bf16[72,192]{1,0:T(8,128)(2,1)S(1)}, bf16[72,192]{1,0:T(8,128)(2,1)}, u32[]{:S(2)}) copy-start(bf16[72,192]{1,0:T(8,128)(2,1)} %get-tuple-element.22) | copy-start | bytes 82948
  98.4 16.8 %all-to-all-start.3 = ((bf16[8,72,640]{2,1,0:T(8,128)(2,1)}), bf16[8,72,640]{2,1,0:T(8,128)(2,1)S(1)}, u32[]{:S(2)}, u32[]{:S(2)}) async-start(bf16[8,72,640]{2,1,0:T(8,128)(2,1)} %copy-done.1), calls=%async_computation.3 | async-start | bytes 1474560 | tf_op jit(solution)/shard_map/all_to_all | solution.py:310
  103.4 17.0 %copy-start.5 = (bf16[12,1408]{1,0:T(8,128)(2,1)S(1)}, bf16[12,1408]{1,0:T(8,128)(2,1)}, u32[]{:S(2)}) copy-start(bf16[12,1408]{1,0:T(8,128)(2,1)} %pick.1) | copy-start | bytes 101380
  116.2 17.2 %all-to-all-start.4 = ((bf16[16,16,640]{2,1,0:T(8,128)(2,1)}), bf16[16,16,640]{2,1,0:T(8,128)(2,1)S(1)}, u32[]{:S(2)}, u32[]{:S(2)}) async-start(bf16[16,16,640]{2,1,0:T(8,128)(2,1)} %bitcast.18), calls=%async_computation.4 | async-start | bytes 655360 | tf_op jit(solution)/shard_map/all_to_all | solution.py:314
